TPU v7x, 32 devices: a whole 2x2x4 slice. The times are simulated.
32 devices in a mesh: grp: 2 (over x), seq: 16 (over z, y, core).
Axes of the slice: x: 2, y: 2, z: 4, core: 2. Of those that a mesh axis runs over, the one named last changes fastest.
Arguments:
- queries: bfloat16 [4096, 4096], P(('grp', 'seq')), parts along dimension 0, may hold values from -24 to 24
- keys: bfloat16 [4096, 512], P(('grp', 'seq')), parts along dimension 0, may hold values from -9 to 9
- values: bfloat16 [4096, 512], P(('grp', 'seq')), parts along dimension 0, may hold values from -8 to 8
- output_gradient: bfloat16 [4096, 4096], P(('grp', 'seq')), parts along dimension 0, may hold values from -8 to 8
- node_of: int32 [4096], P(('grp', 'seq')), parts along dimension 0, may hold values from 0 to 83, as said below
- parent: int32 [168], P('grp'), parts along dimension 0, may hold values from 0 to 67, as said below
Outputs:
- attended: bfloat16 [4096, 4096], P(('grp', 'seq')), parts along dimension 0
- q_grad: bfloat16 [4096, 4096], P(('grp', 'seq')), parts along dimension 0
- keys_gradient: bfloat16 [4096, 512], P(('grp', 'seq')), parts along dimension 0
- values_gradient: bfloat16 [4096, 512], P(('grp', 'seq')), parts along dimension 0
There are 2 independent parts, one for each index of `grp`. A program takes and returns all parts, laid end to end along the dimension named above; each array names one. Nothing has to cross between parts.
Inputs may be any that keep to these rules, and one draw needn't show every extreme that they name: `node_of`: tokens of one node are consecutive around the cycle; tree t holds the nodes t * 21 to t * 21 + 20, its prompt first, on 512 consecutive positions, and a node's ancestors come before it. All ancestors' tokens of a token lie on its own device or on the 4 devices before it around the cycle, and the last token of every tree has its prompt exactly 4 devices back. A prompt is its own parent; every node is at most two parent steps from its prompt.
All inputs are finite; a program needn't handle non-finite values.
Results may differ from a plain program's by a relative error of at most 0.0083.
Values may be sent and summed in bfloat16 or wider, within the bound.
No kernel may reach another device: no remote copies, remote signals or barrier semaphores. Data moves between devices by JAX's collectives and lax.ppermute only.
A program may use at most 128 MiB of HBM per device.

v0:
```python
import jax
import jax.numpy as jnp
from jax import lax
from jax.sharding import PartitionSpec as P

QUERY_HEADS = 32
KEY_VALUE_HEADS = 4
HEAD_WIDTH = 128
REACH = 4


def from_behind(value, axis, by):
    length = lax.axis_size(axis)
    return lax.ppermute(value, axis, [(i, (i + by) % length) for i in range(length)])


def lineage(nodes, parent):
    parents = parent[nodes]
    return jnp.stack([nodes, parents, parent[parents]], axis=1)


def visible(lineage_rows, key_nodes, own_shard):
    matched = jnp.any(lineage_rows[:, :, None] == key_nodes[None, None, :], axis=1)
    if own_shard:
        row_index = lax.broadcasted_iota(jnp.int32, matched.shape, 0)
        col_index = lax.broadcasted_iota(jnp.int32, matched.shape, 1)
        matched = jnp.logical_and(matched, col_index <= row_index)
    return matched


def on_device(queries, keys, values, output_gradient, node_of, parent):
    token_count = queries.shape[0]
    group_share = QUERY_HEADS // KEY_VALUE_HEADS
    inv_root = HEAD_WIDTH ** (-0.5)
    query_block_rows = queries.reshape(token_count, KEY_VALUE_HEADS, group_share, HEAD_WIDTH)
    gradient_rows = output_gradient.reshape(token_count, KEY_VALUE_HEADS, group_share, HEAD_WIDTH)
    lineage_rows = lineage(node_of, parent)
    device_shards = [(keys, values, node_of)]
    carried = (keys, values, node_of)
    for token_offset in range(REACH):
        carried = from_behind((carried[0], carried[1], carried[2]), "seq", 1)
        device_shards.append(carried)
    pair_masks = [
        visible(lineage_rows, device_shards[token_offset][2], token_offset == 0)
        for token_offset in range(REACH + 1)
    ]

    def scores_for(token_offset):
        key_block_rows = device_shards[token_offset][0].reshape(
            token_count, KEY_VALUE_HEADS, HEAD_WIDTH
        )
        raw_scores = (
            jnp.einsum(
                "qhgd,khd->hgqk",
                query_block_rows,
                key_block_rows,
                preferred_element_type=jnp.float32,
            )
            * inv_root
        )
        return jnp.where(pair_masks[token_offset][None, None], raw_scores, -jnp.inf)

    score_tiles = [scores_for(token_offset) for token_offset in range(REACH + 1)]
    row_max = score_tiles[0].max(axis=3)
    for token_offset in range(1, REACH + 1):
        row_max = jnp.maximum(row_max, score_tiles[token_offset].max(axis=3))
    row_total = jnp.zeros((KEY_VALUE_HEADS, group_share, token_count), jnp.float32)
    for token_offset in range(REACH + 1):
        row_total = row_total + jnp.sum(
            jnp.exp(score_tiles[token_offset] - row_max[..., None]), axis=3
        )
    log_total = row_max + jnp.log(row_total)

    def probs_of(token_offset):
        return jnp.where(
            pair_masks[token_offset][None, None],
            jnp.exp(score_tiles[token_offset] - log_total[..., None]),
            0.0,
        )

    context_output = jnp.zeros((token_count, KEY_VALUE_HEADS, group_share, HEAD_WIDTH), jnp.float32)
    for token_offset in range(REACH + 1):
        context_value_block_rows = device_shards[token_offset][1].reshape(
            token_count, KEY_VALUE_HEADS, HEAD_WIDTH
        )
        context_weight_tile = probs_of(token_offset).astype(jnp.bfloat16)
        context_output = context_output + jnp.einsum(
            "hgqk,khd->qhgd",
            context_weight_tile,
            context_value_block_rows,
            preferred_element_type=jnp.float32,
        )
    attended = context_output.reshape(token_count, QUERY_HEADS * HEAD_WIDTH).astype(jnp.bfloat16)
    row_delta = jnp.sum(gradient_rows.astype(jnp.float32) * context_output, axis=3).transpose(
        1, 2, 0
    )
    query_total = jnp.zeros((token_count, KEY_VALUE_HEADS, group_share, HEAD_WIDTH), jnp.float32)
    key_parts = []
    value_parts = []
    for token_offset in range(REACH + 1):
        grads_carried = query_total
        grads_key_block_rows = device_shards[token_offset][0].reshape(
            token_count, KEY_VALUE_HEADS, HEAD_WIDTH
        )
        value_block_rows = device_shards[token_offset][1].reshape(
            token_count, KEY_VALUE_HEADS, HEAD_WIDTH
        )
        attention_tile = probs_of(token_offset)
        weight_tile = attention_tile.astype(jnp.bfloat16)
        prob_grad = jnp.einsum(
            "qhgd,khd->hgqk", gradient_rows, value_block_rows, preferred_element_type=jnp.float32
        )
        score_grad = (attention_tile * (prob_grad - row_delta[..., None])).astype(jnp.bfloat16)
        grads_query_total = grads_carried + jnp.einsum(
            "hgqk,khd->qhgd", score_grad, grads_key_block_rows, preferred_element_type=jnp.float32
        )
        key_portion = (
            jnp.einsum(
                "hgqk,qhgd->khd", score_grad, query_block_rows, preferred_element_type=jnp.float32
            )
            * inv_root
        )
        value_portion = jnp.einsum(
            "hgqk,qhgd->khd", weight_tile, gradient_rows, preferred_element_type=jnp.float32
        )
        query_total, key_portion, value_portion = (
            grads_query_total,
            key_portion.reshape(token_count, KEY_VALUE_HEADS * HEAD_WIDTH),
            value_portion.reshape(token_count, KEY_VALUE_HEADS * HEAD_WIDTH),
        )
        key_parts.append(key_portion)
        value_parts.append(value_portion)
    q_grad = (
        (query_total * inv_root).reshape(token_count, QUERY_HEADS * HEAD_WIDTH).astype(jnp.bfloat16)
    )
    key_total = key_parts[REACH]
    value_total = value_parts[REACH]
    for token_offset in range(REACH - 1, -1, -1):
        key_total, value_total = from_behind((key_total, value_total), "seq", -1)
        key_total = key_total + key_parts[token_offset]
        value_total = value_total + value_parts[token_offset]
    return (attended, q_grad, key_total.astype(jnp.bfloat16), value_total.astype(jnp.bfloat16))


def solution(mesh):
    return jax.shard_map(
        on_device,
        mesh=mesh,
        in_specs=(
            P(("grp", "seq"), None),
            P(("grp", "seq"), None),
            P(("grp", "seq"), None),
            P(("grp", "seq"), None),
            P(("grp", "seq")),
            P("grp"),
        ),
        out_specs=(
            P(("grp", "seq"), None),
            P(("grp", "seq"), None),
            P(("grp", "seq"), None),
            P(("grp", "seq"), None),
        ),
        check_vma=False,
    )
```

profile of v0, /device:TPU:0, one launch (start us, length us, event | category | flops | bytes accessed | tf_op | source)
XLA Modules:
  0.0 147.6 jit_solution(13702124459948672699)
XLA Ops:
  1.2 1.8 %copy.145 = bf16[128,512]{0,1:T(8,128)(2,1)} copy(bf16[128,512]{1,0:T(8,128)(2,1)} %param.7) | data formatting | bytes 262144 | tf_op args[1]
  2.9 2.5 %collective-permute-start.1 = (bf16[128,512]{0,1:T(8,128)(2,1)}, bf16[128,512]{0,1:T(8,128)(2,1)}, u32[]{:S(2)}, u32[]{:S(2)}) collective-permute-start(bf16[128,512]{0,1:T(8,128)(2,1)} %copy.145), channel_id=1, source_target_pairs={{0,1},{1,2},{2,3},{3,4},{4,5},{5,6},{6,7},{7,8},{8,9},{9,10},{10,1... | collective-permute-start | bytes 393224 | tf_op jit(solution)/shard_map/ppermute | solution.py:14
  6.3 1.2 gather_fusion
  7.5 1.5 %collective-permute-start.2 = (s32[128]{0:T(128)S(1)}, s32[128]{0:T(128)S(1)}, u32[]{:S(2)}, u32[]{:S(2)}) collective-permute-start(s32[128]{0:T(128)S(1)} %collective-permute-done), channel_id=1, source_target_pairs={{0,1},{1,2},{2,3},{3,4},{4,5},{5,6},{6,7},{7,8},{8,9},{9,10},{10,1... | collective-permute-start | bytes 1544 | tf_op jit(solution)/shard_map/ppermute | solution.py:14
  9.1 4.2 %collective-permute-done.2 = s32[128]{0:T(128)S(1)} collective-permute-done((s32[128]{0:T(128)S(1)}, s32[128]{0:T(128)S(1)}, u32[]{:S(2)}, u32[]{:S(2)}) %collective-permute-start.2) | collective-permute-done | bytes 544 | tf_op jit(solution)/shard_map/ppermute | solution.py:14
  14.5 4.4 %collective-permute-done.4 = s32[128]{0:T(128)S(1)} collective-permute-done((s32[128]{0:T(128)S(1)}, s32[128]{0:T(128)S(1)}, u32[]{:S(2)}, u32[]{:S(2)}) %collective-permute-start.4) | collective-permute-done | bytes 544 | tf_op jit(solution)/shard_map/ppermute | solution.py:14
  23.0 1.6 %collective-permute-done.6 = s32[128]{0:T(128)S(1)} collective-permute-done((s32[128]{0:T(128)S(1)}, s32[128]{0:T(128)S(1)}, u32[]{:S(2)}, u32[]{:S(2)}) %collective-permute-start.6) | collective-permute-done | bytes 544 | tf_op jit(solution)/shard_map/ppermute | solution.py:14
  24.9 1.8 %fusion.57 = (f32[4,8,128]{2,1,0:T(8,128)S(1)}, f32[4,8,128,128]{2,3,1,0:T(8,128)}) fusion(bf16[128,4,128,1]{0,2,3,1:T(8,128)(2,1)S(1)} %copy.229, bf16[128,4,8,128]{0,3,2,1:T(8,128)(2,1)S(1)} %bitcast.245, pred[128,128]{0,1:T(8,128)(4,1)S(1)} %copy.141), kind=kOutput, calls=%fused_computation.93 | convolution fusion | flops 135786496 | bytes 3309568 | tf_op jit(solution)/shard_map/qhgd,khd->hgqk/dot_general | solution.py:53
  27.3 2.7 %fusion.58 = (f32[4,8,128]{2,1,0:T(8,128)S(1)}, f32[4,8,128,128]{2,3,1,0:T(8,128)}) fusion(bf16[128,4,128,1]{0,2,3,1:T(8,128)(2,1)} %bitcast.97, bf16[128,4,8,128]{0,3,2,1:T(8,128)(2,1)S(1)} %bitcast.246, pred[128,128]{0,1:T(8,128)(4,1)S(1)} %copy.144), kind=kOutput, calls=%fused_computation.94 | convolution fusion | flops 135786496 | bytes 3309568 | tf_op jit(solution)/shard_map/qhgd,khd->hgqk/dot_general | solution.py:53
  31.1 3.5 %collective-permute-done.3 = bf16[128,512]{0,1:T(8,128)(2,1)S(1)} collective-permute-done((bf16[128,512]{0,1:T(8,128)(2,1)}, bf16[128,512]{0,1:T(8,128)(2,1)S(1)}, u32[]{:S(2)}, u32[]{:S(2)}) %collective-permute-start.3) | collective-permute-done | bytes 131104 | tf_op jit(solution)/shard_map/ppermute | solution.py:14
  34.6 1.8 %fusion.56 = (f32[4,8,128]{2,1,0:T(8,128)S(1)}, f32[4,8,128,128]{2,3,1,0:T(8,128)}) fusion(bf16[128,4,128,1]{0,2,3,1:T(8,128)(2,1)S(1)} %bitcast.287, bf16[128,4,8,128]{0,3,2,1:T(8,128)(2,1)S(1)} %bitcast.247, pred[128,128]{0,1:T(8,128)(4,1)S(1)} %copy.148), kind=kOutput, calls=%fused_computation.92 | convolution fusion | flops 135786496 | bytes 3309568 | tf_op jit(solution)/shard_map/qhgd,khd->hgqk/dot_general | solution.py:53
  36.4 2.0 %collective-permute-done.9 = bf16[128,512]{1,0:T(8,128)(2,1)S(1)} collective-permute-done((bf16[128,512]{1,0:T(8,128)(2,1)}, bf16[128,512]{1,0:T(8,128)(2,1)S(1)}, u32[]{:S(2)}, u32[]{:S(2)}) %collective-permute-start.9) | collective-permute-done | bytes 131104 | tf_op jit(solution)/shard_map/ppermute | solution.py:14
  38.6 3.1 %collective-permute-done.5 = bf16[128,512]{0,1:T(8,128)(2,1)S(1)} collective-permute-done((bf16[128,512]{0,1:T(8,128)(2,1)S(1)}, bf16[128,512]{0,1:T(8,128)(2,1)S(1)}, u32[]{:S(2)}, u32[]{:S(2)}) %collective-permute-start.5) | collective-permute-done | bytes 131104 | tf_op jit(solution)/shard_map/ppermute | solution.py:14
  41.7 1.8 %fusion.55 = (f32[4,8,128]{2,1,0:T(8,128)S(1)}, f32[4,8,128,128]{2,3,1,0:T(8,128)}) fusion(bf16[128,4,128,1]{0,2,3,1:T(8,128)(2,1)S(1)} %bitcast.289, bf16[128,4,8,128]{0,3,2,1:T(8,128)(2,1)S(1)} %bitcast.248, pred[128,128]{0,1:T(8,128)(4,1)S(1)} %copy.151), kind=kOutput, calls=%fused_computation.91 | convolution fusion | flops 135786496 | bytes 3309568 | tf_op jit(solution)/shard_map/qhgd,khd->hgqk/dot_general | solution.py:53
  43.5 2.2 %collective-permute-done.10 = bf16[128,512]{1,0:T(8,128)(2,1)S(1)} collective-permute-done((bf16[128,512]{1,0:T(8,128)(2,1)S(1)}, bf16[128,512]{1,0:T(8,128)(2,1)S(1)}, u32[]{:S(2)}, u32[]{:S(2)}) %collective-permute-start.10) | collective-permute-done | bytes 131104 | tf_op jit(solution)/shard_map/ppermute | solution.py:14
  46.1 2.7 %collective-permute-done.7 = bf16[128,512]{0,1:T(8,128)(2,1)S(1)} collective-permute-done((bf16[128,512]{0,1:T(8,128)(2,1)S(1)}, bf16[128,512]{0,1:T(8,128)(2,1)S(1)}, u32[]{:S(2)}, u32[]{:S(2)}) %collective-permute-start.7) | collective-permute-done | bytes 131104 | tf_op jit(solution)/shard_map/ppermute | solution.py:14
  49.3 6.8 %exponential_reduce_fusion.3 = (f32[4,8,128]{2,1,0:T(8,128)S(1)}, f32[4,8,128]{2,1,0:T(8,128)S(1)}, f32[4,8,128]{2,1,0:T(8,128)S(1)}, f32[4,8,128]{2,1,0:T(8,128)S(1)}, f32[4,8,128]{2,1,0:T(8,128)S(1)}) fusion(f32[4,8,128,128]{2,3,1,0:T(8,128)} %get-tuple-element.35, f32[4,8,128]{2,1,0:T(8,128)S(1)} %maximum_maximum_fusion, ...), kind=kLoop, calls=%fused_computation.35 | loop fusion | flops 5222400 | bytes 10584064 | tf_op jit(solution)/shard_map/reduce_sum | solution.py:69
  60.7 1.8 %fusion.34 = f32[4,8,128,128]{2,3,1,0:T(8,128)} fusion(bf16[128,4,128,1]{0,2,3,1:T(8,128)(2,1)S(1)} %bitcast.271, f32[4,8,128,128]{2,3,1,0:T(8,128)S(1)} %copy-done.4, f32[4,8,128]{2,1,0:T(8,128)S(1)} %log_add_fusion, pred[128,128]{0,1:T(8,128)(4,1)S(1)} %copy.144), kind=kOutput, calls=%fused_computation.65 | convolution fusion | flops 135790592 | bytes 4358144 | tf_op jit(solution)/shard_map/hgqk,khd->qhgd/dot_general | solution.py:87
  62.5 1.8 %fusion.30 = f32[4,8,128,128]{2,3,1,0:T(8,128)} fusion(bf16[128,4,128,1]{0,2,3,1:T(8,128)(2,1)S(1)} %bitcast.273, f32[4,8,128,128]{2,3,1,0:T(8,128)S(1)} %copy-done.6, f32[4,8,128]{2,1,0:T(8,128)S(1)} %log_add_fusion, pred[128,128]{0,1:T(8,128)(4,1)S(1)} %copy.148), kind=kOutput, calls=%fused_computation.63 | convolution fusion | flops 135790592 | bytes 4358144 | tf_op jit(solution)/shard_map/hgqk,khd->qhgd/dot_general | solution.py:87
  64.3 1.8 %fusion.26 = f32[4,8,128,128]{2,3,1,0:T(8,128)} fusion(bf16[128,4,128,1]{0,2,3,1:T(8,128)(2,1)S(1)} %bitcast.275, f32[4,8,128,128]{2,3,1,0:T(8,128)S(1)} %copy-done.8, f32[4,8,128]{2,1,0:T(8,128)S(1)} %log_add_fusion, pred[128,128]{0,1:T(8,128)(4,1)S(1)} %copy.151), kind=kOutput, calls=%fused_computation.61 | convolution fusion | flops 135790592 | bytes 4358144 | tf_op jit(solution)/shard_map/hgqk,khd->qhgd/dot_general | solution.py:87
  66.1 1.8 %fusion.38 = f32[4,8,128,128]{2,3,1,0:T(8,128)} fusion(f32[4,8,128,128]{2,3,1,0:T(8,128)S(1)} %copy-done.1, f32[4,8,128]{2,1,0:T(8,128)S(1)} %log_add_fusion, pred[128,128]{0,1:T(8,128)(4,1)S(1)} %copy.141, bf16[128,4,128,1]{2,1,0,3:T(4,128)(2,1)S(1)} %bitcast.269), kind=kOutput, calls=%fused_computation.67 | convolution fusion | flops 135790592 | bytes 4358144 | tf_op jit(solution)/shard_map/hgqk,khd->qhgd/dot_general | solution.py:87
  70.1 5.9 %bitcast_convert_fusion = (bf16[128,4,8,128]{0,3,2,1:T(8,128)(2,1)}, f32[4,8,128,128]{2,3,1,0:T(8,128)S(1)}) fusion(bf16[128,4,128,1]{0,2,3,1:T(8,128)(2,1)S(1)} %bitcast.267, f32[4,8,128,128]{2,3,1,0:T(8,128)} %copy-done.10, f32[4,8,128]{2,1,0:T(8,128)S(1)} %log_add_fusion, pred[128,128]{0,1:T(8,128)(4,1)S(1)} %copy.154, f32[4,8,128,128]{2,3,1,0:T(8,128)} %fusion.26, ...), kind=kOutput, calls=%fused_computation.18 | convolution fusion | flops 138412032 | bytes 13795328 | tf_op jit(solution)/shard_map/hgqk,khd->qhgd/dot_general | solution.py:87
  82.4 1.7 %fusion.1 = bf16[4,8,128,128]{2,3,1,0:T(8,128)(2,1)} fusion(f32[4,8,128,128]{2,3,1,0:T(8,128)S(1)} %copy-done.11, bf16[128,4,128,1]{0,2,3,1:T(8,128)(2,1)S(1)} %bitcast.268, bf16[128,4,8,128]{0,3,2,1:T(8,128)(2,1)S(1)} %bitcast.262, f32[4,8,128]{2,1,0:T(8,128)S(1)} %bitcast.285, f32[4,8,128]{2,1,0:T(8,128)S(1)} %log_add_fusion, pred[128,128]{0,1:T(8,128)(4,1)S(1)} %copy.154), kind=kOutput, calls=%fused_computation.4 | convolution fusion | flops 136839168 | bytes 4374528 | tf_op jit(solution)/shard_map/qhgd,khd->hgqk/dot_general | solution.py:110
  85.9 2.7 %fusion.60 = f32[4,8,128,128]{2,3,1,0:T(8,128)} fusion(bf16[128,4,128,1]{0,2,3,1:T(8,128)(2,1)} %bitcast.97, bf16[4,8,128,128]{2,3,1,0:T(8,128)(2,1)S(1)} %fusion.7), kind=kOutput, calls=%fused_computation.96 | convolution fusion | flops 134217728 | bytes 3276800 | tf_op jit(solution)/shard_map/hgqk,khd->qhgd/dot_general | solution.py:114
  88.6 1.4 fusion.18
  89.9 1.7 %fusion.61 = f32[4,8,128,128]{2,3,1,0:T(8,128)} fusion(bf16[128,4,128,1]{0,2,3,1:T(8,128)(2,1)S(1)} %bitcast.288, bf16[4,8,128,128]{2,3,1,0:T(8,128)(2,1)S(1)} %fusion.5), kind=kOutput, calls=%fused_computation.97 | convolution fusion | flops 134217728 | bytes 3276800 | tf_op jit(solution)/shard_map/hgqk,khd->qhgd/dot_general | solution.py:114
  92.8 1.8 %fusion.62 = f32[4,8,128,128]{2,3,1,0:T(8,128)} fusion(bf16[128,4,128,1]{0,2,3,1:T(8,128)(2,1)S(1)} %bitcast.290, bf16[4,8,128,128]{2,3,1,0:T(8,128)(2,1)S(1)} %fusion.3), kind=kOutput, calls=%fused_computation.98 | convolution fusion | flops 134217728 | bytes 3276800 | tf_op jit(solution)/shard_map/hgqk,khd->qhgd/dot_general | solution.py:114
  94.6 1.8 %copy.206 = f32[128,512]{1,0:T(8,128)} copy(f32[128,512]{0,1:T(8,128)} %bitcast.296) | data formatting | bytes 524288 | tf_op jit(solution)/shard_map/reshape | solution.py:129
  96.4 1.8 %copy.204 = f32[128,512]{1,0:T(8,128)} copy(f32[128,512]{0,1:T(8,128)} %bitcast.295) | data formatting | bytes 524288 | tf_op jit(solution)/shard_map/reshape | solution.py:129
  98.2 1.8 %copy.202 = f32[128,512]{1,0:T(8,128)} copy(f32[128,512]{0,1:T(8,128)} %bitcast.294) | data formatting | bytes 524288 | tf_op jit(solution)/shard_map/reshape | solution.py:129
  100.0 1.8 %copy.200 = f32[128,512]{1,0:T(8,128)} copy(f32[128,512]{0,1:T(8,128)} %bitcast.297) | data formatting | bytes 524288 | tf_op jit(solution)/shard_map/reshape | solution.py:129
  101.8 1.7 %collective-permute-start.16 = (f32[128,512]{1,0:T(8,128)}, f32[128,512]{1,0:T(8,128)}, u32[]{:S(2)}, u32[]{:S(2)}) collective-permute-start(f32[128,512]{1,0:T(8,128)} %copy.200), channel_id=1, source_target_pairs={{0,15},{1,0},{2,1},{3,2},{4,3},{5,4},{6,5},{7,6},{8,7},{9,8},{10,9... | collective-permute-start | bytes 786440 | tf_op jit(solution)/shard_map/ppermute | solution.py:14
  103.5 2.4 %fusion.20 = f32[4,128,128]{1,2,0:T(8,128)} fusion(bf16[4,8,128,128]{2,3,1,0:T(8,128)(2,1)} %fusion.1, bf16[128,4,8,128]{0,3,2,1:T(8,128)(2,1)S(1)} %bitcast.253), kind=kOutput, calls=%fused_computation.51 | convolution fusion | flops 134283264 | bytes 2359296 | tf_op jit(solution)/shard_map/hgqk,qhgd->khd/dot_general | solution.py:118
  105.9 1.8 %copy.186 = f32[128,512]{1,0:T(8,128)} copy(f32[128,512]{0,1:T(8,128)} %bitcast.281) | data formatting | bytes 524288 | tf_op jit(solution)/shard_map/reshape | solution.py:128
  107.7 1.8 %copy.189 = f32[128,512]{1,0:T(8,128)} copy(f32[128,512]{0,1:T(8,128)} %bitcast.279) | data formatting | bytes 524288 | tf_op jit(solution)/shard_map/reshape | solution.py:128
  109.5 1.8 %copy.195 = f32[128,512]{1,0:T(8,128)} copy(f32[128,512]{0,1:T(8,128)} %bitcast.277) | data formatting | bytes 524288 | tf_op jit(solution)/shard_map/reshape | solution.py:128
  111.3 1.8 %copy.192 = f32[128,512]{1,0:T(8,128)} copy(f32[128,512]{0,1:T(8,128)} %bitcast.278) | data formatting | bytes 524288 | tf_op jit(solution)/shard_map/reshape | solution.py:128
  113.6 1.3 add.129
  115.0 2.4 %collective-permute-done.12 = f32[128,512]{1,0:T(8,128)S(1)} collective-permute-done((f32[128,512]{1,0:T(8,128)}, f32[128,512]{1,0:T(8,128)S(1)}, u32[]{:S(2)}, u32[]{:S(2)}) %collective-permute-start.12) | collective-permute-done | bytes 262176 | tf_op jit(solution)/shard_map/ppermute | solution.py:14
  117.5 4.6 %collective-permute-start.13 = (f32[128,512]{1,0:T(8,128)S(1)}, f32[128,512]{1,0:T(8,128)S(1)}, u32[]{:S(2)}, u32[]{:S(2)}) collective-permute-start(f32[128,512]{1,0:T(8,128)S(1)} %add.125), channel_id=1, source_target_pairs={{0,15},{1,0},{2,1},{3,2},{4,3},{5,4},{6,5},{7,6},{8,7},{9,8},{10,9... | collective-permute-start | bytes 786440 | tf_op jit(solution)/shard_map/ppermute | solution.py:14
  122.0 4.0 %multiply_convert_fusion = bf16[4,8,128,128]{2,3,1,0:T(8,128)(2,1)} fusion(f32[4,8,128,128]{2,3,1,0:T(8,128)} %fusion.62, f32[4,8,128,128]{2,3,1,0:T(8,128)} %fusion.61, f32[4,8,128,128]{2,3,1,0:T(8,128)S(1)} %fusion.59, f32[4,8,128,128]{2,3,1,0:T(8,128)S(1)} %copy-done.13, bf16[128,4,128,1]{0,2,3,1:T(8,128)(2,1)S(1)} %bitcast.293, ...), kind=kOutput, calls=%fused_computation.25 | convolution fusion | flops 137363456 | bytes 10616832 | tf_op jit(solution)/shard_map/hgqk,khd->qhgd/dot_general | solution.py:114
  126.4 4.2 %collective-permute-start.14 = (f32[128,512]{1,0:T(8,128)S(1)}, f32[128,512]{1,0:T(8,128)S(1)}, u32[]{:S(2)}, u32[]{:S(2)}) collective-permute-start(f32[128,512]{1,0:T(8,128)S(1)} %add.126), channel_id=1, source_target_pairs={{0,15},{1,0},{2,1},{3,2},{4,3},{5,4},{6,5},{7,6},{8,7},{9,8},{10,9... | collective-permute-start | bytes 786440 | tf_op jit(solution)/shard_map/ppermute | solution.py:14
  132.6 3.0 %collective-permute-start.19 = (f32[128,512]{1,0:T(8,128)}, f32[128,512]{1,0:T(8,128)}, u32[]{:S(2)}, u32[]{:S(2)}) collective-permute-start(f32[128,512]{1,0:T(8,128)} %add.131), channel_id=1, source_target_pairs={{0,15},{1,0},{2,1},{3,2},{4,3},{5,4},{6,5},{7,6},{8,7},{9,8},{10,9... | collective-permute-start | bytes 786440 | tf_op jit(solution)/shard_map/ppermute | solution.py:14
  136.3 3.5 %collective-permute-start.15 = (f32[128,512]{1,0:T(8,128)}, f32[128,512]{1,0:T(8,128)}, u32[]{:S(2)}, u32[]{:S(2)}) collective-permute-start(f32[128,512]{1,0:T(8,128)} %add.127), channel_id=1, source_target_pairs={{0,15},{1,0},{2,1},{3,2},{4,3},{5,4},{6,5},{7,6},{8,7},{9,8},{10,9... | collective-permute-start | bytes 786440 | tf_op jit(solution)/shard_map/ppermute | solution.py:14
  141.5 1.3 copy.209
  142.9 1.3 copy.210
  144.3 1.7 %add_convert_fusion = bf16[128,512]{1,0:T(8,128)(2,1)} fusion(f32[128,512]{1,0:T(8,128)} %collective-permute-done.19, f32[128,512]{1,0:T(8,128)S(1)} %copy.208), kind=kLoop, calls=%fused_computation.52 | loop fusion | flops 131072 | bytes 655360 | tf_op jit(solution)/shard_map/convert_element_type | solution.py:142
  145.9 1.7 %add_convert_fusion.1 = bf16[128,512]{1,0:T(8,128)(2,1)} fusion(f32[128,512]{1,0:T(8,128)} %collective-permute-done.15, f32[128,512]{1,0:T(8,128)S(1)} %copy.198), kind=kLoop, calls=%fused_computation.53 | loop fusion | flops 131072 | bytes 655360 | tf_op jit(solution)/shard_map/convert_element_type | solution.py:142
  (130 shorter events, 30.9 us)
Async XLA Ops:
  0.6 5.7 %copy-start = (s32[84]{0:T(128)S(1)}, s32[84]{0:T(128)}, u32[]{:S(2)}) copy-start(s32[84]{0:T(128)} %param.11) | copy-start | bytes 1012
  0.6 21.0 %copy-start.21 = (bf16[128,4096]{1,0:T(8,128)(2,1)S(1)}, bf16[128,4096]{1,0:T(8,128)(2,1)}, u32[]{:S(2)}) copy-start(bf16[128,4096]{1,0:T(8,128)(2,1)} %param.9) | copy-start | bytes 3145732
  0.7 21.6 %copy-start.22 = (bf16[128,4096]{1,0:T(8,128)(2,1)S(1)}, bf16[128,4096]{1,0:T(8,128)(2,1)}, u32[]{:S(2)}) copy-start(bf16[128,4096]{1,0:T(8,128)(2,1)} %param.6) | copy-start | bytes 3145732
  0.7 6.9 %collective-permute-start = (s32[128]{0:T(128)}, s32[128]{0:T(128)S(1)}, u32[]{:S(2)}, u32[]{:S(2)}) collective-permute-start(s32[128]{0:T(128)} %param.10), channel_id=1, source_target_pairs={{0,1},{1,2},{2,3},{3,4},{4,5},{5,6},{6,7},{7,8},{8,9},{9,10},{10,1... | collective-permute-start | bytes 1544 | tf_op jit(solution)/shard_map/ppermute | solution.py:14
  2.9 24.3 %collective-permute-start.1 = (bf16[128,512]{0,1:T(8,128)(2,1)}, bf16[128,512]{0,1:T(8,128)(2,1)}, u32[]{:S(2)}, u32[]{:S(2)}) collective-permute-start(bf16[128,512]{0,1:T(8,128)(2,1)} %copy.145), channel_id=1, source_target_pairs={{0,1},{1,2},{2,3},{3,4},{4,5},{5,6},{6,7},{7,8},{8,9},{9,10},{10,1... | collective-permute-start | bytes 393224 | tf_op jit(solution)/shard_map/ppermute | solution.py:14
  5.5 24.6 %collective-permute-start.8 = (bf16[128,512]{1,0:T(8,128)(2,1)}, bf16[128,512]{1,0:T(8,128)(2,1)}, u32[]{:S(2)}, u32[]{:S(2)}) collective-permute-start(bf16[128,512]{1,0:T(8,128)(2,1)} %param.8), channel_id=1, source_target_pairs={{0,1},{1,2},{2,3},{3,4},{4,5},{5,6},{6,7},{7,8},{8,9},{9,10},{10,1... | collective-permute-start | bytes 393224 | tf_op jit(solution)/shard_map/ppermute | solution.py:14
  7.5 5.7 %collective-permute-start.2 = (s32[128]{0:T(128)S(1)}, s32[128]{0:T(128)S(1)}, u32[]{:S(2)}, u32[]{:S(2)}) collective-permute-start(s32[128]{0:T(128)S(1)} %collective-permute-done), channel_id=1, source_target_pairs={{0,1},{1,2},{2,3},{3,4},{4,5},{5,6},{6,7},{7,8},{8,9},{9,10},{10,1... | collective-permute-start | bytes 1544 | tf_op jit(solution)/shard_map/ppermute | solution.py:14
  13.2 5.7 %collective-permute-start.4 = (s32[128]{0:T(128)S(1)}, s32[128]{0:T(128)S(1)}, u32[]{:S(2)}, u32[]{:S(2)}) collective-permute-start(s32[128]{0:T(128)S(1)} %collective-permute-done.2), channel_id=1, source_target_pairs={{0,1},{1,2},{2,3},{3,4},{4,5},{5,6},{6,7},{7,8},{8,9},{9,10},{10,1... | collective-permute-start | bytes 1544 | tf_op jit(solution)/shard_map/ppermute | solution.py:14
  18.9 5.7 %collective-permute-start.6 = (s32[128]{0:T(128)S(1)}, s32[128]{0:T(128)S(1)}, u32[]{:S(2)}, u32[]{:S(2)}) collective-permute-start(s32[128]{0:T(128)S(1)} %collective-permute-done.4), channel_id=1, source_target_pairs={{0,1},{1,2},{2,3},{3,4},{4,5},{5,6},{6,7},{7,8},{8,9},{9,10},{10,1... | collective-permute-start | bytes 1544 | tf_op jit(solution)/shard_map/ppermute | solution.py:14
  21.6 3.0 %copy-start.29 = (s32[128]{0:T(128)S(1)}, s32[128]{0:T(128)}, u32[]{:S(2)}) copy-start(s32[128]{0:T(128)} %param.10) | copy-start | bytes 1540
  27.2 7.4 %collective-permute-start.3 = (bf16[128,512]{0,1:T(8,128)(2,1)}, bf16[128,512]{0,1:T(8,128)(2,1)S(1)}, u32[]{:S(2)}, u32[]{:S(2)}) collective-permute-start(bf16[128,512]{0,1:T(8,128)(2,1)} %collective-permute-done.1), channel_id=1, source_target_pairs={{0,1},{1,2},{2,3},{3,4},{4,5},{5,6},{6,7},{7,8},{8,9},{9,10},{10,1... | collective-permute-start | bytes 393224 | tf_op jit(solution)/shard_map/ppermute | solution.py:14
  31.1 7.4 %collective-permute-start.9 = (bf16[128,512]{1,0:T(8,128)(2,1)}, bf16[128,512]{1,0:T(8,128)(2,1)S(1)}, u32[]{:S(2)}, u32[]{:S(2)}) collective-permute-start(bf16[128,512]{1,0:T(8,128)(2,1)} %collective-permute-done.8), channel_id=1, source_target_pairs={{0,1},{1,2},{2,3},{3,4},{4,5},{5,6},{6,7},{7,8},{8,9},{9,10},{10,1... | collective-permute-start | bytes 393224 | tf_op jit(solution)/shard_map/ppermute | solution.py:14
  34.6 8.9 %copy-start.23 = (bf16[128,512]{0,1:T(8,128)(2,1)}, bf16[128,512]{0,1:T(8,128)(2,1)S(1)}, u32[]{:S(2)}) copy-start(bf16[128,512]{0,1:T(8,128)(2,1)S(1)} %collective-permute-done.3) | copy-start | bytes 393220
  34.6 7.1 %collective-permute-start.5 = (bf16[128,512]{0,1:T(8,128)(2,1)S(1)}, bf16[128,512]{0,1:T(8,128)(2,1)S(1)}, u32[]{:S(2)}, u32[]{:S(2)}) collective-permute-start(bf16[128,512]{0,1:T(8,128)(2,1)S(1)} %collective-permute-done.3), channel_id=1, source_target_pairs={{0,1},{1,2},{2,3},{3,4},{4,5},{5,6},{6,7},{7,8},{8,9},{9,10},{10,1... | collective-permute-start | bytes 393224 | tf_op jit(solution)/shard_map/ppermute | solution.py:14
  38.6 7.1 %collective-permute-start.10 = (bf16[128,512]{1,0:T(8,128)(2,1)S(1)}, bf16[128,512]{1,0:T(8,128)(2,1)S(1)}, u32[]{:S(2)}, u32[]{:S(2)}) collective-permute-start(bf16[128,512]{1,0:T(8,128)(2,1)S(1)} %collective-permute-done.9), channel_id=1, source_target_pairs={{0,1},{1,2},{2,3},{3,4},{4,5},{5,6},{6,7},{7,8},{8,9},{9,10},{10,1... | collective-permute-start | bytes 393224 | tf_op jit(solution)/shard_map/ppermute | solution.py:14
  41.7 7.6 %copy-start.25 = (bf16[128,512]{0,1:T(8,128)(2,1)}, bf16[128,512]{0,1:T(8,128)(2,1)S(1)}, u32[]{:S(2)}) copy-start(bf16[128,512]{0,1:T(8,128)(2,1)S(1)} %collective-permute-done.5) | copy-start | bytes 393220
  41.7 7.1 %collective-permute-start.7 = (bf16[128,512]{0,1:T(8,128)(2,1)S(1)}, bf16[128,512]{0,1:T(8,128)(2,1)S(1)}, u32[]{:S(2)}, u32[]{:S(2)}) collective-permute-start(bf16[128,512]{0,1:T(8,128)(2,1)S(1)} %collective-permute-done.5), channel_id=1, source_target_pairs={{0,1},{1,2},{2,3},{3,4},{4,5},{5,6},{6,7},{7,8},{8,9},{9,10},{10,1... | collective-permute-start | bytes 393224 | tf_op jit(solution)/shard_map/ppermute | solution.py:14
  45.8 3.5 %copy-start.1 = (f32[4,8,128,128]{2,3,1,0:T(8,128)S(1)}, f32[4,8,128,128]{2,3,1,0:T(8,128)}, u32[]{:S(2)}) copy-start(f32[4,8,128,128]{2,3,1,0:T(8,128)} %get-tuple-element.33) | copy-start | bytes 6291460
  45.8 23.3 %collective-permute-start.11 = (bf16[128,512]{1,0:T(8,128)(2,1)S(1)}, bf16[128,512]{1,0:T(8,128)(2,1)}, u32[]{:S(2)}, u32[]{:S(2)}) collective-permute-start(bf16[128,512]{1,0:T(8,128)(2,1)S(1)} %collective-permute-done.10), channel_id=1, source_target_pairs={{0,1},{1,2},{2,3},{3,4},{4,5},{5,6},{6,7},{7,8},{8,9},{9,10},{10,1... | collective-permute-start | bytes 393224 | tf_op jit(solution)/shard_map/ppermute | solution.py:14
  48.8 7.4 %copy-start.27 = (bf16[128,512]{0,1:T(8,128)(2,1)}, bf16[128,512]{0,1:T(8,128)(2,1)S(1)}, u32[]{:S(2)}) copy-start(bf16[128,512]{0,1:T(8,128)(2,1)S(1)} %collective-permute-done.7) | copy-start | bytes 393220
  49.3 18.6 %copy-start.10 = (f32[4,8,128,128]{2,3,1,0:T(8,128)}, f32[4,8,128,128]{2,3,1,0:T(8,128)S(1)}, u32[]{:S(2)}) copy-start(f32[4,8,128,128]{2,3,1,0:T(8,128)S(1)} %get-tuple-element.27) | copy-start | bytes 6291460
  49.3 6.9 %copy-start.4 = (f32[4,8,128,128]{2,3,1,0:T(8,128)S(1)}, f32[4,8,128,128]{2,3,1,0:T(8,128)}, u32[]{:S(2)}) copy-start(f32[4,8,128,128]{2,3,1,0:T(8,128)} %get-tuple-element.35) | copy-start | bytes 6291460
  56.2 1.7 %copy-start.6 = (f32[4,8,128,128]{2,3,1,0:T(8,128)S(1)}, f32[4,8,128,128]{2,3,1,0:T(8,128)}, u32[]{:S(2)}) copy-start(f32[4,8,128,128]{2,3,1,0:T(8,128)} %get-tuple-element.31) | copy-start | bytes 6291460
  57.8 1.7 %copy-start.8 = (f32[4,8,128,128]{2,3,1,0:T(8,128)S(1)}, f32[4,8,128,128]{2,3,1,0:T(8,128)}, u32[]{:S(2)}) copy-start(f32[4,8,128,128]{2,3,1,0:T(8,128)} %get-tuple-element.29) | copy-start | bytes 6291460
  76.0 1.6 %copy-start.5 = (f32[4,8,128,128]{2,3,1,0:T(8,128)S(1)}, f32[4,8,128,128]{2,3,1,0:T(8,128)}, u32[]{:S(2)}) copy-start(f32[4,8,128,128]{2,3,1,0:T(8,128)} %get-tuple-element.35) | copy-start | bytes 6291460
  77.6 1.6 %copy-start.7 = (f32[4,8,128,128]{2,3,1,0:T(8,128)S(1)}, f32[4,8,128,128]{2,3,1,0:T(8,128)}, u32[]{:S(2)}) copy-start(f32[4,8,128,128]{2,3,1,0:T(8,128)} %get-tuple-element.31) | copy-start | bytes 6291460
  82.4 1.7 %copy-start.2 = (f32[4,8,128,128]{2,3,1,0:T(8,128)S(1)}, f32[4,8,128,128]{2,3,1,0:T(8,128)}, u32[]{:S(2)}) copy-start(f32[4,8,128,128]{2,3,1,0:T(8,128)} %get-tuple-element.33) | copy-start | bytes 6291460
  85.9 4.1 %copy-start.24 = (bf16[128,512]{0,1:T(8,128)(2,1)S(1)}, bf16[128,512]{0,1:T(8,128)(2,1)}, u32[]{:S(2)}) copy-start(bf16[128,512]{0,1:T(8,128)(2,1)} %copy-done.23) | copy-start | bytes 393220
  89.9 2.9 %copy-start.26 = (bf16[128,512]{0,1:T(8,128)(2,1)S(1)}, bf16[128,512]{0,1:T(8,128)(2,1)}, u32[]{:S(2)}) copy-start(bf16[128,512]{0,1:T(8,128)(2,1)} %copy-done.25) | copy-start | bytes 393220
  101.8 11.8 %collective-permute-start.16 = (f32[128,512]{1,0:T(8,128)}, f32[128,512]{1,0:T(8,128)}, u32[]{:S(2)}, u32[]{:S(2)}) collective-permute-start(f32[128,512]{1,0:T(8,128)} %copy.200), channel_id=1, source_target_pairs={{0,15},{1,0},{2,1},{3,2},{4,3},{5,4},{6,5},{7,6},{8,7},{9,8},{10,9... | collective-permute-start | bytes 786440 | tf_op jit(solution)/shard_map/ppermute | solution.py:14
  113.1 4.3 %copy-start.20 = (f32[128,512]{1,0:T(8,128)S(1)}, f32[128,512]{1,0:T(8,128)}, u32[]{:S(2)}) copy-start(f32[128,512]{1,0:T(8,128)} %copy.189) | copy-start | bytes 786436
  113.1 8.9 %copy-start.12 = (bf16[4,8,128,128]{2,3,1,0:T(8,128)(2,1)S(1)}, bf16[4,8,128,128]{2,3,1,0:T(8,128)(2,1)}, u32[]{:S(2)}) copy-start(bf16[4,8,128,128]{2,3,1,0:T(8,128)(2,1)} %fusion.1) | copy-start | bytes 3145732
  113.1 8.9 %copy-start.13 = (f32[4,8,128,128]{2,3,1,0:T(8,128)S(1)}, f32[4,8,128,128]{2,3,1,0:T(8,128)}, u32[]{:S(2)}) copy-start(f32[4,8,128,128]{2,3,1,0:T(8,128)} %fusion.60) | copy-start | bytes 6291460
  113.1 8.9 %copy-start.28 = (bf16[128,512]{0,1:T(8,128)(2,1)S(1)}, bf16[128,512]{0,1:T(8,128)(2,1)}, u32[]{:S(2)}) copy-start(bf16[128,512]{0,1:T(8,128)(2,1)} %copy-done.27) | copy-start | bytes 393220
  113.1 4.3 %collective-permute-start.12 = (f32[128,512]{1,0:T(8,128)}, f32[128,512]{1,0:T(8,128)S(1)}, u32[]{:S(2)}, u32[]{:S(2)}) collective-permute-start(f32[128,512]{1,0:T(8,128)} %copy.186), channel_id=1, source_target_pairs={{0,15},{1,0},{2,1},{3,2},{4,3},{5,4},{6,5},{7,6},{8,7},{9,8},{10,9... | collective-permute-start | bytes 786440 | tf_op jit(solution)/shard_map/ppermute | solution.py:14
  115.0 11.1 %collective-permute-start.17 = (f32[128,512]{1,0:T(8,128)S(1)}, f32[128,512]{1,0:T(8,128)S(1)}, u32[]{:S(2)}, u32[]{:S(2)}) collective-permute-start(f32[128,512]{1,0:T(8,128)S(1)} %add.129), channel_id=1, source_target_pairs={{0,15},{1,0},{2,1},{3,2},{4,3},{5,4},{6,5},{7,6},{8,7},{9,8},{10,9... | collective-permute-start | bytes 786440 | tf_op jit(solution)/shard_map/ppermute | solution.py:14
  117.4 8.6 %copy-start.18 = (f32[128,512]{1,0:T(8,128)S(1)}, f32[128,512]{1,0:T(8,128)}, u32[]{:S(2)}) copy-start(f32[128,512]{1,0:T(8,128)} %copy.204) | copy-start | bytes 786436
  117.5 8.9 %copy-start.19 = (f32[128,512]{1,0:T(8,128)S(1)}, f32[128,512]{1,0:T(8,128)}, u32[]{:S(2)}) copy-start(f32[128,512]{1,0:T(8,128)} %copy.192) | copy-start | bytes 786436
  117.5 13.2 %copy-start.3 = (f32[4,8,128,128]{2,3,1,0:T(8,128)S(1)}, f32[4,8,128,128]{2,3,1,0:T(8,128)}, u32[]{:S(2)}) copy-start(f32[4,8,128,128]{2,3,1,0:T(8,128)} %get-tuple-element.33) | copy-start | bytes 6291460
  117.5 8.9 %collective-permute-start.13 = (f32[128,512]{1,0:T(8,128)S(1)}, f32[128,512]{1,0:T(8,128)S(1)}, u32[]{:S(2)}, u32[]{:S(2)}) collective-permute-start(f32[128,512]{1,0:T(8,128)S(1)} %add.125), channel_id=1, source_target_pairs={{0,15},{1,0},{2,1},{3,2},{4,3},{5,4},{6,5},{7,6},{8,7},{9,8},{10,9... | collective-permute-start | bytes 786440 | tf_op jit(solution)/shard_map/ppermute | solution.py:14
  126.1 5.7 %copy-start.16 = (f32[128,512]{1,0:T(8,128)S(1)}, f32[128,512]{1,0:T(8,128)}, u32[]{:S(2)}) copy-start(f32[128,512]{1,0:T(8,128)} %copy.206) | copy-start | bytes 786436
  126.1 5.7 %collective-permute-start.18 = (f32[128,512]{1,0:T(8,128)S(1)}, f32[128,512]{1,0:T(8,128)S(1)}, u32[]{:S(2)}, u32[]{:S(2)}) collective-permute-start(f32[128,512]{1,0:T(8,128)S(1)} %add.130), channel_id=1, source_target_pairs={{0,15},{1,0},{2,1},{3,2},{4,3},{5,4},{6,5},{7,6},{8,7},{9,8},{10,9... | collective-permute-start | bytes 786440 | tf_op jit(solution)/shard_map/ppermute | solution.py:14
  126.4 9.2 %copy-start.17 = (f32[128,512]{1,0:T(8,128)S(1)}, f32[128,512]{1,0:T(8,128)}, u32[]{:S(2)}) copy-start(f32[128,512]{1,0:T(8,128)} %copy.195) | copy-start | bytes 786436
  126.4 9.2 %collective-permute-start.14 = (f32[128,512]{1,0:T(8,128)S(1)}, f32[128,512]{1,0:T(8,128)S(1)}, u32[]{:S(2)}, u32[]{:S(2)}) collective-permute-start(f32[128,512]{1,0:T(8,128)S(1)} %add.126), channel_id=1, source_target_pairs={{0,15},{1,0},{2,1},{3,2},{4,3},{5,4},{6,5},{7,6},{8,7},{9,8},{10,9... | collective-permute-start | bytes 786440 | tf_op jit(solution)/shard_map/ppermute | solution.py:14
  131.8 9.7 %copy-start.14 = (bf16[128,4,8,128]{0,3,2,1:T(8,128)(2,1)S(1)}, bf16[128,4,8,128]{0,3,2,1:T(8,128)(2,1)}, u32[]{:S(2)}) copy-start(bf16[128,4,8,128]{0,3,2,1:T(8,128)(2,1)} %get-tuple-element.36) | copy-start | bytes 3145732
  132.6 11.7 %collective-permute-start.19 = (f32[128,512]{1,0:T(8,128)}, f32[128,512]{1,0:T(8,128)}, u32[]{:S(2)}, u32[]{:S(2)}) collective-permute-start(f32[128,512]{1,0:T(8,128)} %add.131), channel_id=1, source_target_pairs={{0,15},{1,0},{2,1},{3,2},{4,3},{5,4},{6,5},{7,6},{8,7},{9,8},{10,9... | collective-permute-start | bytes 786440 | tf_op jit(solution)/shard_map/ppermute | solution.py:14
  136.3 9.6 %collective-permute-start.15 = (f32[128,512]{1,0:T(8,128)}, f32[128,512]{1,0:T(8,128)}, u32[]{:S(2)}, u32[]{:S(2)}) collective-permute-start(f32[128,512]{1,0:T(8,128)} %add.127), channel_id=1, source_target_pairs={{0,15},{1,0},{2,1},{3,2},{4,3},{5,4},{6,5},{7,6},{8,7},{9,8},{10,9... | collective-permute-start | bytes 786440 | tf_op jit(solution)/shard_map/ppermute | solution.py:14
  140.3 2.6 %copy-start.15 = (bf16[4,8,128,128]{2,3,1,0:T(8,128)(2,1)S(1)}, bf16[4,8,128,128]{2,3,1,0:T(8,128)(2,1)}, u32[]{:S(2)}) copy-start(bf16[4,8,128,128]{2,3,1,0:T(8,128)(2,1)} %multiply_convert_fusion) | copy-start | bytes 3145732
  (2 other events, 3.2 us)
where the time goes:
time: 148 us
  matrix products  49.2 us (33%)
  local copies, waits for them, and re-layouts  33.7 us (23%)
  waiting for transfers between devices  26 us (18%)
  starting transfers between devices  22.5 us (15%)
  other arithmetic  14.9 us (10%)
    ppermute x20, waiting for transfers between devices, from_behind(): lax.ppermute(value, axis, [(i, (i + by) % length) for i in range(length)])  26 us
    ppermute x20, starting transfers between devices, from_behind(): lax.ppermute(value, axis, [(i, (i + by) % length) for i in range(length)])  22.5 us
    dot_general x5, matrix products, on_device(): jnp.einsum('hgqk,khd->qhgd', context_weight_tile, context_value_block_row...  13.1 us
    dot_general x5, matrix products, on_device(): jnp.einsum('hgqk,khd->qhgd', score_grad, grads_key_block_rows, preferred_...  10.6 us
    unnamed x64, local copies, waits for them, and re-layouts  10 us
    dot_general x5, matrix products, scores_for(): jnp.einsum('qhgd,khd->hgqk', query_block_rows, key_block_rows, preferred_...  8.7 us
    reshape x5, local copies, waits for them, and re-layouts, on_device(): value_portion.reshape(token_count, KEY_VALUE_HEADS * HEAD_WIDTH)  8.38 us
    reshape x5, local copies, waits for them, and re-layouts, on_device(): key_portion.reshape(token_count, KEY_VALUE_HEADS * HEAD_WIDTH)  7.31 us
  transfers between devices with their start and end apart: 20, of which 9 were waited for; matrix products, arithmetic and copies ran while one was open for 42% of the time, Pallas kernels for 0%

commit v1 on v0

v1 whole, which is shorter than its diff:
```python
import functools

import jax
import jax.numpy as jnp
from jax import lax
from jax.experimental import pallas as pl
from jax.experimental.pallas import tpu as pltpu
from jax.sharding import PartitionSpec as P

QUERY_HEADS = 32
KEY_VALUE_HEADS = 4
HEAD_WIDTH = 128
SHARE = QUERY_HEADS // KEY_VALUE_HEADS
SCALE = HEAD_WIDTH**-0.5
LOG2_E = 1.4426950408889634
HIDDEN = -1e30
ID_BASE = 128
ID_ROWS = 16

NT = (((1,), (1,)), ((), ()))
NN = (((1,), (0,)), ((), ()))
TN = (((0,), (0,)), ((), ()))
f32 = jnp.float32
bf16 = jnp.bfloat16
VMEM = pl.BlockSpec(memory_space=pltpu.VMEM)
SMEM = pl.BlockSpec(memory_space=pltpu.SMEM)
PARAMS = pltpu.CompilerParams(vmem_limit_bytes=16 << 20)


def dot(a, b, dims):
    return lax.dot_general(a, b, dims, preferred_element_type=f32)


def heads(ref, first, count):
    w = HEAD_WIDTH
    return jnp.concatenate([ref[:, (first + j) * w : (first + j + 1) * w] for j in range(count)], axis=0)


def blocks(refs, core, group, t):
    c = slice(group * HEAD_WIDTH, (group + 1) * HEAD_WIDTH)
    own, near, near_other, far, sibling, far_other = [r[:t, c] for r in refs]
    last = jnp.where(core == 0, far_other, sibling)
    return jnp.concatenate([own, near, near_other, far, last], axis=0)


def ids_of(ref, t):
    row = ref[t : t + ID_ROWS, :].astype(f32)[:1]
    return row[:, :t] * ID_BASE + row[:, t : 2 * t]


def store_parts(total, group, t, own_ref, near_ref, far_ref, other_ref):
    c = slice(group * HEAD_WIDTH, (group + 1) * HEAD_WIDTH)
    own_ref[:, c] = total[:t]
    near_ref[:, c] = total[t : 2 * t].astype(bf16)
    far_ref[:, c] = total[3 * t : 4 * t].astype(bf16)
    other_ref[:t, c] = total[2 * t : 3 * t].astype(bf16)
    other_ref[t:, c] = total[4 * t :].astype(bf16)


def probs_kernel(core_ref, parent_ref, q_ref, do_ref, k0, k1, k2, k3, k4, k5,
                 p_ref, own_ref, near_ref, far_ref, other_ref, bias_ref):
    t = q_ref.shape[0]
    core = core_ref[0]
    refs = (k0, k1, k2, k3, k4, k5)
    own_ids = ids_of(k0, t)
    node = jnp.broadcast_to(own_ids, (t, t)).T[:, :1]
    parents = parent_ref[...].astype(f32)
    index = lax.broadcasted_iota(jnp.int32, (t, parents.shape[1]), 1).astype(f32)
    up = jnp.sum(jnp.where(index == node, parents, 0.0), axis=1, keepdims=True)
    upper = jnp.sum(jnp.where(index == up, parents, 0.0), axis=1, keepdims=True)
    tok = lax.broadcasted_iota(jnp.int32, (t, t), 0)
    key = lax.broadcasted_iota(jnp.int32, (t, t), 1)
    last_ids = jnp.where(core == 0, ids_of(k5, t), ids_of(k4, t))
    for slot, ids in enumerate((own_ids, ids_of(k1, t), ids_of(k2, t), ids_of(k3, t), last_ids)):
        seen = (ids == node) | (ids == up) | (ids == upper)
        if slot == 0:
            seen = seen & (key <= tok)
        bias_ref[slot * t : (slot + 1) * t, :] = jnp.where(seen, 0.0, HIDDEN).T
    for g in range(KEY_VALUE_HEADS):
        keys = blocks(refs, core, g, t)
        for h in range(g * SHARE, (g + 1) * SHARE, 2):
            bias = bias_ref[...]
            s = dot(keys, heads(q_ref, h, 2), NT) * (SCALE * LOG2_E) + jnp.concatenate([bias, bias], axis=1)
            e = jnp.exp2(s - jnp.max(s, axis=0, keepdims=True))
            inv = 1.0 / jnp.sum(e, axis=0, keepdims=True)
            p_ref[:, h * t : (h + 2) * t] = (e * inv).astype(bf16)
        dv = dot(p_ref[:, g * SHARE * t : (g + 1) * SHARE * t], heads(do_ref, g * SHARE, SHARE), NN)
        store_parts(dv, g, t, own_ref, near_ref, far_ref, other_ref)


def score_grad_kernel(core_ref, p_ref, q_ref, do_ref, v0, v1, v2, v3, v4, v5,
                      ds_ref, own_ref, near_ref, far_ref, other_ref):
    t = q_ref.shape[0]
    core = core_ref[0]
    refs = (v0, v1, v2, v3, v4, v5)
    for g in range(KEY_VALUE_HEADS):
        vals = blocks(refs, core, g, t)
        for h in range(g * SHARE, (g + 1) * SHARE, 2):
            c = slice(h * t, (h + 2) * t)
            dp = dot(vals, heads(do_ref, h, 2), NT)
            p = p_ref[:, c].astype(f32)
            delta = jnp.sum(p * dp, axis=0, keepdims=True)
            ds_ref[:, c] = (p * (dp - delta)).astype(bf16)
        dk = dot(ds_ref[:, g * SHARE * t : (g + 1) * SHARE * t], heads(q_ref, g * SHARE, SHARE), NN) * SCALE
        store_parts(dk, g, t, own_ref, near_ref, far_ref, other_ref)


def rows_kernel(core_ref, p_ref, ds_ref, k0, k1, k2, k3, k4, k5, v0, v1, v2, v3, v4, v5, o_ref, dq_ref):
    t = o_ref.shape[0]
    w = HEAD_WIDTH
    core = core_ref[0]
    for g in range(KEY_VALUE_HEADS):
        keys = blocks((k0, k1, k2, k3, k4, k5), core, g, t)
        vals = blocks((v0, v1, v2, v3, v4, v5), core, g, t)
        for h in range(g * SHARE, (g + 1) * SHARE, 2):
            c = slice(h * t, (h + 2) * t)
            o = dot(vals, p_ref[:, c], TN).astype(bf16)
            dq = (dot(keys, ds_ref[:, c], TN) * SCALE).astype(bf16)
            for j in range(2):
                o_ref[:, (h + j) * w : (h + j + 1) * w] = o[:, j * t : (j + 1) * t].T
                dq_ref[:, (h + j) * w : (h + j + 1) * w] = dq[:, j * t : (j + 1) * t].T


def parts_shapes(t):
    width = KEY_VALUE_HEADS * HEAD_WIDTH
    s = jax.ShapeDtypeStruct
    return [s((t, width), f32), s((t, width), bf16), s((t, width), bf16), s((2 * t, width), bf16)]


def ahead(value, by):
    n = lax.axis_size("seq")
    return lax.ppermute(value, "seq", [(i, (i + by) % n) for i in range(n)])


def swap(value):
    n = lax.axis_size("seq")
    return lax.ppermute(value, "seq", [(i, i ^ 1) for i in range(n)])


def spread(value):
    far = ahead(value, 4)
    near = ahead(value, 2)
    return value, near, swap(near), far, swap(value), swap(far)


def collect(own, near, far, other, first):
    t = own.shape[0]
    got = swap(other).astype(f32)
    near = (near.astype(f32) + got[:t]).astype(bf16)
    far = (far.astype(f32) + jnp.where(first, 0.0, got[t:])).astype(bf16)
    own = own + jnp.where(first, got[t:], 0.0)
    far, near = ahead(far, -4), ahead(near, -2)
    return (own + near.astype(f32) + far.astype(f32)).astype(bf16)


def on_device(queries, keys, values, output_gradient, node_of, parent):
    t = queries.shape[0]
    core = lax.axis_index("seq") % 2
    first = core == 0
    core = core.astype(jnp.int32).reshape(1)
    ids = jnp.concatenate([node_of // ID_BASE, node_of % ID_BASE]).astype(bf16)
    ids = jnp.pad(ids[None], ((0, ID_ROWS - 1), (0, keys.shape[1] - 2 * t)))
    ks = spread(jnp.concatenate([keys, ids], axis=0))
    vs = spread(values)
    s = jax.ShapeDtypeStruct
    grid_shape = s((5 * t, QUERY_HEADS * t), bf16)
    p, *dv = pl.pallas_call(
        probs_kernel,
        name="probs",
        in_specs=[SMEM] + [VMEM] * 9,
        out_specs=[VMEM] * 5,
        out_shape=[grid_shape] + parts_shapes(t),
        scratch_shapes=[pltpu.VMEM((5 * t, t), f32)],
        compiler_params=PARAMS,
    )(core, parent[None], queries, output_gradient, *ks)
    dv = collect(*dv, first)
    ds, *dk = pl.pallas_call(
        score_grad_kernel,
        name="score_grad",
        in_specs=[SMEM] + [VMEM] * 9,
        out_specs=[VMEM] * 5,
        out_shape=[grid_shape] + parts_shapes(t),
        compiler_params=PARAMS,
    )(core, p, queries, output_gradient, *vs)
    dk = collect(*dk, first)
    attended, q_grad = pl.pallas_call(
        rows_kernel,
        name="rows",
        in_specs=[SMEM] + [VMEM] * 14,
        out_specs=[VMEM] * 2,
        out_shape=[s(queries.shape, bf16), s(queries.shape, bf16)],
        compiler_params=PARAMS,
    )(core, p, ds, *ks, *vs)
    return attended, q_grad, dk, dv


def solution(mesh):
    rows = P(("grp", "seq"), None)
    return jax.shard_map(
        on_device,
        mesh=mesh,
        in_specs=(rows, rows, rows, rows, P(("grp", "seq")), P("grp")),
        out_specs=(rows, rows, rows, rows),
        check_vma=False,
    )
```

time: 148 us -> 65.1 us (0.44)
  matrix products: 49.2 us -> 0 us
  local copies, waits for them, and re-layouts: 33.7 us -> 16.1 us
  Pallas kernels: 0 us -> 14.4 us
  waiting for transfers between devices: 26 us -> 14.6 us
  other arithmetic: 14.9 us -> 4.28 us
  starting transfers between devices: 22.5 us -> 14.6 us
    dot_general x30 -> x0, matrix products: 49.2 us -> none  [the longest x5 13.1 us: on_device(): jnp.einsum('hgqk,khd->qhgd', context_weight_tile, context_value_block_row...]
    reshape x14 -> x0, local copies, waits for them, and re-layouts: 18.4 us -> none  [the longest x5 8.38 us: on_device(): value_portion.reshape(token_count, KEY_VALUE_HEADS * HEAD_WIDTH)]
    pallas_call x0 -> x3, Pallas kernels: none -> 14.4 us  [the longest x1 5.58 us: on_device(): pl.pallas_call(probs_kernel, name='probs', in_specs=[SMEM] + [VMEM] * 9,...]
    ppermute x20 -> x16, waiting for transfers between devices: 26 us -> 14.6 us  [the longest x8 13.5 us: ahead(): return lax.ppermute(value, 'seq', [(i, (i + by) % n) for i in range(n)])]
    ppermute x20 -> x16, starting transfers between devices: 22.5 us -> 14.6 us  [the longest x8 12.7 us: ahead(): return lax.ppermute(value, 'seq', [(i, (i + by) % n) for i in range(n)])]
    reduce_sum x2 -> x0, other arithmetic: 7.17 us -> none  [the longest x1 6.81 us: on_device(): jnp.sum(jnp.exp(score_tiles[token_offset] - row_max[..., None]), axis=3)]
    unnamed x64 -> x22, local copies, waits for them, and re-layouts: 10 us -> 16.1 us
    add x7 -> x0, other arithmetic: 2.92 us -> none  [the longest x3 2.1 us: on_device(): value_total = value_total + value_parts[token_offset]]
  transfers between devices with their start and end apart: 20 -> 16, of which waited for: 9 -> 7; matrix products, arithmetic and copies ran while one was open for 42% -> 3% of each run, Pallas kernels for 0% -> 22%
where the time goes in v1:
time: 65.1 us; the launch traced here: 64.6 us
  local copies, waits for them, and re-layouts  16.1 us (25%)
  starting transfers between devices  14.6 us (22%)
  waiting for transfers between devices  14.6 us (22%)
  Pallas kernels  14.4 us (22%)
  other arithmetic  4.28 us (7%)
  between operations  0.73 us (1%)
    unnamed x22, local copies, waits for them, and re-layouts  16.1 us
    ppermute x8, waiting for transfers between devices, ahead(): return lax.ppermute(value, 'seq', [(i, (i + by) % n) for i in range(n)])  13.5 us
    ppermute x8, starting transfers between devices, ahead(): return lax.ppermute(value, 'seq', [(i, (i + by) % n) for i in range(n)])  12.7 us
    pallas_call x1, Pallas kernels, on_device(): pl.pallas_call(probs_kernel, name='probs', in_specs=[SMEM] + [VMEM] * 9,...  5.58 us
    pallas_call x1, Pallas kernels, on_device(): pl.pallas_call(score_grad_kernel, name='score_grad', in_specs=[SMEM] + [V...  5.39 us
    pallas_call x1, Pallas kernels, on_device(): pl.pallas_call(rows_kernel, name='rows', in_specs=[SMEM] + [VMEM] * 14, o...  3.43 us
    ppermute x8, starting transfers between devices, swap(): return lax.ppermute(value, 'seq', [(i, i ^ 1) for i in range(n)])  1.88 us
    convert_element_type x2, other arithmetic, collect(): return (own + near.astype(f32) + far.astype(f32)).astype(bf16)  1.47 us
  transfers between devices with their start and end apart: 16, of which 7 were waited for; matrix products, arithmetic and copies ran while one was open for 3% of the time, Pallas kernels for 22%

profile of v1, /device:TPU:0, one launch (start us, length us, event | category | flops | bytes accessed | tf_op | source)
XLA Modules:
  0.0 64.6 jit_solution(13959393826203480976)
XLA Ops:
  0.6 0.7 %convert_bitcast_fusion = (bf16[1,128]{1,0:T(2,128)(2,1)S(1)}, bf16[1,128]{1,0:T(2,128)(2,1)S(1)}) fusion(s32[128]{0:T(128)} %param.10), kind=kLoop, calls=%fused_computation.24 | loop fusion | flops 2688 | bytes 1024 | tf_op jit(solution)/shard_map/concatenate | solution.py:161
  1.3 0.9 %pad_maximum_fusion.k0 = bf16[144,512]{1,0:T(8,128)(2,1)S(1)} fusion(bf16[16,512]{1,0:T(8,128)(2,1)S(1)} %fusion.7, bf16[128,512]{1,0:T(8,128)(2,1)} %param.7), kind=kLoop, calls=%fused_computation.8 | loop fusion | flops 294912 | bytes 294912 | tf_op jit(solution)/shard_map/concatenate | solution.py:163
  2.2 3.0 %collective-permute-start = (bf16[144,512]{1,0:T(8,128)(2,1)S(1)}, bf16[144,512]{1,0:T(8,128)(2,1)S(1)}, u32[]{:S(2)}, u32[]{:S(2)}) collective-permute-start(bf16[144,512]{1,0:T(8,128)(2,1)S(1)} %pad_maximum_fusion.k0), channel_id=1, source_target_pairs={{0,2},{1,3},{2,4},{3,5},{4,6},{5,7},{6,8},{7,9},{8,10},{9,11},{10,... | collective-permute-start | bytes 442376 | tf_op jit(solution)/shard_map/ppermute | solution.py:132
  5.2 1.6 %collective-permute-start.2 = (bf16[144,512]{1,0:T(8,128)(2,1)S(1)}, bf16[144,512]{1,0:T(8,128)(2,1)S(1)}, u32[]{:S(2)}, u32[]{:S(2)}) collective-permute-start(bf16[144,512]{1,0:T(8,128)(2,1)S(1)} %pad_maximum_fusion.k0), channel_id=1, source_target_pairs={{0,4},{1,5},{2,6},{3,7},{4,8},{5,9},{6,10},{7,11},{8,12},{9,13},{1... | collective-permute-start | bytes 442376 | tf_op jit(solution)/shard_map/ppermute | solution.py:132
  6.8 0.0 collective-permute-start.3
  6.8 6.1 %collective-permute-done.k1 = bf16[144,512]{1,0:T(8,128)(2,1)S(1)} collective-permute-done((bf16[144,512]{1,0:T(8,128)(2,1)S(1)}, bf16[144,512]{1,0:T(8,128)(2,1)S(1)}, u32[]{:S(2)}, u32[]{:S(2)}) %collective-permute-start) | collective-permute-done | bytes 147488 | tf_op jit(solution)/shard_map/ppermute | solution.py:132
  13.0 0.5 collective-permute-start.4
  13.5 2.4 %collective-permute-start.5 = (bf16[128,512]{1,0:T(8,128)(2,1)}, bf16[128,512]{1,0:T(8,128)(2,1)S(1)}, u32[]{:S(2)}, u32[]{:S(2)}) collective-permute-start(bf16[128,512]{1,0:T(8,128)(2,1)} %v0.3), channel_id=1, source_target_pairs={{0,2},{1,3},{2,4},{3,5},{4,6},{5,7},{6,8},{7,9},{8,10},{9,11},{10,... | collective-permute-start | bytes 393224 | tf_op jit(solution)/shard_map/ppermute | solution.py:132
  15.9 0.0 collective-permute-done.3.k4
  15.9 0.0 collective-permute-done.1.k2
  15.9 0.0 copy-start.4
  15.9 1.2 %copy-done.4 = bf16[128,4096]{1,0:T(8,128)(2,1)S(1)} copy-done((bf16[128,4096]{1,0:T(8,128)(2,1)S(1)}, bf16[128,4096]{1,0:T(8,128)(2,1)}, u32[]{:S(2)}) %copy-start.4) | copy-done | bytes 1048600
  17.1 1.2 %copy-done.6 = bf16[128,4096]{1,0:T(8,128)(2,1)S(1)} copy-done((bf16[128,4096]{1,0:T(8,128)(2,1)S(1)}, bf16[128,4096]{1,0:T(8,128)(2,1)}, u32[]{:S(2)}) %copy-start.6) | copy-done | bytes 1048600
  18.3 0.7 %copy-done.10 = s32[84]{0:T(128)S(1)} copy-done((s32[84]{0:T(128)S(1)}, s32[84]{0:T(128)}, u32[]{:S(2)}) %copy-start.10) | copy-done | bytes 360
  19.0 5.6 %probs.1 = (bf16[640,4096]{1,0:T(8,128)(2,1)S(1)}, f32[128,512]{1,0:T(8,128)S(1)}, bf16[128,512]{1,0:T(8,128)(2,1)S(1)}, bf16[128,512]{1,0:T(8,128)(2,1)S(1)}, bf16[256,512]{1,0:T(8,128)(2,1)S(1)}) custom-call(s32[1]{0:T(128)} %bitcast.core_ref, s32[1,84]{1,0:T(1,128)S(1)} %bitcast.6, bf16[128,4096]{1,0:T(8,128)(2,1)S(1)} %copy-done.4, ...), custom_call_target="tpu_custom_call" | custom-call | tf_op jit(solution)/shard_map/probs/pallas_call | solution.py:167
  24.6 0.3 collective-permute-start.13
  24.9 0.3 collective-permute-start.8
  25.2 0.0 collective-permute-done.5.v1
  25.2 0.2 collective-permute-start.6
  25.4 0.3 collective-permute-start.9
  25.7 0.9 %collective-permute-done.8.v4 = bf16[128,512]{1,0:T(8,128)(2,1)S(1)} collective-permute-done((bf16[128,512]{1,0:T(8,128)(2,1)}, bf16[128,512]{1,0:T(8,128)(2,1)S(1)}, u32[]{:S(2)}, u32[]{:S(2)}) %collective-permute-start.8) | collective-permute-done | bytes 131104 | tf_op jit(solution)/shard_map/ppermute | solution.py:137
  26.6 0.0 collective-permute-done.6.v2
  26.6 0.2 collective-permute-done.9.v5
  26.7 1.2 %copy-done.5 = bf16[128,4096]{1,0:T(8,128)(2,1)S(1)} copy-done((bf16[128,4096]{1,0:T(8,128)(2,1)S(1)}, bf16[128,4096]{1,0:T(8,128)(2,1)}, u32[]{:S(2)}) %copy-start.5) | copy-done | bytes 1048600
  28.0 1.2 %copy-done.7 = bf16[128,4096]{1,0:T(8,128)(2,1)S(1)} copy-done((bf16[128,4096]{1,0:T(8,128)(2,1)S(1)}, bf16[128,4096]{1,0:T(8,128)(2,1)}, u32[]{:S(2)}) %copy-start.7) | copy-done | bytes 1048600
  29.2 0.9 %copy-done.8 = bf16[128,512]{1,0:T(8,128)(2,1)S(1)} copy-done((bf16[128,512]{1,0:T(8,128)(2,1)S(1)}, bf16[128,512]{1,0:T(8,128)(2,1)}, u32[]{:S(2)}) %copy-start.8) | copy-done | bytes 131096
  30.1 5.4 %score_grad.1 = (bf16[640,4096]{1,0:T(8,128)(2,1)S(1)}, f32[128,512]{1,0:T(8,128)S(1)}, bf16[128,512]{1,0:T(8,128)(2,1)S(1)}, bf16[128,512]{1,0:T(8,128)(2,1)S(1)}, bf16[256,512]{1,0:T(8,128)(2,1)S(1)}) custom-call(s32[1]{0:T(128)} %bitcast.core_ref, bf16[640,4096]{1,0:T(8,128)(2,1)S(1)} %get-tuple-element.16.p_ref, bf16[128,4096]{1,0:T(8,128)(2,1)S(1)} %copy-done.5, ...), custom_call_target="tpu_custom_call" | custom-call | tf_op jit(solution)/shard_map/score_grad/pallas_call | solution.py:177
  35.5 2.3 %copy-done = bf16[640,4096]{1,0:T(8,128)(2,1)} copy-done((bf16[640,4096]{1,0:T(8,128)(2,1)}, bf16[640,4096]{1,0:T(8,128)(2,1)S(1)}, u32[]{:S(2)}) %copy-start) | copy-done | bytes 5242904
  37.8 2.4 %copy-done.2 = bf16[640,4096]{1,0:T(8,128)(2,1)} copy-done((bf16[640,4096]{1,0:T(8,128)(2,1)}, bf16[640,4096]{1,0:T(8,128)(2,1)S(1)}, u32[]{:S(2)}) %copy-start.2) | copy-done | bytes 5242904
  40.2 0.3 collective-permute-start.10
  40.5 2.5 %copy-done.1 = bf16[640,4096]{1,0:T(8,128)(2,1)S(1)} copy-done((bf16[640,4096]{1,0:T(8,128)(2,1)S(1)}, bf16[640,4096]{1,0:T(8,128)(2,1)}, u32[]{:S(2)}) %copy-start.1) | copy-done | bytes 5242904
  43.0 2.5 %copy-done.3 = bf16[640,4096]{1,0:T(8,128)(2,1)S(1)} copy-done((bf16[640,4096]{1,0:T(8,128)(2,1)S(1)}, bf16[640,4096]{1,0:T(8,128)(2,1)}, u32[]{:S(2)}) %copy-start.3) | copy-done | bytes 5242904
  45.4 3.4 %rows.1 = (bf16[128,4096]{1,0:T(8,128)(2,1)}, bf16[128,4096]{1,0:T(8,128)(2,1)}) custom-call(s32[1]{0:T(128)} %bitcast.core_ref, bf16[640,4096]{1,0:T(8,128)(2,1)S(1)} %copy-done.1, bf16[640,4096]{1,0:T(8,128)(2,1)S(1)} %copy-done.3, bf16[144,512]{1,0:T(8,128)(2,1)S(1)} %pad_maximum_fusion.k0, bf16[144,512]{1,0:T(8,128)(2,1)S(1)} %collective-permute-done.k1, ...), custom_call_target="tpu_custom_call" | custom-call | tf_op jit(solution)/shard_map/rows/pallas_call | solution.py:186
  48.9 0.0 collective-permute-done.13
  48.9 0.1 convert_element_type.66
  48.9 0.1 fusion
  49.0 3.3 %collective-permute-start.14 = (bf16[128,512]{1,0:T(8,128)(2,1)S(1)}, bf16[128,512]{1,0:T(8,128)(2,1)S(1)}, u32[]{:S(2)}, u32[]{:S(2)}) collective-permute-start(bf16[128,512]{1,0:T(8,128)(2,1)S(1)} %get-tuple-element.28), channel_id=1, source_target_pairs={{0,14},{1,15},{2,0},{3,1},{4,2},{5,3},{6,4},{7,5},{8,6},{9,7},{10,... | collective-permute-start | bytes 393224 | tf_op jit(solution)/shard_map/ppermute | solution.py:132
  52.3 1.1 %collective-permute-start.15 = (bf16[128,512]{1,0:T(8,128)(2,1)S(1)}, bf16[128,512]{1,0:T(8,128)(2,1)S(1)}, u32[]{:S(2)}, u32[]{:S(2)}) collective-permute-start(bf16[128,512]{1,0:T(8,128)(2,1)S(1)} %get-tuple-element.29), channel_id=1, source_target_pairs={{0,12},{1,13},{2,14},{3,15},{4,0},{5,1},{6,2},{7,3},{8,4},{9,5},{1... | collective-permute-start | bytes 393224 | tf_op jit(solution)/shard_map/ppermute | solution.py:132
  53.4 1.0 %convert_element_type.58 = f32[256,512]{1,0:T(8,128)S(1)} convert(bf16[256,512]{1,0:T(8,128)(2,1)} %collective-permute-done.10) | non-fusion elementwise | flops 131072 | bytes 786432 | tf_op jit(solution)/shard_map/convert_element_type | solution.py:148
  54.4 0.1 fusion.1
  54.5 1.0 %collective-permute-start.11 = (bf16[128,512]{1,0:T(8,128)(2,1)S(1)}, bf16[128,512]{1,0:T(8,128)(2,1)S(1)}, u32[]{:S(2)}, u32[]{:S(2)}) collective-permute-start(bf16[128,512]{1,0:T(8,128)(2,1)S(1)} %get-tuple-element.30), channel_id=1, source_target_pairs={{0,14},{1,15},{2,0},{3,1},{4,2},{5,3},{6,4},{7,5},{8,6},{9,7},{10,... | collective-permute-start | bytes 393224 | tf_op jit(solution)/shard_map/ppermute | solution.py:132
  55.5 0.3 collective-permute-start.12
  55.8 0.3 collective-permute-done.14
  56.2 2.8 %collective-permute-done.15 = bf16[128,512]{1,0:T(8,128)(2,1)S(1)} collective-permute-done((bf16[128,512]{1,0:T(8,128)(2,1)S(1)}, bf16[128,512]{1,0:T(8,128)(2,1)S(1)}, u32[]{:S(2)}, u32[]{:S(2)}) %collective-permute-start.15) | collective-permute-done | bytes 131104 | tf_op jit(solution)/shard_map/ppermute | solution.py:132
  59.0 0.7 %add_convert_fusion = bf16[128,512]{1,0:T(8,128)(2,1)} fusion(bf16[128,512]{1,0:T(8,128)(2,1)S(1)} %collective-permute-done.15, bf16[128,512]{1,0:T(8,128)(2,1)S(1)} %collective-permute-done.14, f32[128,512]{1,0:T(8,128)S(1)} %get-tuple-element.24, f32[256,512]{1,0:T(8,128)S(1)} %convert_element_type.66, pred[]{:T(512)S(6)} %eq.7), kind=kLoop, calls=%fused_computation.4 | loop fusion | flops 458752 | bytes 917505 | tf_op jit(solution)/shard_map/convert_element_type | solution.py:153
  59.7 2.1 %collective-permute-done.11 = bf16[128,512]{1,0:T(8,128)(2,1)S(1)} collective-permute-done((bf16[128,512]{1,0:T(8,128)(2,1)S(1)}, bf16[128,512]{1,0:T(8,128)(2,1)S(1)}, u32[]{:S(2)}, u32[]{:S(2)}) %collective-permute-start.11) | collective-permute-done | bytes 131104 | tf_op jit(solution)/shard_map/ppermute | solution.py:132
  61.8 2.1 %collective-permute-done.12 = bf16[128,512]{1,0:T(8,128)(2,1)S(1)} collective-permute-done((bf16[128,512]{1,0:T(8,128)(2,1)S(1)}, bf16[128,512]{1,0:T(8,128)(2,1)S(1)}, u32[]{:S(2)}, u32[]{:S(2)}) %collective-permute-start.12) | collective-permute-done | bytes 131104 | tf_op jit(solution)/shard_map/ppermute | solution.py:132
  63.9 0.7 %add_convert_fusion.2 = bf16[128,512]{1,0:T(8,128)(2,1)} fusion(bf16[128,512]{1,0:T(8,128)(2,1)S(1)} %collective-permute-done.12, bf16[128,512]{1,0:T(8,128)(2,1)S(1)} %collective-permute-done.11, f32[128,512]{1,0:T(8,128)S(1)} %get-tuple-element.20, f32[256,512]{1,0:T(8,128)S(1)} %convert_element_type.58, pred[]{:T(512)S(6)} %eq.7), kind=kLoop, calls=%fused_computation.6 | loop fusion | flops 458752 | bytes 917505 | tf_op jit(solution)/shard_map/convert_element_type | solution.py:153
  (18 shorter events, 0.0 us)
Async XLA Ops:
  2.2 10.7 %collective-permute-start = (bf16[144,512]{1,0:T(8,128)(2,1)S(1)}, bf16[144,512]{1,0:T(8,128)(2,1)S(1)}, u32[]{:S(2)}, u32[]{:S(2)}) collective-permute-start(bf16[144,512]{1,0:T(8,128)(2,1)S(1)} %pad_maximum_fusion.k0), channel_id=1, source_target_pairs={{0,2},{1,3},{2,4},{3,5},{4,6},{5,7},{6,8},{7,9},{8,10},{9,11},{10,... | collective-permute-start | bytes 442376 | tf_op jit(solution)/shard_map/ppermute | solution.py:132
  5.2 7.7 %collective-permute-start.2 = (bf16[144,512]{1,0:T(8,128)(2,1)S(1)}, bf16[144,512]{1,0:T(8,128)(2,1)S(1)}, u32[]{:S(2)}, u32[]{:S(2)}) collective-permute-start(bf16[144,512]{1,0:T(8,128)(2,1)S(1)} %pad_maximum_fusion.k0), channel_id=1, source_target_pairs={{0,4},{1,5},{2,6},{3,7},{4,8},{5,9},{6,10},{7,11},{8,12},{9,13},{1... | collective-permute-start | bytes 442376 | tf_op jit(solution)/shard_map/ppermute | solution.py:132
  6.8 9.0 %collective-permute-start.3 = (bf16[144,512]{1,0:T(8,128)(2,1)S(1)}, bf16[144,512]{1,0:T(8,128)(2,1)S(1)}, u32[]{:S(2)}, u32[]{:S(2)}) collective-permute-start(bf16[144,512]{1,0:T(8,128)(2,1)S(1)} %pad_maximum_fusion.k0), channel_id=1, source_target_pairs={{0,1},{1,0},{2,3},{3,2},{4,5},{5,4},{6,7},{7,6},{8,9},{9,8},{10,11... | collective-permute-start | bytes 442376 | tf_op jit(solution)/shard_map/ppermute | solution.py:137
  13.0 2.9 %collective-permute-start.1 = (bf16[144,512]{1,0:T(8,128)(2,1)S(1)}, bf16[144,512]{1,0:T(8,128)(2,1)S(1)}, u32[]{:S(2)}, u32[]{:S(2)}) collective-permute-start(bf16[144,512]{1,0:T(8,128)(2,1)S(1)} %collective-permute-done.k1), channel_id=1, source_target_pairs={{0,1},{1,0},{2,3},{3,2},{4,5},{5,4},{6,7},{7,6},{8,9},{9,8},{10,11... | collective-permute-start | bytes 442376 | tf_op jit(solution)/shard_map/ppermute | solution.py:137
  13.0 2.9 %collective-permute-start.4 = (bf16[144,512]{1,0:T(8,128)(2,1)S(1)}, bf16[144,512]{1,0:T(8,128)(2,1)S(1)}, u32[]{:S(2)}, u32[]{:S(2)}) collective-permute-start(bf16[144,512]{1,0:T(8,128)(2,1)S(1)} %collective-permute-done.2.k3), channel_id=1, source_target_pairs={{0,1},{1,0},{2,3},{3,2},{4,5},{5,4},{6,7},{7,6},{8,9},{9,8},{10,11... | collective-permute-start | bytes 442376 | tf_op jit(solution)/shard_map/ppermute | solution.py:137
  13.5 11.7 %collective-permute-start.5 = (bf16[128,512]{1,0:T(8,128)(2,1)}, bf16[128,512]{1,0:T(8,128)(2,1)S(1)}, u32[]{:S(2)}, u32[]{:S(2)}) collective-permute-start(bf16[128,512]{1,0:T(8,128)(2,1)} %v0.3), channel_id=1, source_target_pairs={{0,2},{1,3},{2,4},{3,5},{4,6},{5,7},{6,8},{7,9},{8,10},{9,11},{10,... | collective-permute-start | bytes 393224 | tf_op jit(solution)/shard_map/ppermute | solution.py:132
  15.9 9.5 %collective-permute-start.7 = (bf16[128,512]{1,0:T(8,128)(2,1)}, bf16[128,512]{1,0:T(8,128)(2,1)S(1)}, u32[]{:S(2)}, u32[]{:S(2)}) collective-permute-start(bf16[128,512]{1,0:T(8,128)(2,1)} %v0.3), channel_id=1, source_target_pairs={{0,4},{1,5},{2,6},{3,7},{4,8},{5,9},{6,10},{7,11},{8,12},{9,13},{1... | collective-permute-start | bytes 393224 | tf_op jit(solution)/shard_map/ppermute | solution.py:132
  15.9 1.2 %copy-start.4 = (bf16[128,4096]{1,0:T(8,128)(2,1)S(1)}, bf16[128,4096]{1,0:T(8,128)(2,1)}, u32[]{:S(2)}) copy-start(bf16[128,4096]{1,0:T(8,128)(2,1)} %q_ref.3) | copy-start | bytes 3145732
  17.1 1.2 %copy-start.6 = (bf16[128,4096]{1,0:T(8,128)(2,1)S(1)}, bf16[128,4096]{1,0:T(8,128)(2,1)}, u32[]{:S(2)}) copy-start(bf16[128,4096]{1,0:T(8,128)(2,1)} %do_ref.3) | copy-start | bytes 3145732
  18.3 0.7 %copy-start.10 = (s32[84]{0:T(128)S(1)}, s32[84]{0:T(128)}, u32[]{:S(2)}) copy-start(s32[84]{0:T(128)} %param.11) | copy-start | bytes 1012
  19.0 21.5 %copy-start.9 = (bf16[128,512]{1,0:T(8,128)(2,1)S(1)}, bf16[128,512]{1,0:T(8,128)(2,1)}, u32[]{:S(2)}) copy-start(bf16[128,512]{1,0:T(8,128)(2,1)} %v0.3) | copy-start | bytes 393220
  24.6 24.3 %collective-permute-start.13 = (bf16[256,512]{1,0:T(8,128)(2,1)S(1)}, bf16[256,512]{1,0:T(8,128)(2,1)S(1)}, u32[]{:S(2)}, u32[]{:S(2)}) collective-permute-start(bf16[256,512]{1,0:T(8,128)(2,1)S(1)} %get-tuple-element.25), channel_id=1, source_target_pairs={{0,1},{1,0},{2,3},{3,2},{4,5},{5,4},{6,7},{7,6},{8,9},{9,8},{10,11... | collective-permute-start | bytes 786440 | tf_op jit(solution)/shard_map/ppermute | solution.py:137
  24.9 1.7 %collective-permute-start.8 = (bf16[128,512]{1,0:T(8,128)(2,1)}, bf16[128,512]{1,0:T(8,128)(2,1)S(1)}, u32[]{:S(2)}, u32[]{:S(2)}) collective-permute-start(bf16[128,512]{1,0:T(8,128)(2,1)} %v0.3), channel_id=1, source_target_pairs={{0,1},{1,0},{2,3},{3,2},{4,5},{5,4},{6,7},{7,6},{8,9},{9,8},{10,11... | collective-permute-start | bytes 393224 | tf_op jit(solution)/shard_map/ppermute | solution.py:137
  25.2 1.4 %collective-permute-start.6 = (bf16[128,512]{1,0:T(8,128)(2,1)S(1)}, bf16[128,512]{1,0:T(8,128)(2,1)S(1)}, u32[]{:S(2)}, u32[]{:S(2)}) collective-permute-start(bf16[128,512]{1,0:T(8,128)(2,1)S(1)} %collective-permute-done.5.v1), channel_id=1, source_target_pairs={{0,1},{1,0},{2,3},{3,2},{4,5},{5,4},{6,7},{7,6},{8,9},{9,8},{10,11... | collective-permute-start | bytes 393224 | tf_op jit(solution)/shard_map/ppermute | solution.py:137
  25.4 1.4 %collective-permute-start.9 = (bf16[128,512]{1,0:T(8,128)(2,1)S(1)}, bf16[128,512]{1,0:T(8,128)(2,1)S(1)}, u32[]{:S(2)}, u32[]{:S(2)}) collective-permute-start(bf16[128,512]{1,0:T(8,128)(2,1)S(1)} %collective-permute-done.7.v3), channel_id=1, source_target_pairs={{0,1},{1,0},{2,3},{3,2},{4,5},{5,4},{6,7},{7,6},{8,9},{9,8},{10,11... | collective-permute-start | bytes 393224 | tf_op jit(solution)/shard_map/ppermute | solution.py:137
  26.7 1.2 %copy-start.5 = (bf16[128,4096]{1,0:T(8,128)(2,1)S(1)}, bf16[128,4096]{1,0:T(8,128)(2,1)}, u32[]{:S(2)}) copy-start(bf16[128,4096]{1,0:T(8,128)(2,1)} %q_ref.3) | copy-start | bytes 3145732
  28.0 1.2 %copy-start.7 = (bf16[128,4096]{1,0:T(8,128)(2,1)S(1)}, bf16[128,4096]{1,0:T(8,128)(2,1)}, u32[]{:S(2)}) copy-start(bf16[128,4096]{1,0:T(8,128)(2,1)} %do_ref.3) | copy-start | bytes 3145732
  29.2 0.9 %copy-start.8 = (bf16[128,512]{1,0:T(8,128)(2,1)S(1)}, bf16[128,512]{1,0:T(8,128)(2,1)}, u32[]{:S(2)}) copy-start(bf16[128,512]{1,0:T(8,128)(2,1)} %v0.3) | copy-start | bytes 393220
  35.5 2.3 %copy-start = (bf16[640,4096]{1,0:T(8,128)(2,1)}, bf16[640,4096]{1,0:T(8,128)(2,1)S(1)}, u32[]{:S(2)}) copy-start(bf16[640,4096]{1,0:T(8,128)(2,1)S(1)} %get-tuple-element.16.p_ref) | copy-start | bytes 15728644
  37.8 2.4 %copy-start.2 = (bf16[640,4096]{1,0:T(8,128)(2,1)}, bf16[640,4096]{1,0:T(8,128)(2,1)S(1)}, u32[]{:S(2)}) copy-start(bf16[640,4096]{1,0:T(8,128)(2,1)S(1)} %get-tuple-element.17.ds_ref) | copy-start | bytes 15728644
  40.2 13.2 %collective-permute-start.10 = (bf16[256,512]{1,0:T(8,128)(2,1)S(1)}, bf16[256,512]{1,0:T(8,128)(2,1)}, u32[]{:S(2)}, u32[]{:S(2)}) collective-permute-start(bf16[256,512]{1,0:T(8,128)(2,1)S(1)} %get-tuple-element.21), channel_id=1, source_target_pairs={{0,1},{1,0},{2,3},{3,2},{4,5},{5,4},{6,7},{7,6},{8,9},{9,8},{10,11... | collective-permute-start | bytes 786440 | tf_op jit(solution)/shard_map/ppermute | solution.py:137
  40.5 2.5 %copy-start.1 = (bf16[640,4096]{1,0:T(8,128)(2,1)S(1)}, bf16[640,4096]{1,0:T(8,128)(2,1)}, u32[]{:S(2)}) copy-start(bf16[640,4096]{1,0:T(8,128)(2,1)} %copy-done) | copy-start | bytes 15728644
  43.0 2.5 %copy-start.3 = (bf16[640,4096]{1,0:T(8,128)(2,1)S(1)}, bf16[640,4096]{1,0:T(8,128)(2,1)}, u32[]{:S(2)}) copy-start(bf16[640,4096]{1,0:T(8,128)(2,1)} %copy-done.2) | copy-start | bytes 15728644
  49.0 7.1 %collective-permute-start.14 = (bf16[128,512]{1,0:T(8,128)(2,1)S(1)}, bf16[128,512]{1,0:T(8,128)(2,1)S(1)}, u32[]{:S(2)}, u32[]{:S(2)}) collective-permute-start(bf16[128,512]{1,0:T(8,128)(2,1)S(1)} %get-tuple-element.28), channel_id=1, source_target_pairs={{0,14},{1,15},{2,0},{3,1},{4,2},{5,3},{6,4},{7,5},{8,6},{9,7},{10,... | collective-permute-start | bytes 393224 | tf_op jit(solution)/shard_map/ppermute | solution.py:132
  52.3 6.7 %collective-permute-start.15 = (bf16[128,512]{1,0:T(8,128)(2,1)S(1)}, bf16[128,512]{1,0:T(8,128)(2,1)S(1)}, u32[]{:S(2)}, u32[]{:S(2)}) collective-permute-start(bf16[128,512]{1,0:T(8,128)(2,1)S(1)} %get-tuple-element.29), channel_id=1, source_target_pairs={{0,12},{1,13},{2,14},{3,15},{4,0},{5,1},{6,2},{7,3},{8,4},{9,5},{1... | collective-permute-start | bytes 393224 | tf_op jit(solution)/shard_map/ppermute | solution.py:132
  54.5 7.3 %collective-permute-start.11 = (bf16[128,512]{1,0:T(8,128)(2,1)S(1)}, bf16[128,512]{1,0:T(8,128)(2,1)S(1)}, u32[]{:S(2)}, u32[]{:S(2)}) collective-permute-start(bf16[128,512]{1,0:T(8,128)(2,1)S(1)} %get-tuple-element.30), channel_id=1, source_target_pairs={{0,14},{1,15},{2,0},{3,1},{4,2},{5,3},{6,4},{7,5},{8,6},{9,7},{10,... | collective-permute-start | bytes 393224 | tf_op jit(solution)/shard_map/ppermute | solution.py:132
  55.5 8.4 %collective-permute-start.12 = (bf16[128,512]{1,0:T(8,128)(2,1)S(1)}, bf16[128,512]{1,0:T(8,128)(2,1)S(1)}, u32[]{:S(2)}, u32[]{:S(2)}) collective-permute-start(bf16[128,512]{1,0:T(8,128)(2,1)S(1)} %get-tuple-element.31), channel_id=1, source_target_pairs={{0,12},{1,13},{2,14},{3,15},{4,0},{5,1},{6,2},{7,3},{8,4},{9,5},{1... | collective-permute-start | bytes 393224 | tf_op jit(solution)/shard_map/ppermute | solution.py:132

commit v2 on v1

v2 whole, which is shorter than its diff:
```python
import functools

import jax
import jax.numpy as jnp
from jax import lax
from jax.experimental import pallas as pl
from jax.experimental.pallas import tpu as pltpu
from jax.sharding import PartitionSpec as P

QUERY_HEADS = 32
KEY_VALUE_HEADS = 4
HEAD_WIDTH = 128
SHARE = QUERY_HEADS // KEY_VALUE_HEADS
SCALE = HEAD_WIDTH**-0.5
LOG2_E = 1.4426950408889634
HIDDEN = -1e30
ID_BASE = 128
ID_ROWS = 16
PAD_ROWS = 32

NT = (((1,), (1,)), ((), ()))
NN = (((1,), (0,)), ((), ()))
TN = (((0,), (0,)), ((), ()))
f32 = jnp.float32
bf16 = jnp.bfloat16
VMEM = pl.BlockSpec(memory_space=pltpu.VMEM)
SMEM = pl.BlockSpec(memory_space=pltpu.SMEM)
HBM = pl.BlockSpec(memory_space=pltpu.HBM)
LIMIT = 8 << 20
SMALL = 2 << 20
S = jax.ShapeDtypeStruct


def call(kernel, name, ins, outs, shapes, scratch=(), cost=None, limit=LIMIT):
    return pl.pallas_call(
        kernel,
        name=name,
        in_specs=ins,
        out_specs=outs,
        out_shape=shapes,
        scratch_shapes=list(scratch),
        compiler_params=pltpu.CompilerParams(vmem_limit_bytes=limit),
        cost_estimate=pl.CostEstimate(flops=cost, bytes_accessed=1, transcendentals=0) if cost else None,
    )


def dot(a, b, dims):
    return lax.dot_general(a, b, dims, preferred_element_type=f32)


def heads(ref, first, count):
    w = HEAD_WIDTH
    return jnp.concatenate([ref[:, (first + j) * w : (first + j + 1) * w] for j in range(count)], axis=0)


def gather_blocks(refs, core, all_ref, t):
    own, near, near_other, far, sibling, far_other = refs
    for slot, ref in enumerate((own, near, near_other, far)):
        all_ref[slot * t : (slot + 1) * t, :] = ref[:t, :]
    all_ref[4 * t :, :] = jnp.where(core == 0, far_other[:t, :], sibling[:t, :])


def ids_of(ref, t):
    row = ref[t : t + ID_ROWS, :].astype(f32)[:1]
    return row[:, :t] * ID_BASE + row[:, t : 2 * t]


def store_parts(total, group, t, own_ref, near_ref, far_ref, other_ref, last_ref):
    c = slice(group * HEAD_WIDTH, (group + 1) * HEAD_WIDTH)
    own_ref[:, c] = total[:t]
    near_ref[:, c] = total[t : 2 * t].astype(bf16)
    far_ref[:, c] = total[3 * t : 4 * t].astype(bf16)
    other_ref[:, c] = total[2 * t : 3 * t].astype(bf16)
    last_ref[:, c] = total[4 * t :].astype(bf16)


def lineage_kernel(own_ref, parent_ref, line_ref):
    t = line_ref.shape[0]
    node = jnp.broadcast_to(ids_of(own_ref, t), (t, t)).T[:, :1]
    parents = parent_ref[...].astype(f32)
    index = lax.broadcasted_iota(jnp.int32, (t, parents.shape[1]), 1).astype(f32)
    up = jnp.sum(jnp.where(index == node, parents, 0.0), axis=1, keepdims=True)
    upper = jnp.sum(jnp.where(index == up, parents, 0.0), axis=1, keepdims=True)
    lane = lax.broadcasted_iota(jnp.int32, line_ref.shape, 1)
    line_ref[...] = jnp.where(lane == 0, node, jnp.where(lane == 1, up, upper))


def probs_kernel(core_ref, line_ref, q_ref, do_ref, k0, k1, k2, k3, k4, k5,
                 p_ref, keys_ref, own_ref, near_ref, far_ref, other_ref, last_ref, bias_ref):
    t = line_ref.shape[0]
    core = core_ref[0]
    gather_blocks((k0, k1, k2, k3, k4, k5), core, keys_ref, t)
    node, up, upper = (line_ref[:, j : j + 1] for j in range(3))
    tok = lax.broadcasted_iota(jnp.int32, (t, t), 0)
    key = lax.broadcasted_iota(jnp.int32, (t, t), 1)
    last_ids = jnp.where(core == 0, ids_of(k5, t), ids_of(k4, t))
    for slot, ids in enumerate((ids_of(k0, t), ids_of(k1, t), ids_of(k2, t), ids_of(k3, t), last_ids)):
        seen = (ids == node) | (ids == up) | (ids == upper)
        if slot == 0:
            seen = seen & (key <= tok)
        bias_ref[slot * t : (slot + 1) * t, :] = jnp.where(seen, 0.0, HIDDEN).T
    for g in range(KEY_VALUE_HEADS):
        keys = keys_ref[:, g * HEAD_WIDTH : (g + 1) * HEAD_WIDTH]
        for h in range(g * SHARE, (g + 1) * SHARE, 2):
            bias = bias_ref[...]
            s = dot(keys, heads(q_ref, h, 2), NT) * (SCALE * LOG2_E) + jnp.concatenate([bias, bias], axis=1)
            e = jnp.exp2(s - jnp.max(s, axis=0, keepdims=True))
            inv = 1.0 / jnp.sum(e, axis=0, keepdims=True)
            p_ref[:, h * t : (h + 2) * t] = (e * inv).astype(bf16)
        dv = dot(p_ref[:, g * SHARE * t : (g + 1) * SHARE * t], heads(do_ref, g * SHARE, SHARE), NN)
        store_parts(dv, g, t, own_ref, near_ref, far_ref, other_ref, last_ref)


def score_grad_kernel(core_ref, p_ref, q_ref, do_ref, v0, v1, v2, v3, v4, v5,
                      ds_ref, vals_ref, own_ref, near_ref, far_ref, other_ref, last_ref):
    t = own_ref.shape[0]
    core = core_ref[0]
    gather_blocks((v0, v1, v2, v3, v4, v5), core, vals_ref, t)
    for g in range(KEY_VALUE_HEADS):
        vals = vals_ref[:, g * HEAD_WIDTH : (g + 1) * HEAD_WIDTH]
        for h in range(g * SHARE, (g + 1) * SHARE, 2):
            c = slice(h * t, (h + 2) * t)
            dp = dot(vals, heads(do_ref, h, 2), NT)
            p = p_ref[:, c].astype(f32)
            delta = jnp.sum(p * dp, axis=0, keepdims=True)
            ds_ref[:, c] = (p * (dp - delta)).astype(bf16)
        dk = dot(ds_ref[:, g * SHARE * t : (g + 1) * SHARE * t], heads(q_ref, g * SHARE, SHARE), NN) * SCALE
        store_parts(dk, g, t, own_ref, near_ref, far_ref, other_ref, last_ref)


def rows_kernel(p_ref, ds_ref, keys_ref, vals_ref, o_ref, dq_ref):
    t = o_ref.shape[0]
    w = HEAD_WIDTH
    for h in range(0, QUERY_HEADS, 2):
        g = slice(h // SHARE * w, (h // SHARE + 1) * w)
        c = slice(h * t, (h + 2) * t)
        o = dot(vals_ref[:, g], p_ref[:, c], TN).astype(bf16)
        dq = (dot(keys_ref[:, g], ds_ref[:, c], TN) * SCALE).astype(bf16)
        for j in range(2):
            o_ref[:, (h + j) * w : (h + j + 1) * w] = o[:, j * t : (j + 1) * t].T
            dq_ref[:, (h + j) * w : (h + j + 1) * w] = dq[:, j * t : (j + 1) * t].T


def merge_kernel(core_ref, own_ref, near_ref, far_ref, got_ref, got_last_ref, own_out, near_out, far_out):
    t = own_ref.shape[0]
    first = core_ref[0] == 0
    last = got_last_ref[...].astype(f32)
    own_out[...] = own_ref[...] + jnp.where(first, last, 0.0)
    near_out[:t, :] = (near_ref[...].astype(f32) + got_ref[...].astype(f32)).astype(bf16)
    far_out[:t, :] = (far_ref[...].astype(f32) + jnp.where(first, 0.0, last)).astype(bf16)
    if near_out.shape[0] > t:
        near_out[t:, :] = jnp.zeros((near_out.shape[0] - t, near_out.shape[1]), bf16)
        far_out[t:, :] = jnp.zeros((near_out.shape[0] - t, near_out.shape[1]), bf16)


def total_kernel(own_ref, near_ref, far_ref, out_ref):
    t = own_ref.shape[0]
    out_ref[...] = (own_ref[...] + near_ref[:t, :].astype(f32) + far_ref[:t, :].astype(f32)).astype(bf16)


def ahead(value, by):
    n = lax.axis_size("seq")
    return lax.ppermute(value, "seq", [(i, (i + by) % n) for i in range(n)])


def swap(value):
    n = lax.axis_size("seq")
    return lax.ppermute(value, "seq", [(i, i ^ 1) for i in range(n)])


def with_ids(keys, node_of):
    t, width = keys.shape
    rows = t + ID_ROWS
    digits = [jnp.broadcast_to(d.astype(bf16), (rows, t)) for d in (node_of >> 7, node_of & (ID_BASE - 1))]
    ids = jnp.pad(digits[0], ((0, 0), (0, width - t))) + jnp.pad(digits[1], ((0, 0), (t, width - 2 * t)))
    row = lax.broadcasted_iota(jnp.int32, (rows, width), 0)
    return jnp.where(row < t, jnp.pad(keys, ((0, ID_ROWS), (0, 0))), ids)


def spread(value):
    far = ahead(value, 4)
    near = ahead(value, 2)
    return value, near, swap(near), far, swap(value), swap(far)


def merge(core, own, near, far, other, last, pad):
    t, width = own.shape
    sent = S((t + pad, width), bf16)
    return call(merge_kernel, "merge", [SMEM] + [VMEM] * 5, [VMEM] * 3, [S((t, width), f32), sent, sent], cost=1, limit=SMALL)(
        core, own, near, far, swap(other), swap(last)
    )


def home(own, near, far):
    near, far = ahead(near, -2), ahead(far, -4)
    return call(total_kernel, "total", [VMEM] * 3, VMEM, S(own.shape, bf16), cost=1, limit=SMALL)(own, near, far)


def on_device(queries, keys, values, output_gradient, node_of, parent):
    t, width = keys.shape
    core = (lax.axis_index("seq") % 2).astype(jnp.int32).reshape(1)
    ks = spread(with_ids(keys, node_of))
    values = jnp.pad(values, ((0, PAD_ROWS), (0, 0)))
    far, near = ahead(values, 4), ahead(values, 2)
    line = call(lineage_kernel, "lineage", [VMEM, VMEM], VMEM, S((t, t), f32), cost=1 << 32, limit=SMALL)(
        ks[0], parent[None]
    )
    parts = [S((t, width), f32)] + [S((t, width), bf16)] * 4
    square = S((5 * t, QUERY_HEADS * t), bf16)
    blocks = S((5 * t, width), bf16)
    p, keys_all, *dv = call(
        probs_kernel,
        "probs",
        [SMEM] + [VMEM] * 9,
        [VMEM] * 7,
        [square, blocks] + parts,
        [pltpu.VMEM((5 * t, t), f32)],
        cost=1,
    )(core, line, queries, output_gradient, *ks)
    dv_own, dv_near, dv_far = merge(core, *dv, PAD_ROWS)
    p, dv_near, dv_far, near, far = lax.optimization_barrier((p, dv_near, dv_far, near, far))
    vs = values, near, swap(near), far, swap(values), swap(far)
    dv = home(dv_own, dv_near, dv_far)
    ds, vals_all, *dk = call(
        score_grad_kernel,
        "score_grad",
        [SMEM] + [VMEM] * 9,
        [VMEM] * 7,
        [square, blocks] + parts,
        cost=1,
    )(core, p, queries, output_gradient, *vs)
    dk_own, dk_near, dk_far = merge(core, *dk, 0)
    ds, dk_near, dk_far, dv = lax.optimization_barrier((ds, dk_near, dk_far, dv))
    dk = home(dk_own, dk_near, dk_far)
    attended, q_grad = call(
        rows_kernel,
        "rows",
        [VMEM] * 4,
        [VMEM] * 2,
        [S(queries.shape, bf16), S(queries.shape, bf16)],
        cost=1 << 32,
    )(p, ds, keys_all, vals_all)
    return attended, q_grad, dk, dv


def solution(mesh):
    rows = P(("grp", "seq"), None)
    return jax.shard_map(
        on_device,
        mesh=mesh,
        in_specs=(rows, rows, rows, rows, P(("grp", "seq")), P("grp")),
        out_specs=(rows, rows, rows, rows),
        check_vma=False,
    )
```

time: 65.1 us -> 46.1 us (0.71)
  local copies, waits for them, and re-layouts: 16.1 us -> 2.7 us
  waiting for transfers between devices: 14.6 us -> 4.49 us
  starting transfers between devices: 14.6 us -> 19.6 us
  other arithmetic: 4.28 us -> 1.67 us
  Pallas kernels: 14.4 us -> 16.7 us
    unnamed x22 -> x6, local copies, waits for them, and re-layouts: 16.1 us -> 1.79 us
    ppermute x8, waiting for transfers between devices: 13.5 us -> 3.48 us  [ahead(): return lax.ppermute(value, 'seq', [(i, (i + by) % n) for i in range(n)])]
    ppermute x8, starting transfers between devices: 12.7 us -> 17.3 us  [ahead(): return lax.ppermute(value, 'seq', [(i, (i + by) % n) for i in range(n)])]
    pallas_call x3 -> x8, Pallas kernels: 14.4 us -> 16.7 us  [the longest x1 5.35 us: on_device(): call(score_grad_kernel, 'score_grad', [SMEM] + [VMEM] * 9, [VMEM] * 7, [s...]
    convert_element_type x6 -> x1, other arithmetic: 2.68 us -> 0.66 us  [with_ids(): d.astype(bf16)]
    concatenate x3 -> x0, other arithmetic: 1.59 us -> none  [the longest x1 0.91 us: on_device(): ks = spread(jnp.concatenate([keys, ids], axis=0))]
    select_n x0 -> x1, other arithmetic: none -> 0.99 us  [with_ids(): return jnp.where(row < t, jnp.pad(keys, ((0, ID_ROWS), (0, 0))), ids)]
    pad x0 -> x1, local copies, waits for them, and re-layouts: none -> 0.92 us  [on_device(): values = jnp.pad(values, ((0, PAD_ROWS), (0, 0)))]
  transfers between devices with their start and end apart: 16 -> 18, of which waited for: 7 -> 4; matrix products, arithmetic and copies ran while one was open for 3% -> 2% of each run, Pallas kernels for 22% -> 35%
where the time goes in v2:
time: 46.1 us; the launch traced here: 45.9 us
  starting transfers between devices  19.6 us (43%)
  Pallas kernels  16.7 us (36%)
  waiting for transfers between devices  4.49 us (10%)
  local copies, waits for them, and re-layouts  2.7 us (6%)
  other arithmetic  1.67 us (4%)
  between operations  0.76 us (2%)
    ppermute x8, starting transfers between devices, ahead(): return lax.ppermute(value, 'seq', [(i, (i + by) % n) for i in range(n)])  17.3 us
    pallas_call x1, Pallas kernels, on_device(): call(score_grad_kernel, 'score_grad', [SMEM] + [VMEM] * 9, [VMEM] * 7, [s...  5.35 us
    pallas_call x1, Pallas kernels, on_device(): call(probs_kernel, 'probs', [SMEM] + [VMEM] * 9, [VMEM] * 7, [square, blo...  5.21 us
    pallas_call x1, Pallas kernels, on_device(): call(rows_kernel, 'rows', [VMEM] * 4, [VMEM] * 2, [S(queries.shape, bf16)...  4.21 us
    ppermute x8, waiting for transfers between devices, ahead(): return lax.ppermute(value, 'seq', [(i, (i + by) % n) for i in range(n)])  3.48 us
    ppermute x10, starting transfers between devices, swap(): return lax.ppermute(value, 'seq', [(i, i ^ 1) for i in range(n)])  2.3 us
    unnamed x6, local copies, waits for them, and re-layouts  1.79 us
    pallas_call x2, Pallas kernels, home(): call(total_kernel, 'total', [VMEM] * 3, VMEM, S(own.shape, bf16), cost=1,...  1.4 us
  transfers between devices with their start and end apart: 18, of which 4 were waited for; matrix products, arithmetic and copies ran while one was open for 2% of the time, Pallas kernels for 35%

profile of v2, /device:TPU:0, one launch (start us, length us, event | category | flops | bytes accessed | tf_op | source)
XLA Modules:
  0.0 45.9 jit_solution(3624007218369718433)
XLA Ops:
  0.6 0.7 %shift-right-arithmetic_convert_fusion = (bf16[128]{0:T(256)(128)(2,1)S(1)}, bf16[128]{0:T(256)(128)(2,1)S(1)}) fusion(s32[128]{0:T(128)} %param.10), kind=kLoop, calls=%fused_computation.4 | loop fusion | flops 512 | bytes 1024 | tf_op jit(solution)/shard_map/convert_element_type | solution.py:174
  1.3 1.0 %pad_select_fusion.own_ref.k0 = bf16[144,512]{1,0:T(8,128)(2,1)S(1)} fusion(bf16[128,512]{1,0:T(8,128)(2,1)} %param.7, pred[144]{0:T(512)(128)(4,1)S(1)} %iota_compare_fusion, bf16[512]{0:T(512)(128)(2,1)S(1)} %pad_add_fusion), kind=kLoop, calls=%fused_computation | loop fusion | flops 73728 | bytes 279696 | tf_op jit(solution)/shard_map/jit(_where)/select_n | solution.py:177
  2.3 3.0 %collective-permute-start = (bf16[144,512]{1,0:T(8,128)(2,1)S(1)}, bf16[144,512]{1,0:T(8,128)(2,1)S(1)}, u32[]{:S(2)}, u32[]{:S(2)}) collective-permute-start(bf16[144,512]{1,0:T(8,128)(2,1)S(1)} %pad_select_fusion.own_ref.k0), channel_id=1, source_target_pairs={{0,2},{1,3},{2,4},{3,5},{4,6},{5,7},{6,8},{7,9},{8,10},{9,11},{10,... | collective-permute-start | bytes 442376 | tf_op jit(solution)/shard_map/ppermute | solution.py:163
  5.3 1.6 %collective-permute-start.2 = (bf16[144,512]{1,0:T(8,128)(2,1)S(1)}, bf16[144,512]{1,0:T(8,128)(2,1)S(1)}, u32[]{:S(2)}, u32[]{:S(2)}) collective-permute-start(bf16[144,512]{1,0:T(8,128)(2,1)S(1)} %pad_select_fusion.own_ref.k0), channel_id=1, source_target_pairs={{0,4},{1,5},{2,6},{3,7},{4,8},{5,9},{6,10},{7,11},{8,12},{9,13},{1... | collective-permute-start | bytes 442376 | tf_op jit(solution)/shard_map/ppermute | solution.py:163
  6.9 0.0 collective-permute-start.3
  6.9 0.9 %pad.22.v0 = bf16[160,512]{1,0:T(8,128)(2,1)S(1)} pad(bf16[128,512]{1,0:T(8,128)(2,1)} %param.8, bf16[]{:T(256)} %constant.23.clone.1), padding=0_32x0_0 | pad | bytes 294914 | tf_op jit(solution)/shard_map/jit(_pad)/pad | solution.py:203
  7.8 1.6 %collective-permute-start.7 = (bf16[160,512]{1,0:T(8,128)(2,1)S(1)}, bf16[160,512]{1,0:T(8,128)(2,1)S(1)}, u32[]{:S(2)}, u32[]{:S(2)}) collective-permute-start(bf16[160,512]{1,0:T(8,128)(2,1)S(1)} %pad.22.v0), channel_id=1, source_target_pairs={{0,2},{1,3},{2,4},{3,5},{4,6},{5,7},{6,8},{7,9},{8,10},{9,11},{10,... | collective-permute-start | bytes 491528 | tf_op jit(solution)/shard_map/ppermute | solution.py:163
  9.4 1.6 %collective-permute-start.8 = (bf16[160,512]{1,0:T(8,128)(2,1)S(1)}, bf16[160,512]{1,0:T(8,128)(2,1)S(1)}, u32[]{:S(2)}, u32[]{:S(2)}) collective-permute-start(bf16[160,512]{1,0:T(8,128)(2,1)S(1)} %pad.22.v0), channel_id=1, source_target_pairs={{0,4},{1,5},{2,6},{3,7},{4,8},{5,9},{6,10},{7,11},{8,12},{9,13},{1... | collective-permute-start | bytes 491528 | tf_op jit(solution)/shard_map/ppermute | solution.py:163
  11.0 2.1 %collective-permute-done.k1 = bf16[144,512]{1,0:T(8,128)(2,1)S(1)} collective-permute-done((bf16[144,512]{1,0:T(8,128)(2,1)S(1)}, bf16[144,512]{1,0:T(8,128)(2,1)S(1)}, u32[]{:S(2)}, u32[]{:S(2)}) %collective-permute-start) | collective-permute-done | bytes 147488 | tf_op jit(solution)/shard_map/ppermute | solution.py:163
  13.0 0.0 collective-permute-start.1
  13.1 0.0 collective-permute-done.2.k3
  13.1 0.5 %collective-permute-start.4 = (bf16[144,512]{1,0:T(8,128)(2,1)S(1)}, bf16[144,512]{1,0:T(8,128)(2,1)S(1)}, u32[]{:S(2)}, u32[]{:S(2)}) collective-permute-start(bf16[144,512]{1,0:T(8,128)(2,1)S(1)} %collective-permute-done.2.k3), channel_id=1, source_target_pairs={{0,1},{1,0},{2,3},{3,2},{4,5},{5,4},{6,7},{7,6},{8,9},{9,8},{10,11... | collective-permute-start | bytes 442376 | tf_op jit(solution)/shard_map/ppermute | solution.py:168
  13.6 0.7 %copy-done.2 = s32[84]{0:T(128)S(1)} copy-done((s32[84]{0:T(128)S(1)}, s32[84]{0:T(128)}, u32[]{:S(2)}) %copy-start.2) | copy-done | bytes 360
  14.2 0.3 lineage.1.line_ref
  14.6 0.0 collective-permute-done.3.k4
  14.6 0.0 collective-permute-done.1.k2
  14.6 0.0 collective-permute-done.4.k5
  14.6 0.8 %copy-done = bf16[128,4096]{1,0:T(8,128)(2,1)S(1)} copy-done((bf16[128,4096]{1,0:T(8,128)(2,1)S(1)}, bf16[128,4096]{1,0:T(8,128)(2,1)}, u32[]{:S(2)}) %copy-start) | copy-done | bytes 1048600
  15.4 0.3 copy-done.1
  15.8 5.2 %probs.1 = (bf16[640,4096]{1,0:T(8,128)(2,1)S(1)}, bf16[640,512]{1,0:T(8,128)(2,1)S(1)}, f32[128,512]{1,0:T(8,128)S(1)}, bf16[128,512]{1,0:T(8,128)(2,1)S(1)}, b...) custom-call(s32[1]{0:T(128)} %bitcast.core_ref, ...), custom_call_target="tpu_custom_call" | custom-call | flops 1 | bytes 1 | tf_op jit(solution)/shard_map/probs/pallas_call | solution.py:211
  21.0 0.1 collective-permute-start.5
  21.1 0.5 %collective-permute-start.6 = (bf16[128,512]{1,0:T(8,128)(2,1)S(1)}, bf16[128,512]{1,0:T(8,128)(2,1)S(1)}, u32[]{:S(2)}, u32[]{:S(2)}) collective-permute-start(bf16[128,512]{1,0:T(8,128)(2,1)S(1)} %get-tuple-element.40), channel_id=1, source_target_pairs={{0,1},{1,0},{2,3},{3,2},{4,5},{5,4},{6,7},{7,6},{8,9},{9,8},{10,11... | collective-permute-start | bytes 393224 | tf_op jit(solution)/shard_map/ppermute | solution.py:168
  21.6 0.1 collective-permute-start.10
  21.6 0.8 %collective-permute-done.5.got_ref = bf16[128,512]{1,0:T(8,128)(2,1)S(1)} collective-permute-done((bf16[128,512]{1,0:T(8,128)(2,1)S(1)}, bf16[128,512]{1,0:T(8,128)(2,1)S(1)}, u32[]{:S(2)}, u32[]{:S(2)}) %collective-permute-start.5) | collective-permute-done | bytes 131104 | tf_op jit(solution)/shard_map/ppermute | solution.py:168
  22.4 0.2 collective-permute-done.6.got_last_ref
  22.6 0.1 merge.2
  22.7 0.0 collective-permute-done.7.v1
  22.7 0.0 collective-permute-done.8.v3
  22.7 0.4 collective-permute-start.11
  23.1 0.2 collective-permute-start.9
  23.3 5.0 %collective-permute-start.14 = (bf16[160,512]{1,0:T(8,128)(2,1)S(1)}, bf16[160,512]{1,0:T(8,128)(2,1)S(1)}, u32[]{:S(2)}, u32[]{:S(2)}) collective-permute-start(bf16[160,512]{1,0:T(8,128)(2,1)S(1)} %get-tuple-element.55), channel_id=1, source_target_pairs={{0,14},{1,15},{2,0},{3,1},{4,2},{5,3},{6,4},{7,5},{8,6},{9,7},{10,... | collective-permute-start | bytes 491528 | tf_op jit(solution)/shard_map/ppermute | solution.py:163
  28.3 0.4 collective-permute-start.15
  28.7 0.0 collective-permute-done.10.v4
  28.7 0.0 collective-permute-done.11.v5
  28.7 5.4 %score_grad.1 = (bf16[640,4096]{1,0:T(8,128)(2,1)S(1)}, bf16[640,512]{1,0:T(8,128)(2,1)S(1)}, f32[128,512]{1,0:T(8,128)S(1)}, bf16[128,512]{1,0:T(8,128)(2,1)S(1...) custom-call(s32[1]{0:T(128)} %bitcast.core_ref, ...), custom_call_target="tpu_custom_call" | custom-call | flops 1 | bytes 1 | tf_op jit(solution)/shard_map/score_grad/pallas_call | solution.py:224
  34.1 0.1 collective-permute-start.12
  34.1 0.5 %collective-permute-start.13 = (bf16[128,512]{1,0:T(8,128)(2,1)S(1)}, bf16[128,512]{1,0:T(8,128)(2,1)S(1)}, u32[]{:S(2)}, u32[]{:S(2)}) collective-permute-start(bf16[128,512]{1,0:T(8,128)(2,1)S(1)} %get-tuple-element.51), channel_id=1, source_target_pairs={{0,1},{1,0},{2,3},{3,2},{4,5},{5,4},{6,7},{7,6},{8,9},{9,8},{10,11... | collective-permute-start | bytes 393224 | tf_op jit(solution)/shard_map/ppermute | solution.py:168
  34.6 0.0 collective-permute-done.14.near_ref
  34.6 1.4 %collective-permute-done.15.far_ref = bf16[160,512]{1,0:T(8,128)(2,1)S(1)} collective-permute-done((bf16[160,512]{1,0:T(8,128)(2,1)S(1)}, bf16[160,512]{1,0:T(8,128)(2,1)S(1)}, u32[]{:S(2)}, u32[]{:S(2)}) %collective-permute-start.15) | collective-permute-done | bytes 163872 | tf_op jit(solution)/shard_map/ppermute | solution.py:163
  36.0 0.7 %total.2 = bf16[128,512]{1,0:T(8,128)(2,1)} custom-call(f32[128,512]{1,0:T(8,128)S(1)} %get-tuple-element.54.own_ref, bf16[160,512]{1,0:T(8,128)(2,1)S(1)} %collective-permute-done.14.near_ref, bf16[160,512]{1,0:T(8,128)(2,1)S(1)} %collective-permute-done.15.far_ref), custom_call_target="tpu_custom_call" | custom-call | flops 1 | bytes 1 | tf_op jit(solution)/shard_map/total/pallas_call | solution.py:196
  36.7 0.0 collective-permute-done.13.got_last_ref
  36.8 0.1 merge.3
  36.9 2.0 %collective-permute-start.16 = (bf16[128,512]{1,0:T(8,128)(2,1)S(1)}, bf16[128,512]{1,0:T(8,128)(2,1)S(1)}, u32[]{:S(2)}, u32[]{:S(2)}) collective-permute-start(bf16[128,512]{1,0:T(8,128)(2,1)S(1)} %get-tuple-element.63), channel_id=1, source_target_pairs={{0,14},{1,15},{2,0},{3,1},{4,2},{5,3},{6,4},{7,5},{8,6},{9,7},{10,... | collective-permute-start | bytes 393224 | tf_op jit(solution)/shard_map/ppermute | solution.py:163
  38.8 2.1 %collective-permute-start.17 = (bf16[128,512]{1,0:T(8,128)(2,1)S(1)}, bf16[128,512]{1,0:T(8,128)(2,1)S(1)}, u32[]{:S(2)}, u32[]{:S(2)}) collective-permute-start(bf16[128,512]{1,0:T(8,128)(2,1)S(1)} %get-tuple-element.64), channel_id=1, source_target_pairs={{0,12},{1,13},{2,14},{3,15},{4,0},{5,1},{6,2},{7,3},{8,4},{9,5},{1... | collective-permute-start | bytes 393224 | tf_op jit(solution)/shard_map/ppermute | solution.py:163
  41.0 4.2 %rows.1 = (bf16[128,4096]{1,0:T(8,128)(2,1)}, bf16[128,4096]{1,0:T(8,128)(2,1)}) custom-call(bf16[640,4096]{1,0:T(8,128)(2,1)S(1)} %get-tuple-element.43.p_ref, bf16[640,4096]{1,0:T(8,128)(2,1)S(1)} %get-tuple-element.57.ds_ref, bf16[640,512]{1,0:T(8,128)(2,1)S(1)} %get-tuple-element.58.keys_ref, bf16[640,512]{1,0:T(8,128)(2,1)S(1)} %get-tuple-element.59.vals_ref), custom_call_target="tpu_custom_call" | custom-call | flops 4294967296 | bytes 1 | tf_op jit(solution)/shard_map/rows/pallas_call | solution.py:235
  45.2 0.0 collective-permute-done.16.near_ref
  45.2 0.0 collective-permute-done.17.far_ref
  45.2 0.7 %total.3 = bf16[128,512]{1,0:T(8,128)(2,1)} custom-call(f32[128,512]{1,0:T(8,128)S(1)} %get-tuple-element.62.own_ref, bf16[128,512]{1,0:T(8,128)(2,1)S(1)} %collective-permute-done.16.near_ref, bf16[128,512]{1,0:T(8,128)(2,1)S(1)} %collective-permute-done.17.far_ref), custom_call_target="tpu_custom_call" | custom-call | flops 1 | bytes 1 | tf_op jit(solution)/shard_map/total/pallas_call | solution.py:196
  (7 shorter events, 0.0 us)
Async XLA Ops:
  2.3 10.7 %collective-permute-start = (bf16[144,512]{1,0:T(8,128)(2,1)S(1)}, bf16[144,512]{1,0:T(8,128)(2,1)S(1)}, u32[]{:S(2)}, u32[]{:S(2)}) collective-permute-start(bf16[144,512]{1,0:T(8,128)(2,1)S(1)} %pad_select_fusion.own_ref.k0), channel_id=1, source_target_pairs={{0,2},{1,3},{2,4},{3,5},{4,6},{5,7},{6,8},{7,9},{8,10},{9,11},{10,... | collective-permute-start | bytes 442376 | tf_op jit(solution)/shard_map/ppermute | solution.py:163
  5.3 7.7 %collective-permute-start.2 = (bf16[144,512]{1,0:T(8,128)(2,1)S(1)}, bf16[144,512]{1,0:T(8,128)(2,1)S(1)}, u32[]{:S(2)}, u32[]{:S(2)}) collective-permute-start(bf16[144,512]{1,0:T(8,128)(2,1)S(1)} %pad_select_fusion.own_ref.k0), channel_id=1, source_target_pairs={{0,4},{1,5},{2,6},{3,7},{4,8},{5,9},{6,10},{7,11},{8,12},{9,13},{1... | collective-permute-start | bytes 442376 | tf_op jit(solution)/shard_map/ppermute | solution.py:163
  6.9 7.7 %collective-permute-start.3 = (bf16[144,512]{1,0:T(8,128)(2,1)S(1)}, bf16[144,512]{1,0:T(8,128)(2,1)S(1)}, u32[]{:S(2)}, u32[]{:S(2)}) collective-permute-start(bf16[144,512]{1,0:T(8,128)(2,1)S(1)} %pad_select_fusion.own_ref.k0), channel_id=1, source_target_pairs={{0,1},{1,0},{2,3},{3,2},{4,5},{5,4},{6,7},{7,6},{8,9},{9,8},{10,11... | collective-permute-start | bytes 442376 | tf_op jit(solution)/shard_map/ppermute | solution.py:168
  7.8 14.9 %collective-permute-start.7 = (bf16[160,512]{1,0:T(8,128)(2,1)S(1)}, bf16[160,512]{1,0:T(8,128)(2,1)S(1)}, u32[]{:S(2)}, u32[]{:S(2)}) collective-permute-start(bf16[160,512]{1,0:T(8,128)(2,1)S(1)} %pad.22.v0), channel_id=1, source_target_pairs={{0,2},{1,3},{2,4},{3,5},{4,6},{5,7},{6,8},{7,9},{8,10},{9,11},{10,... | collective-permute-start | bytes 491528 | tf_op jit(solution)/shard_map/ppermute | solution.py:163
  9.4 13.3 %collective-permute-start.8 = (bf16[160,512]{1,0:T(8,128)(2,1)S(1)}, bf16[160,512]{1,0:T(8,128)(2,1)S(1)}, u32[]{:S(2)}, u32[]{:S(2)}) collective-permute-start(bf16[160,512]{1,0:T(8,128)(2,1)S(1)} %pad.22.v0), channel_id=1, source_target_pairs={{0,4},{1,5},{2,6},{3,7},{4,8},{5,9},{6,10},{7,11},{8,12},{9,13},{1... | collective-permute-start | bytes 491528 | tf_op jit(solution)/shard_map/ppermute | solution.py:163
  13.0 1.5 %collective-permute-start.1 = (bf16[144,512]{1,0:T(8,128)(2,1)S(1)}, bf16[144,512]{1,0:T(8,128)(2,1)S(1)}, u32[]{:S(2)}, u32[]{:S(2)}) collective-permute-start(bf16[144,512]{1,0:T(8,128)(2,1)S(1)} %collective-permute-done.k1), channel_id=1, source_target_pairs={{0,1},{1,0},{2,3},{3,2},{4,5},{5,4},{6,7},{7,6},{8,9},{9,8},{10,11... | collective-permute-start | bytes 442376 | tf_op jit(solution)/shard_map/ppermute | solution.py:168
  13.1 1.6 %collective-permute-start.4 = (bf16[144,512]{1,0:T(8,128)(2,1)S(1)}, bf16[144,512]{1,0:T(8,128)(2,1)S(1)}, u32[]{:S(2)}, u32[]{:S(2)}) collective-permute-start(bf16[144,512]{1,0:T(8,128)(2,1)S(1)} %collective-permute-done.2.k3), channel_id=1, source_target_pairs={{0,1},{1,0},{2,3},{3,2},{4,5},{5,4},{6,7},{7,6},{8,9},{9,8},{10,11... | collective-permute-start | bytes 442376 | tf_op jit(solution)/shard_map/ppermute | solution.py:168
  13.6 0.7 %copy-start.2 = (s32[84]{0:T(128)S(1)}, s32[84]{0:T(128)}, u32[]{:S(2)}) copy-start(s32[84]{0:T(128)} %param.11) | copy-start | bytes 1012
  14.2 1.2 %copy-start = (bf16[128,4096]{1,0:T(8,128)(2,1)S(1)}, bf16[128,4096]{1,0:T(8,128)(2,1)}, u32[]{:S(2)}) copy-start(bf16[128,4096]{1,0:T(8,128)(2,1)} %q_ref.3) | copy-start | bytes 3145732
  14.2 1.5 %copy-start.1 = (bf16[128,4096]{1,0:T(8,128)(2,1)S(1)}, bf16[128,4096]{1,0:T(8,128)(2,1)}, u32[]{:S(2)}) copy-start(bf16[128,4096]{1,0:T(8,128)(2,1)} %do_ref.3) | copy-start | bytes 3145732
  21.0 1.4 %collective-permute-start.5 = (bf16[128,512]{1,0:T(8,128)(2,1)S(1)}, bf16[128,512]{1,0:T(8,128)(2,1)S(1)}, u32[]{:S(2)}, u32[]{:S(2)}) collective-permute-start(bf16[128,512]{1,0:T(8,128)(2,1)S(1)} %get-tuple-element.39), channel_id=1, source_target_pairs={{0,1},{1,0},{2,3},{3,2},{4,5},{5,4},{6,7},{7,6},{8,9},{9,8},{10,11... | collective-permute-start | bytes 393224 | tf_op jit(solution)/shard_map/ppermute | solution.py:168
  21.1 1.5 %collective-permute-start.6 = (bf16[128,512]{1,0:T(8,128)(2,1)S(1)}, bf16[128,512]{1,0:T(8,128)(2,1)S(1)}, u32[]{:S(2)}, u32[]{:S(2)}) collective-permute-start(bf16[128,512]{1,0:T(8,128)(2,1)S(1)} %get-tuple-element.40), channel_id=1, source_target_pairs={{0,1},{1,0},{2,3},{3,2},{4,5},{5,4},{6,7},{7,6},{8,9},{9,8},{10,11... | collective-permute-start | bytes 393224 | tf_op jit(solution)/shard_map/ppermute | solution.py:168
  21.6 7.1 %collective-permute-start.10 = (bf16[160,512]{1,0:T(8,128)(2,1)S(1)}, bf16[160,512]{1,0:T(8,128)(2,1)S(1)}, u32[]{:S(2)}, u32[]{:S(2)}) collective-permute-start(bf16[160,512]{1,0:T(8,128)(2,1)S(1)} %pad.22.v0), channel_id=1, source_target_pairs={{0,1},{1,0},{2,3},{3,2},{4,5},{5,4},{6,7},{7,6},{8,9},{9,8},{10,11... | collective-permute-start | bytes 491528 | tf_op jit(solution)/shard_map/ppermute | solution.py:168
  22.7 6.0 %collective-permute-start.11 = (bf16[160,512]{1,0:T(8,128)(2,1)S(1)}, bf16[160,512]{1,0:T(8,128)(2,1)S(1)}, u32[]{:S(2)}, u32[]{:S(2)}) collective-permute-start(bf16[160,512]{1,0:T(8,128)(2,1)S(1)} %collective-permute-done.8.v3), channel_id=1, source_target_pairs={{0,1},{1,0},{2,3},{3,2},{4,5},{5,4},{6,7},{7,6},{8,9},{9,8},{10,11... | collective-permute-start | bytes 491528 | tf_op jit(solution)/shard_map/ppermute | solution.py:168
  23.1 5.6 %collective-permute-start.9 = (bf16[160,512]{1,0:T(8,128)(2,1)S(1)}, bf16[160,512]{1,0:T(8,128)(2,1)S(1)}, u32[]{:S(2)}, u32[]{:S(2)}) collective-permute-start(bf16[160,512]{1,0:T(8,128)(2,1)S(1)} %collective-permute-done.7.v1), channel_id=1, source_target_pairs={{0,1},{1,0},{2,3},{3,2},{4,5},{5,4},{6,7},{7,6},{8,9},{9,8},{10,11... | collective-permute-start | bytes 491528 | tf_op jit(solution)/shard_map/ppermute | solution.py:168
  23.3 11.4 %collective-permute-start.14 = (bf16[160,512]{1,0:T(8,128)(2,1)S(1)}, bf16[160,512]{1,0:T(8,128)(2,1)S(1)}, u32[]{:S(2)}, u32[]{:S(2)}) collective-permute-start(bf16[160,512]{1,0:T(8,128)(2,1)S(1)} %get-tuple-element.55), channel_id=1, source_target_pairs={{0,14},{1,15},{2,0},{3,1},{4,2},{5,3},{6,4},{7,5},{8,6},{9,7},{10,... | collective-permute-start | bytes 491528 | tf_op jit(solution)/shard_map/ppermute | solution.py:163
  28.3 7.8 %collective-permute-start.15 = (bf16[160,512]{1,0:T(8,128)(2,1)S(1)}, bf16[160,512]{1,0:T(8,128)(2,1)S(1)}, u32[]{:S(2)}, u32[]{:S(2)}) collective-permute-start(bf16[160,512]{1,0:T(8,128)(2,1)S(1)} %get-tuple-element.56), channel_id=1, source_target_pairs={{0,12},{1,13},{2,14},{3,15},{4,0},{5,1},{6,2},{7,3},{8,4},{9,5},{1... | collective-permute-start | bytes 491528 | tf_op jit(solution)/shard_map/ppermute | solution.py:163
  34.1 2.7 %collective-permute-start.12 = (bf16[128,512]{1,0:T(8,128)(2,1)S(1)}, bf16[128,512]{1,0:T(8,128)(2,1)S(1)}, u32[]{:S(2)}, u32[]{:S(2)}) collective-permute-start(bf16[128,512]{1,0:T(8,128)(2,1)S(1)} %get-tuple-element.50), channel_id=1, source_target_pairs={{0,1},{1,0},{2,3},{3,2},{4,5},{5,4},{6,7},{7,6},{8,9},{9,8},{10,11... | collective-permute-start | bytes 393224 | tf_op jit(solution)/shard_map/ppermute | solution.py:168
  34.1 2.6 %collective-permute-start.13 = (bf16[128,512]{1,0:T(8,128)(2,1)S(1)}, bf16[128,512]{1,0:T(8,128)(2,1)S(1)}, u32[]{:S(2)}, u32[]{:S(2)}) collective-permute-start(bf16[128,512]{1,0:T(8,128)(2,1)S(1)} %get-tuple-element.51), channel_id=1, source_target_pairs={{0,1},{1,0},{2,3},{3,2},{4,5},{5,4},{6,7},{7,6},{8,9},{9,8},{10,11... | collective-permute-start | bytes 393224 | tf_op jit(solution)/shard_map/ppermute | solution.py:168
  36.9 8.3 %collective-permute-start.16 = (bf16[128,512]{1,0:T(8,128)(2,1)S(1)}, bf16[128,512]{1,0:T(8,128)(2,1)S(1)}, u32[]{:S(2)}, u32[]{:S(2)}) collective-permute-start(bf16[128,512]{1,0:T(8,128)(2,1)S(1)} %get-tuple-element.63), channel_id=1, source_target_pairs={{0,14},{1,15},{2,0},{3,1},{4,2},{5,3},{6,4},{7,5},{8,6},{9,7},{10,... | collective-permute-start | bytes 393224 | tf_op jit(solution)/shard_map/ppermute | solution.py:163
  38.8 6.3 %collective-permute-start.17 = (bf16[128,512]{1,0:T(8,128)(2,1)S(1)}, bf16[128,512]{1,0:T(8,128)(2,1)S(1)}, u32[]{:S(2)}, u32[]{:S(2)}) collective-permute-start(bf16[128,512]{1,0:T(8,128)(2,1)S(1)} %get-tuple-element.64), channel_id=1, source_target_pairs={{0,12},{1,13},{2,14},{3,15},{4,0},{5,1},{6,2},{7,3},{8,4},{9,5},{1... | collective-permute-start | bytes 393224 | tf_op jit(solution)/shard_map/ppermute | solution.py:163

commit v3 on v2

v3 whole, which is shorter than its diff:
```python
import functools

import jax
import jax.numpy as jnp
from jax import lax
from jax.experimental import pallas as pl
from jax.experimental.pallas import tpu as pltpu
from jax.sharding import PartitionSpec as P

QUERY_HEADS = 32
KEY_VALUE_HEADS = 4
HEAD_WIDTH = 128
SHARE = QUERY_HEADS // KEY_VALUE_HEADS
SCALE = HEAD_WIDTH**-0.5
LOG2_E = 1.4426950408889634
HIDDEN = -1e30
PAD_ROWS = 16
HALF = KEY_VALUE_HEADS // 2

NT = (((1,), (1,)), ((), ()))
NN = (((1,), (0,)), ((), ()))
TN = (((0,), (0,)), ((), ()))
f32 = jnp.float32
bf16 = jnp.bfloat16
VMEM = pl.BlockSpec(memory_space=pltpu.VMEM)
SMEM = pl.BlockSpec(memory_space=pltpu.SMEM)
HBM = pl.BlockSpec(memory_space=pltpu.HBM)
LIMIT = 8 << 20
SMALL = 2 << 20
S = jax.ShapeDtypeStruct


def call(kernel, name, ins, outs, shapes, scratch=(), cost=None, limit=LIMIT):
    return pl.pallas_call(
        kernel,
        name=name,
        in_specs=ins,
        out_specs=outs,
        out_shape=shapes,
        scratch_shapes=list(scratch),
        compiler_params=pltpu.CompilerParams(vmem_limit_bytes=limit),
        cost_estimate=pl.CostEstimate(flops=cost, bytes_accessed=1, transcendentals=0) if cost else None,
    )


def dot(a, b, dims):
    return lax.dot_general(a, b, dims, preferred_element_type=f32)


def heads(ref, first, count):
    w = HEAD_WIDTH
    return jnp.concatenate([ref[:, (first + j) * w : (first + j + 1) * w] for j in range(count)], axis=0)


def gather_blocks(own, near, near_other, far, sibling, far_other, core, all_ref):
    t = all_ref.shape[0] // 5
    for slot, ref in enumerate((own, near, near_other, far)):
        all_ref[slot * t : (slot + 1) * t, :] = ref[:t, :]
    all_ref[4 * t :, :] = jnp.where(core == 0, far_other[:t, :], sibling[:t, :])


def store_parts(total, group, t, refs):
    c = slice(group * HEAD_WIDTH, (group + 1) * HEAD_WIDTH)
    for slot, ref in zip((0, 1, 3, 2, 4), refs):
        ref[:, c] = total[slot * t : (slot + 1) * t].astype(ref.dtype)


def carry_parts(refs, earlier):
    for ref, old in zip(refs, earlier):
        ref[:, : old.shape[1]] = old[...]


def nodes_kernel(node_ref, near_ref, far_ref, out_ref):
    row = lax.broadcasted_iota(jnp.int32, out_ref.shape, 0)
    own, near, far = (jnp.broadcast_to(r[...], out_ref.shape) for r in (node_ref, near_ref, far_ref))
    out_ref[...] = jnp.where(row == 0, own, jnp.where(row == 1, near, far))


def lineage_kernel(node_ref, parent_ref, line_ref):
    t = node_ref.shape[1]
    node = jnp.broadcast_to(node_ref[...].astype(f32), (t, t)).T[:, :1]
    parents = parent_ref[...].astype(f32)
    index = lax.broadcasted_iota(jnp.int32, (t, parents.shape[1]), 1).astype(f32)
    up = jnp.sum(jnp.where(index == node, parents, 0.0), axis=1, keepdims=True)
    upper = jnp.sum(jnp.where(index == up, parents, 0.0), axis=1, keepdims=True)
    lane = lax.broadcasted_iota(jnp.int32, line_ref.shape, 1)
    line_ref[...] = jnp.where(lane == 0, node, jnp.where(lane == 1, up, upper))


def probs_of(groups, keys_ref, bias_ref, q_ref, do_ref, e_ref, scaled_ref, inv_ref, parts):
    t = q_ref.shape[0]
    w = HEAD_WIDTH
    for g in groups:
        keys = keys_ref[:, g * w : (g + 1) * w]
        first = (g - groups[0]) * SHARE
        for h in range(first, first + SHARE, 2):
            bias = bias_ref[...]
            s = dot(keys, heads(q_ref, groups[0] * SHARE + h, 2), NT) * (SCALE * LOG2_E)
            s = s + jnp.concatenate([bias, bias], axis=1)
            e = jnp.exp2(s - jnp.max(s, axis=0, keepdims=True))
            inv = 1.0 / jnp.sum(e, axis=0, keepdims=True)
            e_ref[:, h * t : (h + 2) * t] = e.astype(bf16)
            inv_ref[h : h + 1, :] = inv[:, :t]
            inv_ref[h + 1 : h + 2, :] = inv[:, t:]
        for j in range(first, first + SHARE):
            c = slice((groups[0] * SHARE + j) * w, (groups[0] * SHARE + j + 1) * w)
            column = jnp.broadcast_to(inv_ref[j : j + 1, :], (w, t)).T
            scaled_ref[:, j * w : (j + 1) * w] = (do_ref[:, c].astype(f32) * column).astype(bf16)
        dv = dot(e_ref[:, first * t : (first + SHARE) * t], heads(scaled_ref, first, SHARE), NN)
        store_parts(dv, g, t, parts)


def first_probs_kernel(core_ref, line_ref, q_ref, do_ref, mine_ref, others_ref,
                       k0, k1, k2, k3, k4, k5,
                       e_ref, scaled_ref, inv_ref, keys_ref, bias_ref, *parts):
    t = line_ref.shape[0]
    core = core_ref[0]
    gather_blocks(k0, k1, k2, k3, k4, k5, core, keys_ref)
    mine, others = mine_ref[...].astype(f32), others_ref[...].astype(f32)
    node, up, upper = (line_ref[:, j : j + 1] for j in range(3))
    tok = lax.broadcasted_iota(jnp.int32, (t, t), 0)
    key = lax.broadcasted_iota(jnp.int32, (t, t), 1)
    last_ids = jnp.where(core == 0, others[2:3], others[0:1])
    for slot, ids in enumerate((mine[0:1], mine[1:2], others[1:2], mine[2:3], last_ids)):
        seen = (ids == node) | (ids == up) | (ids == upper)
        if slot == 0:
            seen = seen & (key <= tok)
        bias_ref[slot * t : (slot + 1) * t, :] = jnp.where(seen, 0.0, HIDDEN).T
    probs_of(range(HALF), keys_ref, bias_ref, q_ref, do_ref, e_ref, scaled_ref, inv_ref, parts)


def second_probs_kernel(q_ref, do_ref, keys_ref, bias_ref, *refs):
    earlier, (e_ref, scaled_ref, inv_ref), parts = refs[:5], refs[5:8], refs[8:]
    carry_parts(parts, earlier)
    probs_of(range(HALF, KEY_VALUE_HEADS), keys_ref, bias_ref, q_ref, do_ref, e_ref, scaled_ref, inv_ref, parts)


def score_grads_of(groups, vals_ref, e_ref, scaled_ref, inv_ref, q_ref, ds_ref, context_ref, parts):
    t = q_ref.shape[0]
    w = HEAD_WIDTH
    for g in groups:
        vals = vals_ref[:, g * w : (g + 1) * w]
        first = (g - groups[0]) * SHARE
        for h in range(first, first + SHARE, 2):
            c = slice(h * t, (h + 2) * t)
            e = e_ref[:, c]
            inv = jnp.concatenate([inv_ref[h : h + 1, :], inv_ref[h + 1 : h + 2, :]], axis=1)
            context = dot(vals, e, TN) * inv
            context_ref[:, c] = context.astype(bf16)
            rows = heads(scaled_ref, h, 2)
            delta = jnp.sum(rows.T.astype(f32) * context, axis=0, keepdims=True)
            ds_ref[:, c] = (e.astype(f32) * (dot(vals, rows, NT) - delta)).astype(bf16)
        dk = dot(ds_ref[:, first * t : (first + SHARE) * t], heads(q_ref, g * SHARE, SHARE), NN) * SCALE
        store_parts(dk, g, t, parts)


def first_score_grad_kernel(core_ref, e_ref, scaled_ref, inv_ref, q_ref, v0, v1, v2, v3, v4, v5,
                            ds_ref, context_ref, vals_ref, *parts):
    gather_blocks(v0, v1, v2, v3, v4, v5, core_ref[0], vals_ref)
    score_grads_of(range(HALF), vals_ref, e_ref, scaled_ref, inv_ref, q_ref, ds_ref, context_ref, parts)


def second_score_grad_kernel(e_ref, scaled_ref, inv_ref, q_ref, vals_ref, *refs):
    earlier, (ds_ref, context_ref), parts = refs[:5], refs[5:7], refs[7:]
    carry_parts(parts, earlier)
    groups = range(HALF, KEY_VALUE_HEADS)
    score_grads_of(groups, vals_ref, e_ref, scaled_ref, inv_ref, q_ref, ds_ref, context_ref, parts)


def rows_kernel(c0, c1, ds0, ds1, keys_ref, o_ref, dq_ref):
    t = o_ref.shape[0]
    w = HEAD_WIDTH
    for h in range(0, QUERY_HEADS, 2):
        context_ref, ds_ref = ((c0, ds0), (c1, ds1))[h // (HALF * SHARE)]
        g = slice(h // SHARE * w, (h // SHARE + 1) * w)
        c = slice(h % (HALF * SHARE) * t, (h % (HALF * SHARE) + 2) * t)
        dq = (dot(keys_ref[:, g], ds_ref[:, c], TN) * SCALE).astype(bf16)
        o = context_ref[:, c]
        for j in range(2):
            o_ref[:, (h + j) * w : (h + j + 1) * w] = o[:, j * t : (j + 1) * t].T
            dq_ref[:, (h + j) * w : (h + j + 1) * w] = dq[:, j * t : (j + 1) * t].T


def merge_kernel(core_ref, own_ref, near_ref, far_ref, got_ref, got_last_ref, own_out, near_out, far_out):
    first = core_ref[0] == 0
    last = got_last_ref[...].astype(f32)
    own_out[...] = own_ref[...] + jnp.where(first, last, 0.0)
    t = own_ref.shape[0]
    near_out[:t, :] = (near_ref[...].astype(f32) + got_ref[...].astype(f32)).astype(bf16)
    far_out[:t, :] = (far_ref[...].astype(f32) + jnp.where(first, 0.0, last)).astype(bf16)
    for out in (near_out, far_out):
        if out.shape[0] > t:
            out[t:, :] = jnp.zeros((out.shape[0] - t, out.shape[1]), bf16)


def total_kernel(own_ref, near_ref, far_ref, out_ref):
    t = own_ref.shape[0]
    out_ref[...] = (own_ref[...] + near_ref[:t, :].astype(f32) + far_ref[:t, :].astype(f32)).astype(bf16)


def ahead(value, by):
    n = lax.axis_size("seq")
    return lax.ppermute(value, "seq", [(i, (i + by) % n) for i in range(n)])


def swap(value):
    n = lax.axis_size("seq")
    return lax.ppermute(value, "seq", [(i, i ^ 1) for i in range(n)])


def merge(core, own, near, far, got, got_last, pad=0):
    sent = S((near.shape[0] + pad, near.shape[1]), bf16)
    return call(
        merge_kernel, "merge", [SMEM] + [VMEM] * 5, [VMEM] * 3, [S(own.shape, f32), sent, sent], cost=1, limit=SMALL
    )(core, own, near, far, got, got_last)


def home(own, near, far, cost=1):
    far, near = ahead(far, -4), ahead(near, -2)
    return call(total_kernel, "total", [VMEM] * 3, VMEM, S(own.shape, bf16), cost=cost, limit=SMALL)(own, near, far)


def on_device(queries, keys, values, output_gradient, node_of, parent):
    t, width = keys.shape
    core = (lax.axis_index("seq") % 2).astype(jnp.int32).reshape(1)
    node = node_of[None]
    near, far = ahead(keys, 2), ahead(keys, 4)
    near_node, far_node = ahead(node, 2), ahead(node, 4)
    line = call(lineage_kernel, "lineage", [VMEM, VMEM], VMEM, S((t, t), f32), cost=1 << 32, limit=SMALL)(
        node, parent[None]
    )
    mine = call(nodes_kernel, "nodes", [VMEM] * 3, VMEM, S((8, t), jnp.int32), cost=1, limit=SMALL)(
        node, near_node, far_node
    )
    own, _ = lax.optimization_barrier((keys, line))
    ks = (keys, near, swap(near), far, swap(own), swap(far))
    values = jnp.pad(values, ((0, PAD_ROWS), (0, 0)))
    far, near = ahead(values, 4), ahead(values, 2)
    parts = [S((t, width), f32)] + [S((t, width), bf16)] * 4
    half_parts = [S((t, HALF * HEAD_WIDTH), p.dtype) for p in parts]
    square = S((5 * t, HALF * SHARE * t), bf16)
    blocks = S((5 * t, width), bf16)
    scaled = S((t, HALF * SHARE * HEAD_WIDTH), bf16)
    inv = S((HALF * SHARE, t), f32)
    e0, scaled0, inv0, keys_all, bias, *dv = call(
        first_probs_kernel,
        "first_probs",
        [SMEM] + [VMEM] * 11,
        [VMEM] * 10,
        [square, scaled, inv, blocks, S((5 * t, t), f32)] + half_parts,
        cost=1,
    )(core, line, queries, output_gradient, mine, swap(mine), *ks)
    dv[0], near, far = lax.optimization_barrier((dv[0], near, far))
    near_other, sibling, far_other = swap(near), swap(values), swap(far)
    e1, scaled1, inv1, *dv = call(
        second_probs_kernel, "second_probs", [VMEM] * 9, [VMEM] * 8, [square, scaled, inv] + parts, cost=1
    )(queries, output_gradient, keys_all, bias, *dv)
    near_other, sibling, far_other, e1, e0 = lax.optimization_barrier((near_other, sibling, far_other, e1, e0))
    context = S((HEAD_WIDTH, HALF * SHARE * t), bf16)
    ds0, context0, vals_all, *dk = call(
        first_score_grad_kernel,
        "first_score_grad",
        [SMEM] + [VMEM] * 10,
        [VMEM] * 8,
        [square, context, blocks] + half_parts,
        cost=1,
    )(core, e0, scaled0, inv0, queries, values, near, near_other, far, sibling, far_other)
    got, got_last, ds0 = lax.optimization_barrier((swap(dv[3]), swap(dv[4]), ds0))
    dv_own, dv_near, dv_far = merge(core, *dv[:3], got, got_last, PAD_ROWS)
    dk[0], dv_near, dv_far = lax.optimization_barrier((dk[0], dv_near, dv_far))
    dv = home(dv_own, dv_near, dv_far)
    ds1, context1, *dk = call(
        second_score_grad_kernel, "second_score_grad", [VMEM] * 10, [VMEM] * 7, [square, context] + parts, cost=1
    )(e1, scaled1, inv1, queries, vals_all, *dk)
    dk_own, dk_near, dk_far = merge(core, *dk[:3], swap(dk[3]), swap(dk[4]))
    ds0, ds1, dk_near, dk_far = lax.optimization_barrier((ds0, ds1, dk_near, dk_far))
    dk = home(dk_own, dk_near, dk_far)
    ds0, dv = lax.optimization_barrier((ds0, dv))
    attended, q_grad = call(
        rows_kernel,
        "rows",
        [VMEM] * 5,
        [VMEM] * 2,
        [S(queries.shape, bf16), S(queries.shape, bf16)],
        cost=1 << 32,
    )(context0, context1, ds0, ds1, keys_all)
    return attended, q_grad, dk, dv


def solution(mesh):
    rows = P(("grp", "seq"), None)
    return jax.shard_map(
        on_device,
        mesh=mesh,
        in_specs=(rows, rows, rows, rows, P(("grp", "seq")), P("grp")),
        out_specs=(rows, rows, rows, rows),
        check_vma=False,
    )
```

time: 46.1 us -> 43.7 us (0.948)
  waiting for transfers between devices: 4.49 us -> 8.12 us
  starting transfers between devices: 19.6 us -> 16.4 us
  other arithmetic: 1.67 us -> 0 us
  Pallas kernels: 16.7 us -> 15.6 us
    ppermute x8 -> x10, starting transfers between devices: 17.3 us -> 13.8 us  [ahead(): return lax.ppermute(value, 'seq', [(i, (i + by) % n) for i in range(n)])]
    ppermute x8 -> x10, waiting for transfers between devices: 3.48 us -> 6.08 us  [ahead(): return lax.ppermute(value, 'seq', [(i, (i + by) % n) for i in range(n)])]
    pallas_call x7 -> x10, Pallas kernels: 16.4 us -> 15.3 us  [the longest x1 3.59 us: on_device(): call(rows_kernel, 'rows', [VMEM] * 5, [VMEM] * 2, [S(queries.shape, bf16)...]
    ppermute x10 -> x11, waiting for transfers between devices: 1.01 us -> 2.04 us  [swap(): return lax.ppermute(value, 'seq', [(i, i ^ 1) for i in range(n)])]
    select_n x1 -> x0, other arithmetic: 0.99 us -> none  [with_ids(): return jnp.where(row < t, jnp.pad(keys, ((0, ID_ROWS), (0, 0))), ids)]
    convert_element_type x1 -> x0, other arithmetic: 0.66 us -> none  [with_ids(): d.astype(bf16)]
    ppermute x10 -> x11, starting transfers between devices: 2.3 us -> 2.67 us  [swap(): return lax.ppermute(value, 'seq', [(i, i ^ 1) for i in range(n)])]
    unnamed x6 -> x10, local copies, waits for them, and re-layouts: 1.79 us -> 1.72 us
  transfers between devices with their start and end apart: 18 -> 21, of which waited for: 4 -> 7; matrix products, arithmetic and copies ran while one was open for 2% -> 2% of each run, Pallas kernels for 35% -> 34%
where the time goes in v3:
time: 43.7 us; the launch traced here: 43.5 us
  starting transfers between devices  16.4 us (38%)
  Pallas kernels  15.6 us (36%)
  waiting for transfers between devices  8.12 us (19%)
  local copies, waits for them, and re-layouts  2.63 us (6%)
  between operations  0.75 us (2%)
    ppermute x10, starting transfers between devices, ahead(): return lax.ppermute(value, 'seq', [(i, (i + by) % n) for i in range(n)])  13.8 us
    ppermute x10, waiting for transfers between devices, ahead(): return lax.ppermute(value, 'seq', [(i, (i + by) % n) for i in range(n)])  6.08 us
    pallas_call x1, Pallas kernels, on_device(): call(rows_kernel, 'rows', [VMEM] * 5, [VMEM] * 2, [S(queries.shape, bf16)...  3.59 us
    pallas_call x1, Pallas kernels, on_device(): call(second_probs_kernel, 'second_probs', [VMEM] * 9, [VMEM] * 8, [square...  2.78 us
    pallas_call x1, Pallas kernels, on_device(): call(first_probs_kernel, 'first_probs', [SMEM] + [VMEM] * 11, [VMEM] * 10...  2.76 us
    ppermute x11, starting transfers between devices, swap(): return lax.ppermute(value, 'seq', [(i, i ^ 1) for i in range(n)])  2.67 us
    pallas_call x1, Pallas kernels, on_device(): call(first_score_grad_kernel, 'first_score_grad', [SMEM] + [VMEM] * 10, [...  2.27 us
    pallas_call x1, Pallas kernels, on_device(): call(second_score_grad_kernel, 'second_score_grad', [VMEM] * 10, [VMEM] *...  2.27 us
  transfers between devices with their start and end apart: 21, of which 7 were waited for; matrix products, arithmetic and copies ran while one was open for 2% of the time, Pallas kernels for 34%

profile of v3, /device:TPU:0, one launch (start us, length us, event | category | flops | bytes accessed | tf_op | source)
XLA Modules:
  0.0 43.5 jit_solution(182800670911528708)
XLA Ops:
  0.6 3.1 %collective-permute-start.1 = (s32[1,128]{1,0:T(1,128)}, s32[1,128]{1,0:T(1,128)S(1)}, u32[]{:S(2)}, u32[]{:S(2)}) collective-permute-start(s32[1,128]{1,0:T(1,128)} %bitcast.3), channel_id=1, source_target_pairs={{0,4},{1,5},{2,6},{3,7},{4,8},{5,9},{6,10},{7,11},{8,12},{9,13},{1... | collective-permute-start | bytes 1544 | tf_op jit(solution)/shard_map/ppermute | solution.py:203
  3.7 1.5 %collective-permute-start = (s32[1,128]{1,0:T(1,128)}, s32[1,128]{1,0:T(1,128)S(1)}, u32[]{:S(2)}, u32[]{:S(2)}) collective-permute-start(s32[1,128]{1,0:T(1,128)} %bitcast.4), channel_id=1, source_target_pairs={{0,2},{1,3},{2,4},{3,5},{4,6},{5,7},{6,8},{7,9},{8,10},{9,11},{10,... | collective-permute-start | bytes 1544 | tf_op jit(solution)/shard_map/ppermute | solution.py:203
  5.2 1.6 %collective-permute-start.5 = (bf16[128,512]{1,0:T(8,128)(2,1)}, bf16[128,512]{1,0:T(8,128)(2,1)S(1)}, u32[]{:S(2)}, u32[]{:S(2)}) collective-permute-start(bf16[128,512]{1,0:T(8,128)(2,1)} %k0.1), channel_id=1, source_target_pairs={{0,4},{1,5},{2,6},{3,7},{4,8},{5,9},{6,10},{7,11},{8,12},{9,13},{1... | collective-permute-start | bytes 393224 | tf_op jit(solution)/shard_map/ppermute | solution.py:203
  6.8 1.5 %collective-permute-start.3 = (bf16[128,512]{1,0:T(8,128)(2,1)}, bf16[128,512]{1,0:T(8,128)(2,1)S(1)}, u32[]{:S(2)}, u32[]{:S(2)}) collective-permute-start(bf16[128,512]{1,0:T(8,128)(2,1)} %k0.1), channel_id=1, source_target_pairs={{0,2},{1,3},{2,4},{3,5},{4,6},{5,7},{6,8},{7,9},{8,10},{9,11},{10,... | collective-permute-start | bytes 393224 | tf_op jit(solution)/shard_map/ppermute | solution.py:203
  8.3 0.9 %pad.4.v0 = bf16[144,512]{1,0:T(8,128)(2,1)S(1)} pad(bf16[128,512]{1,0:T(8,128)(2,1)} %param.8, bf16[]{:T(256)} %constant.19.clone.1), padding=0_16x0_0 | pad | bytes 278530 | tf_op jit(solution)/shard_map/jit(_pad)/pad | solution.py:237
  9.2 0.1 collective-permute-start.9
  9.4 0.0 collective-permute-done.1.far_ref
  9.4 1.7 %collective-permute-start.8 = (bf16[144,512]{1,0:T(8,128)(2,1)S(1)}, bf16[144,512]{1,0:T(8,128)(2,1)S(1)}, u32[]{:S(2)}, u32[]{:S(2)}) collective-permute-start(bf16[144,512]{1,0:T(8,128)(2,1)S(1)} %pad.4.v0), channel_id=1, source_target_pairs={{0,2},{1,3},{2,4},{3,5},{4,6},{5,7},{6,8},{7,9},{8,10},{9,11},{10,... | collective-permute-start | bytes 442376 | tf_op jit(solution)/shard_map/ppermute | solution.py:203
  11.0 0.7 %copy-done.3 = s32[128]{0:T(128)S(1)} copy-done((s32[128]{0:T(128)S(1)}, s32[128]{0:T(128)}, u32[]{:S(2)}) %copy-start.3) | copy-done | bytes 536
  11.7 0.0 collective-permute-start.2
  11.7 0.0 copy-start.4
  11.7 0.6 %copy-done.4 = s32[84]{0:T(128)S(1)} copy-done((s32[84]{0:T(128)S(1)}, s32[84]{0:T(128)}, u32[]{:S(2)}) %copy-start.4) | copy-done | bytes 360
  12.4 0.3 lineage.1.line_ref
  12.7 0.2 collective-permute-done.2.others_ref
  12.9 0.4 copy-done.2
  13.3 0.5 %collective-permute-start.6 = (bf16[128,512]{1,0:T(8,128)(2,1)S(1)}, bf16[128,512]{1,0:T(8,128)(2,1)S(1)}, u32[]{:S(2)}, u32[]{:S(2)}) collective-permute-start(bf16[128,512]{1,0:T(8,128)(2,1)S(1)} %copy-done.2), channel_id=1, source_target_pairs={{0,1},{1,0},{2,3},{3,2},{4,5},{5,4},{6,7},{7,6},{8,9},{9,8},{10,11... | collective-permute-start | bytes 393224 | tf_op jit(solution)/shard_map/ppermute | solution.py:208
  13.8 0.0 collective-permute-done.5.k3
  13.8 0.0 collective-permute-start.7
  13.8 3.6 %collective-permute-done.3.k1 = bf16[128,512]{1,0:T(8,128)(2,1)S(1)} collective-permute-done((bf16[128,512]{1,0:T(8,128)(2,1)}, bf16[128,512]{1,0:T(8,128)(2,1)S(1)}, u32[]{:S(2)}, u32[]{:S(2)}) %collective-permute-start.3) | collective-permute-done | bytes 131104 | tf_op jit(solution)/shard_map/ppermute | solution.py:203
  17.4 0.0 collective-permute-done.6.k4
  17.4 0.5 %collective-permute-start.11 = (bf16[144,512]{1,0:T(8,128)(2,1)S(1)}, bf16[144,512]{1,0:T(8,128)(2,1)S(1)}, u32[]{:S(2)}, u32[]{:S(2)}) collective-permute-start(bf16[144,512]{1,0:T(8,128)(2,1)S(1)} %pad.4.v0), channel_id=1, source_target_pairs={{0,1},{1,0},{2,3},{3,2},{4,5},{5,4},{6,7},{7,6},{8,9},{9,8},{10,11... | collective-permute-start | bytes 442376 | tf_op jit(solution)/shard_map/ppermute | solution.py:208
  18.0 0.0 collective-permute-done.7.k5
  18.0 0.8 %collective-permute-done.4.k2 = bf16[128,512]{1,0:T(8,128)(2,1)S(1)} collective-permute-done((bf16[128,512]{1,0:T(8,128)(2,1)S(1)}, bf16[128,512]{1,0:T(8,128)(2,1)S(1)}, u32[]{:S(2)}, u32[]{:S(2)}) %collective-permute-start.4) | collective-permute-done | bytes 131104 | tf_op jit(solution)/shard_map/ppermute | solution.py:208
  18.8 2.8 %first_probs.1 = (bf16[640,2048]{1,0:T(8,128)(2,1)S(1)}, bf16[128,2048]{1,0:T(8,128)(2,1)S(1)}, f32[16,128]{1,0:T(8,128)S(1)}, bf16[640,512]{1,0:T(8,128)(2,1)S(...) custom-call(s32[1]{0:T(128)} %bitcast.core_ref, ...), custom_call_target="tpu_custom_call" | custom-call | flops 1 | bytes 1 | tf_op jit(solution)/shard_map/first_probs/pallas_call | solution.py:245
  21.6 0.0 collective-permute-done.9.v3
  21.6 0.4 collective-permute-done.8.v1
  22.0 0.0 collective-permute-start.10
  22.0 0.5 %collective-permute-start.12 = (bf16[144,512]{1,0:T(8,128)(2,1)S(1)}, bf16[144,512]{1,0:T(8,128)(2,1)S(1)}, u32[]{:S(2)}, u32[]{:S(2)}) collective-permute-start(bf16[144,512]{1,0:T(8,128)(2,1)S(1)} %collective-permute-done.9.v3), channel_id=1, source_target_pairs={{0,1},{1,0},{2,3},{3,2},{4,5},{5,4},{6,7},{7,6},{8,9},{9,8},{10,11... | collective-permute-start | bytes 442376 | tf_op jit(solution)/shard_map/ppermute | solution.py:208
  22.5 2.8 %second_probs.1 = (bf16[640,2048]{1,0:T(8,128)(2,1)S(1)}, bf16[128,2048]{1,0:T(8,128)(2,1)S(1)}, f32[16,128]{1,0:T(8,128)S(1)}, f32[128,512]{1,0:T(8,128)S(1)}, ...) custom-call(bf16[128,4096]{1,0:T(8,128)(2,1)S(1)} %copy-done, ...), custom_call_target="tpu_custom_call" | custom-call | flops 1 | bytes 1 | tf_op jit(solution)/shard_map/second_probs/pallas_call | solution.py:255
  25.3 0.1 collective-permute-start.13
  25.4 0.5 %collective-permute-start.14 = (bf16[128,512]{1,0:T(8,128)(2,1)S(1)}, bf16[128,512]{1,0:T(8,128)(2,1)S(1)}, u32[]{:S(2)}, u32[]{:S(2)}) collective-permute-start(bf16[128,512]{1,0:T(8,128)(2,1)S(1)} %get-tuple-element.95), channel_id=1, source_target_pairs={{0,1},{1,0},{2,3},{3,2},{4,5},{5,4},{6,7},{7,6},{8,9},{9,8},{10,11... | collective-permute-start | bytes 393224 | tf_op jit(solution)/shard_map/ppermute | solution.py:208
  25.9 0.0 collective-permute-done.10.v2
  25.9 2.3 %first_score_grad.1 = (bf16[640,2048]{1,0:T(8,128)(2,1)S(1)}, bf16[128,2048]{1,0:T(8,128)(2,1)S(1)}, bf16[640,512]{1,0:T(8,128)(2,1)S(1)}, f32[128,256]{1,0:T(8,...) custom-call(s32[1]{0:T(128)} %bitcast.core_ref, ...), custom_call_target="tpu_custom_call" | custom-call | flops 1 | bytes 1 | tf_op jit(solution)/shard_map/first_score_grad/pallas_call | solution.py:260
  28.2 0.1 merge.2
  28.3 0.1 collective-permute-start.17
  28.4 1.2 %collective-permute-start.18 = (bf16[144,512]{1,0:T(8,128)(2,1)S(1)}, bf16[144,512]{1,0:T(8,128)(2,1)S(1)}, u32[]{:S(2)}, u32[]{:S(2)}) collective-permute-start(bf16[144,512]{1,0:T(8,128)(2,1)S(1)} %get-tuple-element.119), channel_id=1, source_target_pairs={{0,12},{1,13},{2,14},{3,15},{4,0},{5,1},{6,2},{7,3},{8,4},{9,5},{1... | collective-permute-start | bytes 442376 | tf_op jit(solution)/shard_map/ppermute | solution.py:203
  29.5 2.3 %second_score_grad.1 = (bf16[640,2048]{1,0:T(8,128)(2,1)S(1)}, bf16[128,2048]{1,0:T(8,128)(2,1)S(1)}, f32[128,512]{1,0:T(8,128)S(1)}, bf16[128,512]{1,0:T(8,128)...) custom-call(bf16[640,2048]{1,0:T(8,128)(2,1)S(1)} %get-tuple-element.86.e_ref, ...), custom_call_target="tpu_custom_call" | custom-call | flops 1 | bytes 1 | tf_op jit(solution)/shard_map/second_score_grad/pallas_call | solution.py:272
  31.8 0.1 collective-permute-start.15
  31.9 0.5 %collective-permute-start.16 = (bf16[128,512]{1,0:T(8,128)(2,1)S(1)}, bf16[128,512]{1,0:T(8,128)(2,1)S(1)}, u32[]{:S(2)}, u32[]{:S(2)}) collective-permute-start(bf16[128,512]{1,0:T(8,128)(2,1)S(1)} %get-tuple-element.113), channel_id=1, source_target_pairs={{0,1},{1,0},{2,3},{3,2},{4,5},{5,4},{6,7},{7,6},{8,9},{9,8},{10,11... | collective-permute-start | bytes 393224 | tf_op jit(solution)/shard_map/ppermute | solution.py:208
  32.4 0.8 %collective-permute-done.15.got_ref = bf16[128,512]{1,0:T(8,128)(2,1)S(1)} collective-permute-done((bf16[128,512]{1,0:T(8,128)(2,1)S(1)}, bf16[128,512]{1,0:T(8,128)(2,1)S(1)}, u32[]{:S(2)}, u32[]{:S(2)}) %collective-permute-start.15) | collective-permute-done | bytes 131104 | tf_op jit(solution)/shard_map/ppermute | solution.py:208
  33.2 0.2 collective-permute-done.16.got_last_ref
  33.4 0.1 merge.3
  33.5 1.4 %collective-permute-start.19 = (bf16[128,512]{1,0:T(8,128)(2,1)S(1)}, bf16[128,512]{1,0:T(8,128)(2,1)S(1)}, u32[]{:S(2)}, u32[]{:S(2)}) collective-permute-start(bf16[128,512]{1,0:T(8,128)(2,1)S(1)} %get-tuple-element.125), channel_id=1, source_target_pairs={{0,14},{1,15},{2,0},{3,1},{4,2},{5,3},{6,4},{7,5},{8,6},{9,7},{10,... | collective-permute-start | bytes 393224 | tf_op jit(solution)/shard_map/ppermute | solution.py:203
  34.9 1.7 %collective-permute-start.20 = (bf16[128,512]{1,0:T(8,128)(2,1)S(1)}, bf16[128,512]{1,0:T(8,128)(2,1)S(1)}, u32[]{:S(2)}, u32[]{:S(2)}) collective-permute-start(bf16[128,512]{1,0:T(8,128)(2,1)S(1)} %get-tuple-element.126), channel_id=1, source_target_pairs={{0,12},{1,13},{2,14},{3,15},{4,0},{5,1},{6,2},{7,3},{8,4},{9,5},{1... | collective-permute-start | bytes 393224 | tf_op jit(solution)/shard_map/ppermute | solution.py:203
  36.6 0.7 %total.2 = bf16[128,512]{1,0:T(8,128)(2,1)} custom-call(f32[128,512]{1,0:T(8,128)S(1)} %get-tuple-element.117.own_ref, bf16[144,512]{1,0:T(8,128)(2,1)S(1)} %collective-permute-done.17.near_ref, bf16[144,512]{1,0:T(8,128)(2,1)S(1)} %collective-permute-done.18.far_ref), custom_call_target="tpu_custom_call" | custom-call | flops 1 | bytes 1 | tf_op jit(solution)/shard_map/total/pallas_call | solution.py:220
  37.3 3.6 %rows.1 = (bf16[128,4096]{1,0:T(8,128)(2,1)}, bf16[128,4096]{1,0:T(8,128)(2,1)}) custom-call(bf16[128,2048]{1,0:T(8,128)(2,1)S(1)} %get-tuple-element.85.c0, bf16[128,2048]{1,0:T(8,128)(2,1)S(1)} %get-tuple-element.106.c1, bf16[640,2048]{1,0:T(8,128)(2,1)S(1)} %get-tuple-element.120.ds0, bf16[640,2048]{1,0:T(8,128)(2,1)S(1)} %get-tuple-element.121.ds1, ...), custom_call_target="tpu_custom_call" | custom-call | flops 4294967296 | bytes 1 | tf_op jit(solution)/shard_map/rows/pallas_call | solution.py:279
  40.9 2.0 %collective-permute-done.20.far_ref = bf16[128,512]{1,0:T(8,128)(2,1)S(1)} collective-permute-done((bf16[128,512]{1,0:T(8,128)(2,1)S(1)}, bf16[128,512]{1,0:T(8,128)(2,1)S(1)}, u32[]{:S(2)}, u32[]{:S(2)}) %collective-permute-start.20) | collective-permute-done | bytes 131104 | tf_op jit(solution)/shard_map/ppermute | solution.py:203
  42.8 0.7 %total.3 = bf16[128,512]{1,0:T(8,128)(2,1)} custom-call(f32[128,512]{1,0:T(8,128)S(1)} %get-tuple-element.124.own_ref, bf16[128,512]{1,0:T(8,128)(2,1)S(1)} %collective-permute-done.19.near_ref, bf16[128,512]{1,0:T(8,128)(2,1)S(1)} %collective-permute-done.20.far_ref), custom_call_target="tpu_custom_call" | custom-call | flops 1 | bytes 1 | tf_op jit(solution)/shard_map/total/pallas_call | solution.py:220
  (16 shorter events, 0.0 us)
Async XLA Ops:
  0.6 8.7 %collective-permute-start.1 = (s32[1,128]{1,0:T(1,128)}, s32[1,128]{1,0:T(1,128)S(1)}, u32[]{:S(2)}, u32[]{:S(2)}) collective-permute-start(s32[1,128]{1,0:T(1,128)} %bitcast.3), channel_id=1, source_target_pairs={{0,4},{1,5},{2,6},{3,7},{4,8},{5,9},{6,10},{7,11},{8,12},{9,13},{1... | collective-permute-start | bytes 1544 | tf_op jit(solution)/shard_map/ppermute | solution.py:203
  3.7 7.3 %collective-permute-start = (s32[1,128]{1,0:T(1,128)}, s32[1,128]{1,0:T(1,128)S(1)}, u32[]{:S(2)}, u32[]{:S(2)}) collective-permute-start(s32[1,128]{1,0:T(1,128)} %bitcast.4), channel_id=1, source_target_pairs={{0,2},{1,3},{2,4},{3,5},{4,6},{5,7},{6,8},{7,9},{8,10},{9,11},{10,... | collective-permute-start | bytes 1544 | tf_op jit(solution)/shard_map/ppermute | solution.py:203
  5.2 8.6 %collective-permute-start.5 = (bf16[128,512]{1,0:T(8,128)(2,1)}, bf16[128,512]{1,0:T(8,128)(2,1)S(1)}, u32[]{:S(2)}, u32[]{:S(2)}) collective-permute-start(bf16[128,512]{1,0:T(8,128)(2,1)} %k0.1), channel_id=1, source_target_pairs={{0,4},{1,5},{2,6},{3,7},{4,8},{5,9},{6,10},{7,11},{8,12},{9,13},{1... | collective-permute-start | bytes 393224 | tf_op jit(solution)/shard_map/ppermute | solution.py:203
  6.8 10.6 %collective-permute-start.3 = (bf16[128,512]{1,0:T(8,128)(2,1)}, bf16[128,512]{1,0:T(8,128)(2,1)S(1)}, u32[]{:S(2)}, u32[]{:S(2)}) collective-permute-start(bf16[128,512]{1,0:T(8,128)(2,1)} %k0.1), channel_id=1, source_target_pairs={{0,2},{1,3},{2,4},{3,5},{4,6},{5,7},{6,8},{7,9},{8,10},{9,11},{10,... | collective-permute-start | bytes 393224 | tf_op jit(solution)/shard_map/ppermute | solution.py:203
  9.2 12.3 %collective-permute-start.9 = (bf16[144,512]{1,0:T(8,128)(2,1)S(1)}, bf16[144,512]{1,0:T(8,128)(2,1)S(1)}, u32[]{:S(2)}, u32[]{:S(2)}) collective-permute-start(bf16[144,512]{1,0:T(8,128)(2,1)S(1)} %pad.4.v0), channel_id=1, source_target_pairs={{0,4},{1,5},{2,6},{3,7},{4,8},{5,9},{6,10},{7,11},{8,12},{9,13},{1... | collective-permute-start | bytes 442376 | tf_op jit(solution)/shard_map/ppermute | solution.py:203
  9.4 12.6 %collective-permute-start.8 = (bf16[144,512]{1,0:T(8,128)(2,1)S(1)}, bf16[144,512]{1,0:T(8,128)(2,1)S(1)}, u32[]{:S(2)}, u32[]{:S(2)}) collective-permute-start(bf16[144,512]{1,0:T(8,128)(2,1)S(1)} %pad.4.v0), channel_id=1, source_target_pairs={{0,2},{1,3},{2,4},{3,5},{4,6},{5,7},{6,8},{7,9},{8,10},{9,11},{10,... | collective-permute-start | bytes 442376 | tf_op jit(solution)/shard_map/ppermute | solution.py:203
  11.0 0.7 %copy-start.3 = (s32[128]{0:T(128)S(1)}, s32[128]{0:T(128)}, u32[]{:S(2)}) copy-start(s32[128]{0:T(128)} %param.10) | copy-start | bytes 1540
  11.7 1.2 %collective-permute-start.2 = (s32[8,128]{1,0:T(8,128)S(1)}, s32[8,128]{1,0:T(8,128)S(1)}, u32[]{:S(2)}, u32[]{:S(2)}) collective-permute-start(s32[8,128]{1,0:T(8,128)S(1)} %nodes.1.mine_ref), channel_id=1, source_target_pairs={{0,1},{1,0},{2,3},{3,2},{4,5},{5,4},{6,7},{7,6},{8,9},{9,8},{10,11... | collective-permute-start | bytes 12296 | tf_op jit(solution)/shard_map/ppermute | solution.py:208
  11.7 0.7 %copy-start.4 = (s32[84]{0:T(128)S(1)}, s32[84]{0:T(128)}, u32[]{:S(2)}) copy-start(s32[84]{0:T(128)} %param.11) | copy-start | bytes 1012
  12.4 0.9 %copy-start.2 = (bf16[128,512]{1,0:T(8,128)(2,1)S(1)}, bf16[128,512]{1,0:T(8,128)(2,1)}, u32[]{:S(2)}) copy-start(bf16[128,512]{1,0:T(8,128)(2,1)} %k0.1) | copy-start | bytes 393220
  12.4 6.4 %copy-start = (bf16[128,4096]{1,0:T(8,128)(2,1)S(1)}, bf16[128,4096]{1,0:T(8,128)(2,1)}, u32[]{:S(2)}) copy-start(bf16[128,4096]{1,0:T(8,128)(2,1)} %q_ref.7) | copy-start | bytes 3145732
  12.4 6.4 %copy-start.1 = (bf16[128,4096]{1,0:T(8,128)(2,1)S(1)}, bf16[128,4096]{1,0:T(8,128)(2,1)}, u32[]{:S(2)}) copy-start(bf16[128,4096]{1,0:T(8,128)(2,1)} %do_ref.3) | copy-start | bytes 3145732
  13.3 4.2 %collective-permute-start.6 = (bf16[128,512]{1,0:T(8,128)(2,1)S(1)}, bf16[128,512]{1,0:T(8,128)(2,1)S(1)}, u32[]{:S(2)}, u32[]{:S(2)}) collective-permute-start(bf16[128,512]{1,0:T(8,128)(2,1)S(1)} %copy-done.2), channel_id=1, source_target_pairs={{0,1},{1,0},{2,3},{3,2},{4,5},{5,4},{6,7},{7,6},{8,9},{9,8},{10,11... | collective-permute-start | bytes 393224 | tf_op jit(solution)/shard_map/ppermute | solution.py:208
  13.8 4.2 %collective-permute-start.7 = (bf16[128,512]{1,0:T(8,128)(2,1)S(1)}, bf16[128,512]{1,0:T(8,128)(2,1)S(1)}, u32[]{:S(2)}, u32[]{:S(2)}) collective-permute-start(bf16[128,512]{1,0:T(8,128)(2,1)S(1)} %collective-permute-done.5.k3), channel_id=1, source_target_pairs={{0,1},{1,0},{2,3},{3,2},{4,5},{5,4},{6,7},{7,6},{8,9},{9,8},{10,11... | collective-permute-start | bytes 393224 | tf_op jit(solution)/shard_map/ppermute | solution.py:208
  17.4 1.3 %collective-permute-start.4 = (bf16[128,512]{1,0:T(8,128)(2,1)S(1)}, bf16[128,512]{1,0:T(8,128)(2,1)S(1)}, u32[]{:S(2)}, u32[]{:S(2)}) collective-permute-start(bf16[128,512]{1,0:T(8,128)(2,1)S(1)} %collective-permute-done.3.k1), channel_id=1, source_target_pairs={{0,1},{1,0},{2,3},{3,2},{4,5},{5,4},{6,7},{7,6},{8,9},{9,8},{10,11... | collective-permute-start | bytes 393224 | tf_op jit(solution)/shard_map/ppermute | solution.py:208
  17.4 8.4 %collective-permute-start.11 = (bf16[144,512]{1,0:T(8,128)(2,1)S(1)}, bf16[144,512]{1,0:T(8,128)(2,1)S(1)}, u32[]{:S(2)}, u32[]{:S(2)}) collective-permute-start(bf16[144,512]{1,0:T(8,128)(2,1)S(1)} %pad.4.v0), channel_id=1, source_target_pairs={{0,1},{1,0},{2,3},{3,2},{4,5},{5,4},{6,7},{7,6},{8,9},{9,8},{10,11... | collective-permute-start | bytes 442376 | tf_op jit(solution)/shard_map/ppermute | solution.py:208
  22.0 3.9 %collective-permute-start.10 = (bf16[144,512]{1,0:T(8,128)(2,1)S(1)}, bf16[144,512]{1,0:T(8,128)(2,1)S(1)}, u32[]{:S(2)}, u32[]{:S(2)}) collective-permute-start(bf16[144,512]{1,0:T(8,128)(2,1)S(1)} %collective-permute-done.8.v1), channel_id=1, source_target_pairs={{0,1},{1,0},{2,3},{3,2},{4,5},{5,4},{6,7},{7,6},{8,9},{9,8},{10,11... | collective-permute-start | bytes 442376 | tf_op jit(solution)/shard_map/ppermute | solution.py:208
  22.0 3.9 %collective-permute-start.12 = (bf16[144,512]{1,0:T(8,128)(2,1)S(1)}, bf16[144,512]{1,0:T(8,128)(2,1)S(1)}, u32[]{:S(2)}, u32[]{:S(2)}) collective-permute-start(bf16[144,512]{1,0:T(8,128)(2,1)S(1)} %collective-permute-done.9.v3), channel_id=1, source_target_pairs={{0,1},{1,0},{2,3},{3,2},{4,5},{5,4},{6,7},{7,6},{8,9},{9,8},{10,11... | collective-permute-start | bytes 442376 | tf_op jit(solution)/shard_map/ppermute | solution.py:208
  25.3 2.9 %collective-permute-start.13 = (bf16[128,512]{1,0:T(8,128)(2,1)S(1)}, bf16[128,512]{1,0:T(8,128)(2,1)S(1)}, u32[]{:S(2)}, u32[]{:S(2)}) collective-permute-start(bf16[128,512]{1,0:T(8,128)(2,1)S(1)} %get-tuple-element.94), channel_id=1, source_target_pairs={{0,1},{1,0},{2,3},{3,2},{4,5},{5,4},{6,7},{7,6},{8,9},{9,8},{10,11... | collective-permute-start | bytes 393224 | tf_op jit(solution)/shard_map/ppermute | solution.py:208
  25.4 2.8 %collective-permute-start.14 = (bf16[128,512]{1,0:T(8,128)(2,1)S(1)}, bf16[128,512]{1,0:T(8,128)(2,1)S(1)}, u32[]{:S(2)}, u32[]{:S(2)}) collective-permute-start(bf16[128,512]{1,0:T(8,128)(2,1)S(1)} %get-tuple-element.95), channel_id=1, source_target_pairs={{0,1},{1,0},{2,3},{3,2},{4,5},{5,4},{6,7},{7,6},{8,9},{9,8},{10,11... | collective-permute-start | bytes 393224 | tf_op jit(solution)/shard_map/ppermute | solution.py:208
  28.3 8.3 %collective-permute-start.17 = (bf16[144,512]{1,0:T(8,128)(2,1)S(1)}, bf16[144,512]{1,0:T(8,128)(2,1)S(1)}, u32[]{:S(2)}, u32[]{:S(2)}) collective-permute-start(bf16[144,512]{1,0:T(8,128)(2,1)S(1)} %get-tuple-element.118), channel_id=1, source_target_pairs={{0,14},{1,15},{2,0},{3,1},{4,2},{5,3},{6,4},{7,5},{8,6},{9,7},{10,... | collective-permute-start | bytes 442376 | tf_op jit(solution)/shard_map/ppermute | solution.py:203
  28.4 8.2 %collective-permute-start.18 = (bf16[144,512]{1,0:T(8,128)(2,1)S(1)}, bf16[144,512]{1,0:T(8,128)(2,1)S(1)}, u32[]{:S(2)}, u32[]{:S(2)}) collective-permute-start(bf16[144,512]{1,0:T(8,128)(2,1)S(1)} %get-tuple-element.119), channel_id=1, source_target_pairs={{0,12},{1,13},{2,14},{3,15},{4,0},{5,1},{6,2},{7,3},{8,4},{9,5},{1... | collective-permute-start | bytes 442376 | tf_op jit(solution)/shard_map/ppermute | solution.py:203
  31.8 1.4 %collective-permute-start.15 = (bf16[128,512]{1,0:T(8,128)(2,1)S(1)}, bf16[128,512]{1,0:T(8,128)(2,1)S(1)}, u32[]{:S(2)}, u32[]{:S(2)}) collective-permute-start(bf16[128,512]{1,0:T(8,128)(2,1)S(1)} %get-tuple-element.112), channel_id=1, source_target_pairs={{0,1},{1,0},{2,3},{3,2},{4,5},{5,4},{6,7},{7,6},{8,9},{9,8},{10,11... | collective-permute-start | bytes 393224 | tf_op jit(solution)/shard_map/ppermute | solution.py:208
  31.9 1.5 %collective-permute-start.16 = (bf16[128,512]{1,0:T(8,128)(2,1)S(1)}, bf16[128,512]{1,0:T(8,128)(2,1)S(1)}, u32[]{:S(2)}, u32[]{:S(2)}) collective-permute-start(bf16[128,512]{1,0:T(8,128)(2,1)S(1)} %get-tuple-element.113), channel_id=1, source_target_pairs={{0,1},{1,0},{2,3},{3,2},{4,5},{5,4},{6,7},{7,6},{8,9},{9,8},{10,11... | collective-permute-start | bytes 393224 | tf_op jit(solution)/shard_map/ppermute | solution.py:208
  33.5 7.3 %collective-permute-start.19 = (bf16[128,512]{1,0:T(8,128)(2,1)S(1)}, bf16[128,512]{1,0:T(8,128)(2,1)S(1)}, u32[]{:S(2)}, u32[]{:S(2)}) collective-permute-start(bf16[128,512]{1,0:T(8,128)(2,1)S(1)} %get-tuple-element.125), channel_id=1, source_target_pairs={{0,14},{1,15},{2,0},{3,1},{4,2},{5,3},{6,4},{7,5},{8,6},{9,7},{10,... | collective-permute-start | bytes 393224 | tf_op jit(solution)/shard_map/ppermute | solution.py:203
  34.9 8.0 %collective-permute-start.20 = (bf16[128,512]{1,0:T(8,128)(2,1)S(1)}, bf16[128,512]{1,0:T(8,128)(2,1)S(1)}, u32[]{:S(2)}, u32[]{:S(2)}) collective-permute-start(bf16[128,512]{1,0:T(8,128)(2,1)S(1)} %get-tuple-element.126), channel_id=1, source_target_pairs={{0,12},{1,13},{2,14},{3,15},{4,0},{5,1},{6,2},{7,3},{8,4},{9,5},{1... | collective-permute-start | bytes 393224 | tf_op jit(solution)/shard_map/ppermute | solution.py:203

commit v4 on v3

--- a/solution.py
+++ b/solution.py
@@ -193,9 +193,9 @@
             out[t:, :] = jnp.zeros((out.shape[0] - t, out.shape[1]), bf16)
 
 
-def total_kernel(own_ref, near_ref, far_ref, out_ref):
+def add_kernel(own_ref, part_ref, out_ref):
     t = own_ref.shape[0]
-    out_ref[...] = (own_ref[...] + near_ref[:t, :].astype(f32) + far_ref[:t, :].astype(f32)).astype(bf16)
+    out_ref[...] = (own_ref[...] + part_ref[:t, :].astype(f32)).astype(out_ref.dtype)
 
 
 def ahead(value, by):
@@ -215,9 +215,13 @@
     )(core, own, near, far, got, got_last)
 
 
-def home(own, near, far, cost=1):
+def add(own, part, dtype, cost):
+    return call(add_kernel, "add", [VMEM] * 2, VMEM, S(own.shape, dtype), cost=cost, limit=SMALL)(own, part)
+
+
+def home(own, near, far):
     far, near = ahead(far, -4), ahead(near, -2)
-    return call(total_kernel, "total", [VMEM] * 3, VMEM, S(own.shape, bf16), cost=cost, limit=SMALL)(own, near, far)
+    return add(add(own, far, f32, 1 << 26), near, bf16, 1)
 
 
 def on_device(queries, keys, values, output_gradient, node_of, parent):

time: 43.7 us -> 42.3 us (0.968); the launches traced: 43.5 us -> 41.7 us
  waiting for transfers between devices: 8.12 us -> 6.23 us
    ppermute x10, waiting for transfers between devices: 6.08 us -> 4.19 us  [ahead(): return lax.ppermute(value, 'seq', [(i, (i + by) % n) for i in range(n)])]
    pallas_call x2 -> x4, Pallas kernels: 1.4 us -> 1.41 us  [add(): call(add_kernel, 'add', [VMEM] * 2, VMEM, S(own.shape, dtype), cost=cost,...]
  transfers between devices with their start and end apart: 21 -> 21, of which waited for: 7 -> 7; matrix products, arithmetic and copies ran while one was open for 2% -> 2% of each run, Pallas kernels for 34% -> 36%
where the time goes in v4:
time: 42.3 us; the launch traced here: 41.7 us
  starting transfers between devices  16.4 us (39%)
  Pallas kernels  15.6 us (37%)
  waiting for transfers between devices  6.23 us (15%)
  local copies, waits for them, and re-layouts  2.63 us (6%)
  between operations  0.77 us (2%)
    ppermute x10, starting transfers between devices, ahead(): return lax.ppermute(value, 'seq', [(i, (i + by) % n) for i in range(n)])  13.8 us
    ppermute x10, waiting for transfers between devices, ahead(): return lax.ppermute(value, 'seq', [(i, (i + by) % n) for i in range(n)])  4.19 us
    pallas_call x1, Pallas kernels, on_device(): call(rows_kernel, 'rows', [VMEM] * 5, [VMEM] * 2, [S(queries.shape, bf16)...  3.59 us
    pallas_call x1, Pallas kernels, on_device(): call(second_probs_kernel, 'second_probs', [VMEM] * 9, [VMEM] * 8, [square...  2.78 us
    pallas_call x1, Pallas kernels, on_device(): call(first_probs_kernel, 'first_probs', [SMEM] + [VMEM] * 11, [VMEM] * 10...  2.76 us
    ppermute x11, starting transfers between devices, swap(): return lax.ppermute(value, 'seq', [(i, i ^ 1) for i in range(n)])  2.67 us
    pallas_call x1, Pallas kernels, on_device(): call(first_score_grad_kernel, 'first_score_grad', [SMEM] + [VMEM] * 10, [...  2.27 us
    pallas_call x1, Pallas kernels, on_device(): call(second_score_grad_kernel, 'second_score_grad', [VMEM] * 10, [VMEM] *...  2.27 us
  transfers between devices with their start and end apart: 21, of which 7 were waited for; matrix products, arithmetic and copies ran while one was open for 2% of the time, Pallas kernels for 36%

profile of v4, /device:TPU:0, one launch (start us, length us, event | category | flops | bytes accessed | tf_op | source)
XLA Modules:
  0.0 41.7 jit_solution(15927948358329941215)
XLA Ops:
  0.6 3.1 %collective-permute-start.1 = (s32[1,128]{1,0:T(1,128)}, s32[1,128]{1,0:T(1,128)S(1)}, u32[]{:S(2)}, u32[]{:S(2)}) collective-permute-start(s32[1,128]{1,0:T(1,128)} %bitcast.3), channel_id=1, source_target_pairs={{0,4},{1,5},{2,6},{3,7},{4,8},{5,9},{6,10},{7,11},{8,12},{9,13},{1... | collective-permute-start | bytes 1544 | tf_op jit(solution)/shard_map/ppermute | solution.py:203
  3.7 1.5 %collective-permute-start = (s32[1,128]{1,0:T(1,128)}, s32[1,128]{1,0:T(1,128)S(1)}, u32[]{:S(2)}, u32[]{:S(2)}) collective-permute-start(s32[1,128]{1,0:T(1,128)} %bitcast.4), channel_id=1, source_target_pairs={{0,2},{1,3},{2,4},{3,5},{4,6},{5,7},{6,8},{7,9},{8,10},{9,11},{10,... | collective-permute-start | bytes 1544 | tf_op jit(solution)/shard_map/ppermute | solution.py:203
  5.2 1.6 %collective-permute-start.5 = (bf16[128,512]{1,0:T(8,128)(2,1)}, bf16[128,512]{1,0:T(8,128)(2,1)S(1)}, u32[]{:S(2)}, u32[]{:S(2)}) collective-permute-start(bf16[128,512]{1,0:T(8,128)(2,1)} %k0.1), channel_id=1, source_target_pairs={{0,4},{1,5},{2,6},{3,7},{4,8},{5,9},{6,10},{7,11},{8,12},{9,13},{1... | collective-permute-start | bytes 393224 | tf_op jit(solution)/shard_map/ppermute | solution.py:203
  6.8 1.5 %collective-permute-start.3 = (bf16[128,512]{1,0:T(8,128)(2,1)}, bf16[128,512]{1,0:T(8,128)(2,1)S(1)}, u32[]{:S(2)}, u32[]{:S(2)}) collective-permute-start(bf16[128,512]{1,0:T(8,128)(2,1)} %k0.1), channel_id=1, source_target_pairs={{0,2},{1,3},{2,4},{3,5},{4,6},{5,7},{6,8},{7,9},{8,10},{9,11},{10,... | collective-permute-start | bytes 393224 | tf_op jit(solution)/shard_map/ppermute | solution.py:203
  8.3 0.9 %pad.4.v0 = bf16[144,512]{1,0:T(8,128)(2,1)S(1)} pad(bf16[128,512]{1,0:T(8,128)(2,1)} %param.8, bf16[]{:T(256)} %constant.19.clone.1), padding=0_16x0_0 | pad | bytes 278530 | tf_op jit(solution)/shard_map/jit(_pad)/pad | solution.py:241
  9.2 0.1 collective-permute-start.9
  9.4 0.0 collective-permute-done.1.far_ref
  9.4 1.7 %collective-permute-start.8 = (bf16[144,512]{1,0:T(8,128)(2,1)S(1)}, bf16[144,512]{1,0:T(8,128)(2,1)S(1)}, u32[]{:S(2)}, u32[]{:S(2)}) collective-permute-start(bf16[144,512]{1,0:T(8,128)(2,1)S(1)} %pad.4.v0), channel_id=1, source_target_pairs={{0,2},{1,3},{2,4},{3,5},{4,6},{5,7},{6,8},{7,9},{8,10},{9,11},{10,... | collective-permute-start | bytes 442376 | tf_op jit(solution)/shard_map/ppermute | solution.py:203
  11.0 0.0 collective-permute-done.near_ref
  11.0 0.7 %copy-done.3 = s32[128]{0:T(128)S(1)} copy-done((s32[128]{0:T(128)S(1)}, s32[128]{0:T(128)}, u32[]{:S(2)}) %copy-start.3) | copy-done | bytes 536
  11.7 0.0 collective-permute-start.2
  11.7 0.0 copy-start.4
  11.7 0.6 %copy-done.4 = s32[84]{0:T(128)S(1)} copy-done((s32[84]{0:T(128)S(1)}, s32[84]{0:T(128)}, u32[]{:S(2)}) %copy-start.4) | copy-done | bytes 360
  12.4 0.3 lineage.1.line_ref
  12.7 0.2 collective-permute-done.2.others_ref
  12.9 0.4 copy-done.2
  13.3 0.5 %collective-permute-start.6 = (bf16[128,512]{1,0:T(8,128)(2,1)S(1)}, bf16[128,512]{1,0:T(8,128)(2,1)S(1)}, u32[]{:S(2)}, u32[]{:S(2)}) collective-permute-start(bf16[128,512]{1,0:T(8,128)(2,1)S(1)} %copy-done.2), channel_id=1, source_target_pairs={{0,1},{1,0},{2,3},{3,2},{4,5},{5,4},{6,7},{7,6},{8,9},{9,8},{10,11... | collective-permute-start | bytes 393224 | tf_op jit(solution)/shard_map/ppermute | solution.py:208
  13.8 0.0 collective-permute-done.5.k3
  13.8 0.0 collective-permute-start.7
  13.8 3.6 %collective-permute-done.3.k1 = bf16[128,512]{1,0:T(8,128)(2,1)S(1)} collective-permute-done((bf16[128,512]{1,0:T(8,128)(2,1)}, bf16[128,512]{1,0:T(8,128)(2,1)S(1)}, u32[]{:S(2)}, u32[]{:S(2)}) %collective-permute-start.3) | collective-permute-done | bytes 131104 | tf_op jit(solution)/shard_map/ppermute | solution.py:203
  17.4 0.5 %collective-permute-start.11 = (bf16[144,512]{1,0:T(8,128)(2,1)S(1)}, bf16[144,512]{1,0:T(8,128)(2,1)S(1)}, u32[]{:S(2)}, u32[]{:S(2)}) collective-permute-start(bf16[144,512]{1,0:T(8,128)(2,1)S(1)} %pad.4.v0), channel_id=1, source_target_pairs={{0,1},{1,0},{2,3},{3,2},{4,5},{5,4},{6,7},{7,6},{8,9},{9,8},{10,11... | collective-permute-start | bytes 442376 | tf_op jit(solution)/shard_map/ppermute | solution.py:208
  18.0 0.8 %collective-permute-done.4.k2 = bf16[128,512]{1,0:T(8,128)(2,1)S(1)} collective-permute-done((bf16[128,512]{1,0:T(8,128)(2,1)S(1)}, bf16[128,512]{1,0:T(8,128)(2,1)S(1)}, u32[]{:S(2)}, u32[]{:S(2)}) %collective-permute-start.4) | collective-permute-done | bytes 131104 | tf_op jit(solution)/shard_map/ppermute | solution.py:208
  18.8 2.8 %first_probs.1 = (bf16[640,2048]{1,0:T(8,128)(2,1)S(1)}, bf16[128,2048]{1,0:T(8,128)(2,1)S(1)}, f32[16,128]{1,0:T(8,128)S(1)}, bf16[640,512]{1,0:T(8,128)(2,1)S(...) custom-call(s32[1]{0:T(128)} %bitcast.core_ref, ...), custom_call_target="tpu_custom_call" | custom-call | flops 1 | bytes 1 | tf_op jit(solution)/shard_map/first_probs/pallas_call | solution.py:249
  21.6 0.0 collective-permute-done.9.v3
  21.6 0.4 %collective-permute-done.8.v1 = bf16[144,512]{1,0:T(8,128)(2,1)S(1)} collective-permute-done((bf16[144,512]{1,0:T(8,128)(2,1)S(1)}, bf16[144,512]{1,0:T(8,128)(2,1)S(1)}, u32[]{:S(2)}, u32[]{:S(2)}) %collective-permute-start.8) | collective-permute-done | bytes 147488 | tf_op jit(solution)/shard_map/ppermute | solution.py:203
  22.0 0.0 collective-permute-start.10
  22.0 0.5 %collective-permute-start.12 = (bf16[144,512]{1,0:T(8,128)(2,1)S(1)}, bf16[144,512]{1,0:T(8,128)(2,1)S(1)}, u32[]{:S(2)}, u32[]{:S(2)}) collective-permute-start(bf16[144,512]{1,0:T(8,128)(2,1)S(1)} %collective-permute-done.9.v3), channel_id=1, source_target_pairs={{0,1},{1,0},{2,3},{3,2},{4,5},{5,4},{6,7},{7,6},{8,9},{9,8},{10,11... | collective-permute-start | bytes 442376 | tf_op jit(solution)/shard_map/ppermute | solution.py:208
  22.5 2.8 %second_probs.1 = (bf16[640,2048]{1,0:T(8,128)(2,1)S(1)}, bf16[128,2048]{1,0:T(8,128)(2,1)S(1)}, f32[16,128]{1,0:T(8,128)S(1)}, f32[128,512]{1,0:T(8,128)S(1)}, ...) custom-call(bf16[128,4096]{1,0:T(8,128)(2,1)S(1)} %copy-done, ...), custom_call_target="tpu_custom_call" | custom-call | flops 1 | bytes 1 | tf_op jit(solution)/shard_map/second_probs/pallas_call | solution.py:259
  25.3 0.1 collective-permute-start.13
  25.4 0.5 %collective-permute-start.14 = (bf16[128,512]{1,0:T(8,128)(2,1)S(1)}, bf16[128,512]{1,0:T(8,128)(2,1)S(1)}, u32[]{:S(2)}, u32[]{:S(2)}) collective-permute-start(bf16[128,512]{1,0:T(8,128)(2,1)S(1)} %get-tuple-element.95), channel_id=1, source_target_pairs={{0,1},{1,0},{2,3},{3,2},{4,5},{5,4},{6,7},{7,6},{8,9},{9,8},{10,11... | collective-permute-start | bytes 393224 | tf_op jit(solution)/shard_map/ppermute | solution.py:208
  25.9 2.3 %first_score_grad.1 = (bf16[640,2048]{1,0:T(8,128)(2,1)S(1)}, bf16[128,2048]{1,0:T(8,128)(2,1)S(1)}, bf16[640,512]{1,0:T(8,128)(2,1)S(1)}, f32[128,256]{1,0:T(8,...) custom-call(s32[1]{0:T(128)} %bitcast.core_ref, ...), custom_call_target="tpu_custom_call" | custom-call | flops 1 | bytes 1 | tf_op jit(solution)/shard_map/first_score_grad/pallas_call | solution.py:264
  28.2 0.0 collective-permute-done.13.got_ref
  28.2 0.0 collective-permute-done.14.got_last_ref
  28.2 0.1 merge.2
  28.3 0.5 %collective-permute-start.17 = (bf16[144,512]{1,0:T(8,128)(2,1)S(1)}, bf16[144,512]{1,0:T(8,128)(2,1)S(1)}, u32[]{:S(2)}, u32[]{:S(2)}) collective-permute-start(bf16[144,512]{1,0:T(8,128)(2,1)S(1)} %get-tuple-element.118), channel_id=1, source_target_pairs={{0,12},{1,13},{2,14},{3,15},{4,0},{5,1},{6,2},{7,3},{8,4},{9,5},{1... | collective-permute-start | bytes 442376 | tf_op jit(solution)/shard_map/ppermute | solution.py:203
  28.8 0.7 %collective-permute-start.18 = (bf16[144,512]{1,0:T(8,128)(2,1)S(1)}, bf16[144,512]{1,0:T(8,128)(2,1)S(1)}, u32[]{:S(2)}, u32[]{:S(2)}) collective-permute-start(bf16[144,512]{1,0:T(8,128)(2,1)S(1)} %get-tuple-element.119), channel_id=1, source_target_pairs={{0,14},{1,15},{2,0},{3,1},{4,2},{5,3},{6,4},{7,5},{8,6},{9,7},{10,... | collective-permute-start | bytes 442376 | tf_op jit(solution)/shard_map/ppermute | solution.py:203
  29.5 2.3 %second_score_grad.1 = (bf16[640,2048]{1,0:T(8,128)(2,1)S(1)}, bf16[128,2048]{1,0:T(8,128)(2,1)S(1)}, f32[128,512]{1,0:T(8,128)S(1)}, bf16[128,512]{1,0:T(8,128)...) custom-call(bf16[640,2048]{1,0:T(8,128)(2,1)S(1)} %get-tuple-element.86.e_ref, ...), custom_call_target="tpu_custom_call" | custom-call | flops 1 | bytes 1 | tf_op jit(solution)/shard_map/second_score_grad/pallas_call | solution.py:276
  31.8 0.1 collective-permute-start.15
  31.9 0.5 %collective-permute-start.16 = (bf16[128,512]{1,0:T(8,128)(2,1)S(1)}, bf16[128,512]{1,0:T(8,128)(2,1)S(1)}, u32[]{:S(2)}, u32[]{:S(2)}) collective-permute-start(bf16[128,512]{1,0:T(8,128)(2,1)S(1)} %get-tuple-element.113), channel_id=1, source_target_pairs={{0,1},{1,0},{2,3},{3,2},{4,5},{5,4},{6,7},{7,6},{8,9},{9,8},{10,11... | collective-permute-start | bytes 393224 | tf_op jit(solution)/shard_map/ppermute | solution.py:208
  32.4 0.8 %collective-permute-done.15.got_ref = bf16[128,512]{1,0:T(8,128)(2,1)S(1)} collective-permute-done((bf16[128,512]{1,0:T(8,128)(2,1)S(1)}, bf16[128,512]{1,0:T(8,128)(2,1)S(1)}, u32[]{:S(2)}, u32[]{:S(2)}) %collective-permute-start.15) | collective-permute-done | bytes 131104 | tf_op jit(solution)/shard_map/ppermute | solution.py:208
  33.2 0.2 collective-permute-done.16.got_last_ref
  33.4 0.1 merge.3
  33.5 0.5 %collective-permute-start.19 = (bf16[128,512]{1,0:T(8,128)(2,1)S(1)}, bf16[128,512]{1,0:T(8,128)(2,1)S(1)}, u32[]{:S(2)}, u32[]{:S(2)}) collective-permute-start(bf16[128,512]{1,0:T(8,128)(2,1)S(1)} %get-tuple-element.125), channel_id=1, source_target_pairs={{0,12},{1,13},{2,14},{3,15},{4,0},{5,1},{6,2},{7,3},{8,4},{9,5},{1... | collective-permute-start | bytes 393224 | tf_op jit(solution)/shard_map/ppermute | solution.py:203
  34.0 2.5 %collective-permute-start.20 = (bf16[128,512]{1,0:T(8,128)(2,1)S(1)}, bf16[128,512]{1,0:T(8,128)(2,1)S(1)}, u32[]{:S(2)}, u32[]{:S(2)}) collective-permute-start(bf16[128,512]{1,0:T(8,128)(2,1)S(1)} %get-tuple-element.126), channel_id=1, source_target_pairs={{0,14},{1,15},{2,0},{3,1},{4,2},{5,3},{6,4},{7,5},{8,6},{9,7},{10,... | collective-permute-start | bytes 393224 | tf_op jit(solution)/shard_map/ppermute | solution.py:203
  36.6 0.7 %add.12 = bf16[128,512]{1,0:T(8,128)(2,1)} custom-call(f32[128,512]{1,0:T(8,128)S(1)} %add.11.own_ref, bf16[144,512]{1,0:T(8,128)(2,1)S(1)} %collective-permute-done.18.part_ref), custom_call_target="tpu_custom_call" | custom-call | flops 1 | bytes 1 | tf_op jit(solution)/shard_map/add/pallas_call | solution.py:219
  37.3 3.6 %rows.1 = (bf16[128,4096]{1,0:T(8,128)(2,1)}, bf16[128,4096]{1,0:T(8,128)(2,1)}) custom-call(bf16[128,2048]{1,0:T(8,128)(2,1)S(1)} %get-tuple-element.85.c0, bf16[128,2048]{1,0:T(8,128)(2,1)S(1)} %get-tuple-element.106.c1, bf16[640,2048]{1,0:T(8,128)(2,1)S(1)} %get-tuple-element.120.ds0, bf16[640,2048]{1,0:T(8,128)(2,1)S(1)} %get-tuple-element.121.ds1, ...), custom_call_target="tpu_custom_call" | custom-call | flops 4294967296 | bytes 1 | tf_op jit(solution)/shard_map/rows/pallas_call | solution.py:283
  40.9 0.1 collective-permute-done.19.part_ref
  41.0 0.7 %add.14 = bf16[128,512]{1,0:T(8,128)(2,1)} custom-call(f32[128,512]{1,0:T(8,128)S(1)} %add.13.own_ref, bf16[128,512]{1,0:T(8,128)(2,1)S(1)} %collective-permute-done.20.part_ref), custom_call_target="tpu_custom_call" | custom-call | flops 1 | bytes 1 | tf_op jit(solution)/shard_map/add/pallas_call | solution.py:219
  (18 shorter events, 0.1 us)
Async XLA Ops:
  0.6 8.7 %collective-permute-start.1 = (s32[1,128]{1,0:T(1,128)}, s32[1,128]{1,0:T(1,128)S(1)}, u32[]{:S(2)}, u32[]{:S(2)}) collective-permute-start(s32[1,128]{1,0:T(1,128)} %bitcast.3), channel_id=1, source_target_pairs={{0,4},{1,5},{2,6},{3,7},{4,8},{5,9},{6,10},{7,11},{8,12},{9,13},{1... | collective-permute-start | bytes 1544 | tf_op jit(solution)/shard_map/ppermute | solution.py:203
  3.7 7.3 %collective-permute-start = (s32[1,128]{1,0:T(1,128)}, s32[1,128]{1,0:T(1,128)S(1)}, u32[]{:S(2)}, u32[]{:S(2)}) collective-permute-start(s32[1,128]{1,0:T(1,128)} %bitcast.4), channel_id=1, source_target_pairs={{0,2},{1,3},{2,4},{3,5},{4,6},{5,7},{6,8},{7,9},{8,10},{9,11},{10,... | collective-permute-start | bytes 1544 | tf_op jit(solution)/shard_map/ppermute | solution.py:203
  5.2 8.6 %collective-permute-start.5 = (bf16[128,512]{1,0:T(8,128)(2,1)}, bf16[128,512]{1,0:T(8,128)(2,1)S(1)}, u32[]{:S(2)}, u32[]{:S(2)}) collective-permute-start(bf16[128,512]{1,0:T(8,128)(2,1)} %k0.1), channel_id=1, source_target_pairs={{0,4},{1,5},{2,6},{3,7},{4,8},{5,9},{6,10},{7,11},{8,12},{9,13},{1... | collective-permute-start | bytes 393224 | tf_op jit(solution)/shard_map/ppermute | solution.py:203
  6.8 10.6 %collective-permute-start.3 = (bf16[128,512]{1,0:T(8,128)(2,1)}, bf16[128,512]{1,0:T(8,128)(2,1)S(1)}, u32[]{:S(2)}, u32[]{:S(2)}) collective-permute-start(bf16[128,512]{1,0:T(8,128)(2,1)} %k0.1), channel_id=1, source_target_pairs={{0,2},{1,3},{2,4},{3,5},{4,6},{5,7},{6,8},{7,9},{8,10},{9,11},{10,... | collective-permute-start | bytes 393224 | tf_op jit(solution)/shard_map/ppermute | solution.py:203
  9.2 12.3 %collective-permute-start.9 = (bf16[144,512]{1,0:T(8,128)(2,1)S(1)}, bf16[144,512]{1,0:T(8,128)(2,1)S(1)}, u32[]{:S(2)}, u32[]{:S(2)}) collective-permute-start(bf16[144,512]{1,0:T(8,128)(2,1)S(1)} %pad.4.v0), channel_id=1, source_target_pairs={{0,4},{1,5},{2,6},{3,7},{4,8},{5,9},{6,10},{7,11},{8,12},{9,13},{1... | collective-permute-start | bytes 442376 | tf_op jit(solution)/shard_map/ppermute | solution.py:203
  9.4 12.6 %collective-permute-start.8 = (bf16[144,512]{1,0:T(8,128)(2,1)S(1)}, bf16[144,512]{1,0:T(8,128)(2,1)S(1)}, u32[]{:S(2)}, u32[]{:S(2)}) collective-permute-start(bf16[144,512]{1,0:T(8,128)(2,1)S(1)} %pad.4.v0), channel_id=1, source_target_pairs={{0,2},{1,3},{2,4},{3,5},{4,6},{5,7},{6,8},{7,9},{8,10},{9,11},{10,... | collective-permute-start | bytes 442376 | tf_op jit(solution)/shard_map/ppermute | solution.py:203
  11.0 0.7 %copy-start.3 = (s32[128]{0:T(128)S(1)}, s32[128]{0:T(128)}, u32[]{:S(2)}) copy-start(s32[128]{0:T(128)} %param.10) | copy-start | bytes 1540
  11.7 1.2 %collective-permute-start.2 = (s32[8,128]{1,0:T(8,128)S(1)}, s32[8,128]{1,0:T(8,128)S(1)}, u32[]{:S(2)}, u32[]{:S(2)}) collective-permute-start(s32[8,128]{1,0:T(8,128)S(1)} %nodes.1.mine_ref), channel_id=1, source_target_pairs={{0,1},{1,0},{2,3},{3,2},{4,5},{5,4},{6,7},{7,6},{8,9},{9,8},{10,11... | collective-permute-start | bytes 12296 | tf_op jit(solution)/shard_map/ppermute | solution.py:208
  11.7 0.7 %copy-start.4 = (s32[84]{0:T(128)S(1)}, s32[84]{0:T(128)}, u32[]{:S(2)}) copy-start(s32[84]{0:T(128)} %param.11) | copy-start | bytes 1012
  12.4 0.9 %copy-start.2 = (bf16[128,512]{1,0:T(8,128)(2,1)S(1)}, bf16[128,512]{1,0:T(8,128)(2,1)}, u32[]{:S(2)}) copy-start(bf16[128,512]{1,0:T(8,128)(2,1)} %k0.1) | copy-start | bytes 393220
  12.4 6.4 %copy-start = (bf16[128,4096]{1,0:T(8,128)(2,1)S(1)}, bf16[128,4096]{1,0:T(8,128)(2,1)}, u32[]{:S(2)}) copy-start(bf16[128,4096]{1,0:T(8,128)(2,1)} %q_ref.7) | copy-start | bytes 3145732
  12.4 6.4 %copy-start.1 = (bf16[128,4096]{1,0:T(8,128)(2,1)S(1)}, bf16[128,4096]{1,0:T(8,128)(2,1)}, u32[]{:S(2)}) copy-start(bf16[128,4096]{1,0:T(8,128)(2,1)} %do_ref.3) | copy-start | bytes 3145732
  13.3 4.2 %collective-permute-start.6 = (bf16[128,512]{1,0:T(8,128)(2,1)S(1)}, bf16[128,512]{1,0:T(8,128)(2,1)S(1)}, u32[]{:S(2)}, u32[]{:S(2)}) collective-permute-start(bf16[128,512]{1,0:T(8,128)(2,1)S(1)} %copy-done.2), channel_id=1, source_target_pairs={{0,1},{1,0},{2,3},{3,2},{4,5},{5,4},{6,7},{7,6},{8,9},{9,8},{10,11... | collective-permute-start | bytes 393224 | tf_op jit(solution)/shard_map/ppermute | solution.py:208
  13.8 4.2 %collective-permute-start.7 = (bf16[128,512]{1,0:T(8,128)(2,1)S(1)}, bf16[128,512]{1,0:T(8,128)(2,1)S(1)}, u32[]{:S(2)}, u32[]{:S(2)}) collective-permute-start(bf16[128,512]{1,0:T(8,128)(2,1)S(1)} %collective-permute-done.5.k3), channel_id=1, source_target_pairs={{0,1},{1,0},{2,3},{3,2},{4,5},{5,4},{6,7},{7,6},{8,9},{9,8},{10,11... | collective-permute-start | bytes 393224 | tf_op jit(solution)/shard_map/ppermute | solution.py:208
  17.4 1.3 %collective-permute-start.4 = (bf16[128,512]{1,0:T(8,128)(2,1)S(1)}, bf16[128,512]{1,0:T(8,128)(2,1)S(1)}, u32[]{:S(2)}, u32[]{:S(2)}) collective-permute-start(bf16[128,512]{1,0:T(8,128)(2,1)S(1)} %collective-permute-done.3.k1), channel_id=1, source_target_pairs={{0,1},{1,0},{2,3},{3,2},{4,5},{5,4},{6,7},{7,6},{8,9},{9,8},{10,11... | collective-permute-start | bytes 393224 | tf_op jit(solution)/shard_map/ppermute | solution.py:208
  17.4 8.4 %collective-permute-start.11 = (bf16[144,512]{1,0:T(8,128)(2,1)S(1)}, bf16[144,512]{1,0:T(8,128)(2,1)S(1)}, u32[]{:S(2)}, u32[]{:S(2)}) collective-permute-start(bf16[144,512]{1,0:T(8,128)(2,1)S(1)} %pad.4.v0), channel_id=1, source_target_pairs={{0,1},{1,0},{2,3},{3,2},{4,5},{5,4},{6,7},{7,6},{8,9},{9,8},{10,11... | collective-permute-start | bytes 442376 | tf_op jit(solution)/shard_map/ppermute | solution.py:208
  22.0 3.9 %collective-permute-start.10 = (bf16[144,512]{1,0:T(8,128)(2,1)S(1)}, bf16[144,512]{1,0:T(8,128)(2,1)S(1)}, u32[]{:S(2)}, u32[]{:S(2)}) collective-permute-start(bf16[144,512]{1,0:T(8,128)(2,1)S(1)} %collective-permute-done.8.v1), channel_id=1, source_target_pairs={{0,1},{1,0},{2,3},{3,2},{4,5},{5,4},{6,7},{7,6},{8,9},{9,8},{10,11... | collective-permute-start | bytes 442376 | tf_op jit(solution)/shard_map/ppermute | solution.py:208
  22.0 3.9 %collective-permute-start.12 = (bf16[144,512]{1,0:T(8,128)(2,1)S(1)}, bf16[144,512]{1,0:T(8,128)(2,1)S(1)}, u32[]{:S(2)}, u32[]{:S(2)}) collective-permute-start(bf16[144,512]{1,0:T(8,128)(2,1)S(1)} %collective-permute-done.9.v3), channel_id=1, source_target_pairs={{0,1},{1,0},{2,3},{3,2},{4,5},{5,4},{6,7},{7,6},{8,9},{9,8},{10,11... | collective-permute-start | bytes 442376 | tf_op jit(solution)/shard_map/ppermute | solution.py:208
  25.3 2.9 %collective-permute-start.13 = (bf16[128,512]{1,0:T(8,128)(2,1)S(1)}, bf16[128,512]{1,0:T(8,128)(2,1)S(1)}, u32[]{:S(2)}, u32[]{:S(2)}) collective-permute-start(bf16[128,512]{1,0:T(8,128)(2,1)S(1)} %get-tuple-element.94), channel_id=1, source_target_pairs={{0,1},{1,0},{2,3},{3,2},{4,5},{5,4},{6,7},{7,6},{8,9},{9,8},{10,11... | collective-permute-start | bytes 393224 | tf_op jit(solution)/shard_map/ppermute | solution.py:208
  25.4 2.8 %collective-permute-start.14 = (bf16[128,512]{1,0:T(8,128)(2,1)S(1)}, bf16[128,512]{1,0:T(8,128)(2,1)S(1)}, u32[]{:S(2)}, u32[]{:S(2)}) collective-permute-start(bf16[128,512]{1,0:T(8,128)(2,1)S(1)} %get-tuple-element.95), channel_id=1, source_target_pairs={{0,1},{1,0},{2,3},{3,2},{4,5},{5,4},{6,7},{7,6},{8,9},{9,8},{10,11... | collective-permute-start | bytes 393224 | tf_op jit(solution)/shard_map/ppermute | solution.py:208
  28.3 8.3 %collective-permute-start.17 = (bf16[144,512]{1,0:T(8,128)(2,1)S(1)}, bf16[144,512]{1,0:T(8,128)(2,1)S(1)}, u32[]{:S(2)}, u32[]{:S(2)}) collective-permute-start(bf16[144,512]{1,0:T(8,128)(2,1)S(1)} %get-tuple-element.118), channel_id=1, source_target_pairs={{0,12},{1,13},{2,14},{3,15},{4,0},{5,1},{6,2},{7,3},{8,4},{9,5},{1... | collective-permute-start | bytes 442376 | tf_op jit(solution)/shard_map/ppermute | solution.py:203
  28.8 7.8 %collective-permute-start.18 = (bf16[144,512]{1,0:T(8,128)(2,1)S(1)}, bf16[144,512]{1,0:T(8,128)(2,1)S(1)}, u32[]{:S(2)}, u32[]{:S(2)}) collective-permute-start(bf16[144,512]{1,0:T(8,128)(2,1)S(1)} %get-tuple-element.119), channel_id=1, source_target_pairs={{0,14},{1,15},{2,0},{3,1},{4,2},{5,3},{6,4},{7,5},{8,6},{9,7},{10,... | collective-permute-start | bytes 442376 | tf_op jit(solution)/shard_map/ppermute | solution.py:203
  31.8 1.4 %collective-permute-start.15 = (bf16[128,512]{1,0:T(8,128)(2,1)S(1)}, bf16[128,512]{1,0:T(8,128)(2,1)S(1)}, u32[]{:S(2)}, u32[]{:S(2)}) collective-permute-start(bf16[128,512]{1,0:T(8,128)(2,1)S(1)} %get-tuple-element.112), channel_id=1, source_target_pairs={{0,1},{1,0},{2,3},{3,2},{4,5},{5,4},{6,7},{7,6},{8,9},{9,8},{10,11... | collective-permute-start | bytes 393224 | tf_op jit(solution)/shard_map/ppermute | solution.py:208
  31.9 1.5 %collective-permute-start.16 = (bf16[128,512]{1,0:T(8,128)(2,1)S(1)}, bf16[128,512]{1,0:T(8,128)(2,1)S(1)}, u32[]{:S(2)}, u32[]{:S(2)}) collective-permute-start(bf16[128,512]{1,0:T(8,128)(2,1)S(1)} %get-tuple-element.113), channel_id=1, source_target_pairs={{0,1},{1,0},{2,3},{3,2},{4,5},{5,4},{6,7},{7,6},{8,9},{9,8},{10,11... | collective-permute-start | bytes 393224 | tf_op jit(solution)/shard_map/ppermute | solution.py:208
  33.5 7.5 %collective-permute-start.19 = (bf16[128,512]{1,0:T(8,128)(2,1)S(1)}, bf16[128,512]{1,0:T(8,128)(2,1)S(1)}, u32[]{:S(2)}, u32[]{:S(2)}) collective-permute-start(bf16[128,512]{1,0:T(8,128)(2,1)S(1)} %get-tuple-element.125), channel_id=1, source_target_pairs={{0,12},{1,13},{2,14},{3,15},{4,0},{5,1},{6,2},{7,3},{8,4},{9,5},{1... | collective-permute-start | bytes 393224 | tf_op jit(solution)/shard_map/ppermute | solution.py:203
  34.0 7.0 %collective-permute-start.20 = (bf16[128,512]{1,0:T(8,128)(2,1)S(1)}, bf16[128,512]{1,0:T(8,128)(2,1)S(1)}, u32[]{:S(2)}, u32[]{:S(2)}) collective-permute-start(bf16[128,512]{1,0:T(8,128)(2,1)S(1)} %get-tuple-element.126), channel_id=1, source_target_pairs={{0,14},{1,15},{2,0},{3,1},{4,2},{5,3},{6,4},{7,5},{8,6},{9,7},{10,... | collective-permute-start | bytes 393224 | tf_op jit(solution)/shard_map/ppermute | solution.py:203

commit v5 on v4

--- a/solution.py
+++ b/solution.py
@@ -193,6 +193,10 @@
             out[t:, :] = jnp.zeros((out.shape[0] - t, out.shape[1]), bf16)
 
 
+def copy_kernel(in_ref, out_ref):
+    out_ref[...] = in_ref[...]
+
+
 def add_kernel(own_ref, part_ref, out_ref):
     t = own_ref.shape[0]
     out_ref[...] = (own_ref[...] + part_ref[:t, :].astype(f32)).astype(out_ref.dtype)
@@ -213,6 +217,10 @@
     return call(
         merge_kernel, "merge", [SMEM] + [VMEM] * 5, [VMEM] * 3, [S(own.shape, f32), sent, sent], cost=1, limit=SMALL
     )(core, own, near, far, got, got_last)
+
+
+def passed(value, cost=1 << 24):
+    return call(copy_kernel, "passed", [VMEM], VMEM, S(value.shape, value.dtype), cost=cost, limit=SMALL)(value)
 
 
 def add(own, part, dtype, cost):
@@ -237,7 +245,7 @@
         node, near_node, far_node
     )
     own, _ = lax.optimization_barrier((keys, line))
-    ks = (keys, near, swap(near), far, swap(own), swap(far))
+    ks = (keys, near, passed(swap(near)), far, swap(own), swap(far))
     values = jnp.pad(values, ((0, PAD_ROWS), (0, 0)))
     far, near = ahead(values, 4), ahead(values, 2)
     parts = [S((t, width), f32)] + [S((t, width), bf16)] * 4
@@ -253,7 +261,7 @@
         [VMEM] * 10,
         [square, scaled, inv, blocks, S((5 * t, t), f32)] + half_parts,
         cost=1,
-    )(core, line, queries, output_gradient, mine, swap(mine), *ks)
+    )(core, line, queries, output_gradient, mine, passed(swap(mine), 1 << 30), *ks)
     dv[0], near, far = lax.optimization_barrier((dv[0], near, far))
     near_other, sibling, far_other = swap(near), swap(values), swap(far)
     e1, scaled1, inv1, *dv = call(

time: 42.3 us -> 41.5 us (0.981)
  starting transfers between devices: 16.4 us -> 15.9 us
    ppermute x10, starting transfers between devices: 13.8 us -> 13.2 us  [ahead(): return lax.ppermute(value, 'seq', [(i, (i + by) % n) for i in range(n)])]
  transfers between devices with their start and end apart: 21 -> 21, of which waited for: 7 -> 10; matrix products, arithmetic and copies ran while one was open for 2% -> 2% of each run, Pallas kernels for 36% -> 36%
where the time goes in v5:
time: 41.5 us; the launch traced here: 41.2 us
  starting transfers between devices  15.9 us (38%)
  Pallas kernels  15.6 us (38%)
  waiting for transfers between devices  6.07 us (15%)
  local copies, waits for them, and re-layouts  2.78 us (7%)
  between operations  0.78 us (2%)
    ppermute x10, starting transfers between devices, ahead(): return lax.ppermute(value, 'seq', [(i, (i + by) % n) for i in range(n)])  13.2 us
    ppermute x10, waiting for transfers between devices, ahead(): return lax.ppermute(value, 'seq', [(i, (i + by) % n) for i in range(n)])  4.21 us
    pallas_call x1, Pallas kernels, on_device(): call(rows_kernel, 'rows', [VMEM] * 5, [VMEM] * 2, [S(queries.shape, bf16)...  3.59 us
    pallas_call x1, Pallas kernels, on_device(): call(second_probs_kernel, 'second_probs', [VMEM] * 9, [VMEM] * 8, [square...  2.78 us
    pallas_call x1, Pallas kernels, on_device(): call(first_probs_kernel, 'first_probs', [SMEM] + [VMEM] * 11, [VMEM] * 10...  2.76 us
    ppermute x11, starting transfers between devices, swap(): return lax.ppermute(value, 'seq', [(i, i ^ 1) for i in range(n)])  2.73 us
    pallas_call x1, Pallas kernels, on_device(): call(first_score_grad_kernel, 'first_score_grad', [SMEM] + [VMEM] * 10, [...  2.27 us
    pallas_call x1, Pallas kernels, on_device(): call(second_score_grad_kernel, 'second_score_grad', [VMEM] * 10, [VMEM] *...  2.27 us
  transfers between devices with their start and end apart: 21, of which 10 were waited for; matrix products, arithmetic and copies ran while one was open for 2% of the time, Pallas kernels for 36%

profile of v5, /device:TPU:0, one launch (start us, length us, event | category | flops | bytes accessed | tf_op | source)
XLA Modules:
  0.0 41.2 jit_solution(884667669482809247)
XLA Ops:
  0.6 3.0 %collective-permute-start.3 = (bf16[128,512]{1,0:T(8,128)(2,1)}, bf16[128,512]{1,0:T(8,128)(2,1)S(1)}, u32[]{:S(2)}, u32[]{:S(2)}) collective-permute-start(bf16[128,512]{1,0:T(8,128)(2,1)} %k0.1), channel_id=1, source_target_pairs={{0,2},{1,3},{2,4},{3,5},{4,6},{5,7},{6,8},{7,9},{8,10},{9,11},{10,... | collective-permute-start | bytes 393224 | tf_op jit(solution)/shard_map/ppermute | solution.py:207
  3.6 1.6 %collective-permute-start.1 = (s32[1,128]{1,0:T(1,128)}, s32[1,128]{1,0:T(1,128)S(1)}, u32[]{:S(2)}, u32[]{:S(2)}) collective-permute-start(s32[1,128]{1,0:T(1,128)} %bitcast.3), channel_id=1, source_target_pairs={{0,4},{1,5},{2,6},{3,7},{4,8},{5,9},{6,10},{7,11},{8,12},{9,13},{1... | collective-permute-start | bytes 1544 | tf_op jit(solution)/shard_map/ppermute | solution.py:207
  5.2 1.5 %collective-permute-start = (s32[1,128]{1,0:T(1,128)}, s32[1,128]{1,0:T(1,128)S(1)}, u32[]{:S(2)}, u32[]{:S(2)}) collective-permute-start(s32[1,128]{1,0:T(1,128)} %bitcast.4), channel_id=1, source_target_pairs={{0,2},{1,3},{2,4},{3,5},{4,6},{5,7},{6,8},{7,9},{8,10},{9,11},{10,... | collective-permute-start | bytes 1544 | tf_op jit(solution)/shard_map/ppermute | solution.py:207
  6.7 1.6 %collective-permute-start.5 = (bf16[128,512]{1,0:T(8,128)(2,1)}, bf16[128,512]{1,0:T(8,128)(2,1)S(1)}, u32[]{:S(2)}, u32[]{:S(2)}) collective-permute-start(bf16[128,512]{1,0:T(8,128)(2,1)} %k0.1), channel_id=1, source_target_pairs={{0,4},{1,5},{2,6},{3,7},{4,8},{5,9},{6,10},{7,11},{8,12},{9,13},{1... | collective-permute-start | bytes 393224 | tf_op jit(solution)/shard_map/ppermute | solution.py:207
  8.3 0.9 %pad.4.v0 = bf16[144,512]{1,0:T(8,128)(2,1)S(1)} pad(bf16[128,512]{1,0:T(8,128)(2,1)} %param.8, bf16[]{:T(256)} %constant.19.clone.1), padding=0_16x0_0 | pad | bytes 278530 | tf_op jit(solution)/shard_map/jit(_pad)/pad | solution.py:249
  9.2 0.2 collective-permute-start.9
  9.4 1.6 %collective-permute-start.8 = (bf16[144,512]{1,0:T(8,128)(2,1)S(1)}, bf16[144,512]{1,0:T(8,128)(2,1)S(1)}, u32[]{:S(2)}, u32[]{:S(2)}) collective-permute-start(bf16[144,512]{1,0:T(8,128)(2,1)S(1)} %pad.4.v0), channel_id=1, source_target_pairs={{0,2},{1,3},{2,4},{3,5},{4,6},{5,7},{6,8},{7,9},{8,10},{9,11},{10,... | collective-permute-start | bytes 442376 | tf_op jit(solution)/shard_map/ppermute | solution.py:207
  11.0 0.6 %collective-permute-done.near_ref = s32[1,128]{1,0:T(1,128)S(1)} collective-permute-done((s32[1,128]{1,0:T(1,128)}, s32[1,128]{1,0:T(1,128)S(1)}, u32[]{:S(2)}, u32[]{:S(2)}) %collective-permute-start) | collective-permute-done | bytes 544 | tf_op jit(solution)/shard_map/ppermute | solution.py:207
  11.6 0.7 %copy-done.3 = s32[128]{0:T(128)S(1)} copy-done((s32[128]{0:T(128)S(1)}, s32[128]{0:T(128)}, u32[]{:S(2)}) %copy-start.3) | copy-done | bytes 536
  12.3 0.0 collective-permute-start.2
  12.3 0.5 %collective-permute-start.4 = (bf16[128,512]{1,0:T(8,128)(2,1)S(1)}, bf16[128,512]{1,0:T(8,128)(2,1)S(1)}, u32[]{:S(2)}, u32[]{:S(2)}) collective-permute-start(bf16[128,512]{1,0:T(8,128)(2,1)S(1)} %collective-permute-done.3.k1), channel_id=1, source_target_pairs={{0,1},{1,0},{2,3},{3,2},{4,5},{5,4},{6,7},{7,6},{8,9},{9,8},{10,11... | collective-permute-start | bytes 393224 | tf_op jit(solution)/shard_map/ppermute | solution.py:212
  12.8 0.7 %copy-done.4 = s32[84]{0:T(128)S(1)} copy-done((s32[84]{0:T(128)S(1)}, s32[84]{0:T(128)}, u32[]{:S(2)}) %copy-start.4) | copy-done | bytes 360
  13.4 0.3 lineage.1.line_ref
  13.8 0.0 copy-start
  13.8 0.0 copy-start.1
  13.8 0.5 %copy-done.2 = bf16[128,512]{1,0:T(8,128)(2,1)S(1)} copy-done((bf16[128,512]{1,0:T(8,128)(2,1)S(1)}, bf16[128,512]{1,0:T(8,128)(2,1)}, u32[]{:S(2)}) %copy-start.2) | copy-done | bytes 131096
  14.3 0.1 collective-permute-start.6
  14.4 0.6 %collective-permute-done.5.k3 = bf16[128,512]{1,0:T(8,128)(2,1)S(1)} collective-permute-done((bf16[128,512]{1,0:T(8,128)(2,1)}, bf16[128,512]{1,0:T(8,128)(2,1)S(1)}, u32[]{:S(2)}, u32[]{:S(2)}) %collective-permute-start.5) | collective-permute-done | bytes 131104 | tf_op jit(solution)/shard_map/ppermute | solution.py:207
  15.0 0.0 collective-permute-start.7
  15.1 0.0 collective-permute-done.4.in_ref
  15.1 0.5 %collective-permute-start.11 = (bf16[144,512]{1,0:T(8,128)(2,1)S(1)}, bf16[144,512]{1,0:T(8,128)(2,1)S(1)}, u32[]{:S(2)}, u32[]{:S(2)}) collective-permute-start(bf16[144,512]{1,0:T(8,128)(2,1)S(1)} %pad.4.v0), channel_id=1, source_target_pairs={{0,1},{1,0},{2,3},{3,2},{4,5},{5,4},{6,7},{7,6},{8,9},{9,8},{10,11... | collective-permute-start | bytes 442376 | tf_op jit(solution)/shard_map/ppermute | solution.py:212
  15.6 0.1 collective-permute-done.6.k4
  15.7 0.7 %collective-permute-done.7.k5 = bf16[128,512]{1,0:T(8,128)(2,1)S(1)} collective-permute-done((bf16[128,512]{1,0:T(8,128)(2,1)S(1)}, bf16[128,512]{1,0:T(8,128)(2,1)S(1)}, u32[]{:S(2)}, u32[]{:S(2)}) %collective-permute-start.7) | collective-permute-done | bytes 131104 | tf_op jit(solution)/shard_map/ppermute | solution.py:212
  16.4 2.8 %first_probs.1 = (bf16[640,2048]{1,0:T(8,128)(2,1)S(1)}, bf16[128,2048]{1,0:T(8,128)(2,1)S(1)}, f32[16,128]{1,0:T(8,128)S(1)}, bf16[640,512]{1,0:T(8,128)(2,1)S(...) custom-call(s32[1]{0:T(128)} %bitcast.core_ref, ...), custom_call_target="tpu_custom_call" | custom-call | flops 1 | bytes 1 | tf_op jit(solution)/shard_map/first_probs/pallas_call | solution.py:257
  19.2 1.8 %collective-permute-done.8.v1 = bf16[144,512]{1,0:T(8,128)(2,1)S(1)} collective-permute-done((bf16[144,512]{1,0:T(8,128)(2,1)S(1)}, bf16[144,512]{1,0:T(8,128)(2,1)S(1)}, u32[]{:S(2)}, u32[]{:S(2)}) %collective-permute-start.8) | collective-permute-done | bytes 147488 | tf_op jit(solution)/shard_map/ppermute | solution.py:207
  21.0 0.5 %collective-permute-start.12 = (bf16[144,512]{1,0:T(8,128)(2,1)S(1)}, bf16[144,512]{1,0:T(8,128)(2,1)S(1)}, u32[]{:S(2)}, u32[]{:S(2)}) collective-permute-start(bf16[144,512]{1,0:T(8,128)(2,1)S(1)} %collective-permute-done.9.v3), channel_id=1, source_target_pairs={{0,1},{1,0},{2,3},{3,2},{4,5},{5,4},{6,7},{7,6},{8,9},{9,8},{10,11... | collective-permute-start | bytes 442376 | tf_op jit(solution)/shard_map/ppermute | solution.py:212
  21.5 2.8 %second_probs.1 = (bf16[640,2048]{1,0:T(8,128)(2,1)S(1)}, bf16[128,2048]{1,0:T(8,128)(2,1)S(1)}, f32[16,128]{1,0:T(8,128)S(1)}, f32[128,512]{1,0:T(8,128)S(1)}, ...) custom-call(bf16[128,4096]{1,0:T(8,128)(2,1)S(1)} %copy-done, ...), custom_call_target="tpu_custom_call" | custom-call | flops 1 | bytes 1 | tf_op jit(solution)/shard_map/second_probs/pallas_call | solution.py:267
  24.3 0.1 collective-permute-start.13
  24.4 0.5 %collective-permute-start.14 = (bf16[128,512]{1,0:T(8,128)(2,1)S(1)}, bf16[128,512]{1,0:T(8,128)(2,1)S(1)}, u32[]{:S(2)}, u32[]{:S(2)}) collective-permute-start(bf16[128,512]{1,0:T(8,128)(2,1)S(1)} %get-tuple-element.95), channel_id=1, source_target_pairs={{0,1},{1,0},{2,3},{3,2},{4,5},{5,4},{6,7},{7,6},{8,9},{9,8},{10,11... | collective-permute-start | bytes 393224 | tf_op jit(solution)/shard_map/ppermute | solution.py:212
  24.9 0.0 collective-permute-done.11.v4
  24.9 2.3 %first_score_grad.1 = (bf16[640,2048]{1,0:T(8,128)(2,1)S(1)}, bf16[128,2048]{1,0:T(8,128)(2,1)S(1)}, bf16[640,512]{1,0:T(8,128)(2,1)S(1)}, f32[128,256]{1,0:T(8,...) custom-call(s32[1]{0:T(128)} %bitcast.core_ref, ...), custom_call_target="tpu_custom_call" | custom-call | flops 1 | bytes 1 | tf_op jit(solution)/shard_map/first_score_grad/pallas_call | solution.py:272
  27.2 0.1 merge.2
  27.3 0.8 %collective-permute-start.17 = (bf16[144,512]{1,0:T(8,128)(2,1)S(1)}, bf16[144,512]{1,0:T(8,128)(2,1)S(1)}, u32[]{:S(2)}, u32[]{:S(2)}) collective-permute-start(bf16[144,512]{1,0:T(8,128)(2,1)S(1)} %get-tuple-element.118), channel_id=1, source_target_pairs={{0,12},{1,13},{2,14},{3,15},{4,0},{5,1},{6,2},{7,3},{8,4},{9,5},{1... | collective-permute-start | bytes 442376 | tf_op jit(solution)/shard_map/ppermute | solution.py:207
  28.1 1.4 %collective-permute-start.18 = (bf16[144,512]{1,0:T(8,128)(2,1)S(1)}, bf16[144,512]{1,0:T(8,128)(2,1)S(1)}, u32[]{:S(2)}, u32[]{:S(2)}) collective-permute-start(bf16[144,512]{1,0:T(8,128)(2,1)S(1)} %get-tuple-element.119), channel_id=1, source_target_pairs={{0,14},{1,15},{2,0},{3,1},{4,2},{5,3},{6,4},{7,5},{8,6},{9,7},{10,... | collective-permute-start | bytes 442376 | tf_op jit(solution)/shard_map/ppermute | solution.py:207
  29.5 2.3 %second_score_grad.1 = (bf16[640,2048]{1,0:T(8,128)(2,1)S(1)}, bf16[128,2048]{1,0:T(8,128)(2,1)S(1)}, f32[128,512]{1,0:T(8,128)S(1)}, bf16[128,512]{1,0:T(8,128)...) custom-call(bf16[640,2048]{1,0:T(8,128)(2,1)S(1)} %get-tuple-element.86.e_ref, ...), custom_call_target="tpu_custom_call" | custom-call | flops 1 | bytes 1 | tf_op jit(solution)/shard_map/second_score_grad/pallas_call | solution.py:284
  31.8 0.1 collective-permute-start.15
  31.9 0.5 %collective-permute-start.16 = (bf16[128,512]{1,0:T(8,128)(2,1)S(1)}, bf16[128,512]{1,0:T(8,128)(2,1)S(1)}, u32[]{:S(2)}, u32[]{:S(2)}) collective-permute-start(bf16[128,512]{1,0:T(8,128)(2,1)S(1)} %get-tuple-element.113), channel_id=1, source_target_pairs={{0,1},{1,0},{2,3},{3,2},{4,5},{5,4},{6,7},{7,6},{8,9},{9,8},{10,11... | collective-permute-start | bytes 393224 | tf_op jit(solution)/shard_map/ppermute | solution.py:212
  32.4 0.8 %collective-permute-done.15.got_ref = bf16[128,512]{1,0:T(8,128)(2,1)S(1)} collective-permute-done((bf16[128,512]{1,0:T(8,128)(2,1)S(1)}, bf16[128,512]{1,0:T(8,128)(2,1)S(1)}, u32[]{:S(2)}, u32[]{:S(2)}) %collective-permute-start.15) | collective-permute-done | bytes 131104 | tf_op jit(solution)/shard_map/ppermute | solution.py:212
  33.2 0.2 collective-permute-done.16.got_last_ref
  33.4 0.1 merge.3
  33.5 0.5 %collective-permute-start.19 = (bf16[128,512]{1,0:T(8,128)(2,1)S(1)}, bf16[128,512]{1,0:T(8,128)(2,1)S(1)}, u32[]{:S(2)}, u32[]{:S(2)}) collective-permute-start(bf16[128,512]{1,0:T(8,128)(2,1)S(1)} %get-tuple-element.125), channel_id=1, source_target_pairs={{0,12},{1,13},{2,14},{3,15},{4,0},{5,1},{6,2},{7,3},{8,4},{9,5},{1... | collective-permute-start | bytes 393224 | tf_op jit(solution)/shard_map/ppermute | solution.py:207
  34.0 1.0 %collective-permute-start.20 = (bf16[128,512]{1,0:T(8,128)(2,1)S(1)}, bf16[128,512]{1,0:T(8,128)(2,1)S(1)}, u32[]{:S(2)}, u32[]{:S(2)}) collective-permute-start(bf16[128,512]{1,0:T(8,128)(2,1)S(1)} %get-tuple-element.126), channel_id=1, source_target_pairs={{0,14},{1,15},{2,0},{3,1},{4,2},{5,3},{6,4},{7,5},{8,6},{9,7},{10,... | collective-permute-start | bytes 393224 | tf_op jit(solution)/shard_map/ppermute | solution.py:207
  35.0 0.2 collective-permute-done.18.part_ref
  35.2 0.7 %add.12 = bf16[128,512]{1,0:T(8,128)(2,1)} custom-call(f32[128,512]{1,0:T(8,128)S(1)} %add.11.own_ref, bf16[144,512]{1,0:T(8,128)(2,1)S(1)} %collective-permute-done.18.part_ref), custom_call_target="tpu_custom_call" | custom-call | flops 1 | bytes 1 | tf_op jit(solution)/shard_map/add/pallas_call | solution.py:227
  35.9 3.6 %rows.1 = (bf16[128,4096]{1,0:T(8,128)(2,1)}, bf16[128,4096]{1,0:T(8,128)(2,1)}) custom-call(bf16[128,2048]{1,0:T(8,128)(2,1)S(1)} %get-tuple-element.85.c0, bf16[128,2048]{1,0:T(8,128)(2,1)S(1)} %get-tuple-element.106.c1, bf16[640,2048]{1,0:T(8,128)(2,1)S(1)} %get-tuple-element.120.ds0, bf16[640,2048]{1,0:T(8,128)(2,1)S(1)} %get-tuple-element.121.ds1, ...), custom_call_target="tpu_custom_call" | custom-call | flops 4294967296 | bytes 1 | tf_op jit(solution)/shard_map/rows/pallas_call | solution.py:291
  39.5 0.4 collective-permute-done.19.part_ref
  39.9 0.6 %collective-permute-done.20.part_ref = bf16[128,512]{1,0:T(8,128)(2,1)S(1)} collective-permute-done((bf16[128,512]{1,0:T(8,128)(2,1)S(1)}, bf16[128,512]{1,0:T(8,128)(2,1)S(1)}, u32[]{:S(2)}, u32[]{:S(2)}) %collective-permute-start.20) | collective-permute-done | bytes 131104 | tf_op jit(solution)/shard_map/ppermute | solution.py:207
  40.5 0.7 %add.14 = bf16[128,512]{1,0:T(8,128)(2,1)} custom-call(f32[128,512]{1,0:T(8,128)S(1)} %add.13.own_ref, bf16[128,512]{1,0:T(8,128)(2,1)S(1)} %collective-permute-done.20.part_ref), custom_call_target="tpu_custom_call" | custom-call | flops 1 | bytes 1 | tf_op jit(solution)/shard_map/add/pallas_call | solution.py:227
  (20 shorter events, 0.1 us)
Async XLA Ops:
  0.6 11.6 %collective-permute-start.3 = (bf16[128,512]{1,0:T(8,128)(2,1)}, bf16[128,512]{1,0:T(8,128)(2,1)S(1)}, u32[]{:S(2)}, u32[]{:S(2)}) collective-permute-start(bf16[128,512]{1,0:T(8,128)(2,1)} %k0.1), channel_id=1, source_target_pairs={{0,2},{1,3},{2,4},{3,5},{4,6},{5,7},{6,8},{7,9},{8,10},{9,11},{10,... | collective-permute-start | bytes 393224 | tf_op jit(solution)/shard_map/ppermute | solution.py:207
  3.6 5.8 %collective-permute-start.1 = (s32[1,128]{1,0:T(1,128)}, s32[1,128]{1,0:T(1,128)S(1)}, u32[]{:S(2)}, u32[]{:S(2)}) collective-permute-start(s32[1,128]{1,0:T(1,128)} %bitcast.3), channel_id=1, source_target_pairs={{0,4},{1,5},{2,6},{3,7},{4,8},{5,9},{6,10},{7,11},{8,12},{9,13},{1... | collective-permute-start | bytes 1544 | tf_op jit(solution)/shard_map/ppermute | solution.py:207
  5.2 6.4 %collective-permute-start = (s32[1,128]{1,0:T(1,128)}, s32[1,128]{1,0:T(1,128)S(1)}, u32[]{:S(2)}, u32[]{:S(2)}) collective-permute-start(s32[1,128]{1,0:T(1,128)} %bitcast.4), channel_id=1, source_target_pairs={{0,2},{1,3},{2,4},{3,5},{4,6},{5,7},{6,8},{7,9},{8,10},{9,11},{10,... | collective-permute-start | bytes 1544 | tf_op jit(solution)/shard_map/ppermute | solution.py:207
  6.7 8.3 %collective-permute-start.5 = (bf16[128,512]{1,0:T(8,128)(2,1)}, bf16[128,512]{1,0:T(8,128)(2,1)S(1)}, u32[]{:S(2)}, u32[]{:S(2)}) collective-permute-start(bf16[128,512]{1,0:T(8,128)(2,1)} %k0.1), channel_id=1, source_target_pairs={{0,4},{1,5},{2,6},{3,7},{4,8},{5,9},{6,10},{7,11},{8,12},{9,13},{1... | collective-permute-start | bytes 393224 | tf_op jit(solution)/shard_map/ppermute | solution.py:207
  9.2 9.9 %collective-permute-start.9 = (bf16[144,512]{1,0:T(8,128)(2,1)S(1)}, bf16[144,512]{1,0:T(8,128)(2,1)S(1)}, u32[]{:S(2)}, u32[]{:S(2)}) collective-permute-start(bf16[144,512]{1,0:T(8,128)(2,1)S(1)} %pad.4.v0), channel_id=1, source_target_pairs={{0,4},{1,5},{2,6},{3,7},{4,8},{5,9},{6,10},{7,11},{8,12},{9,13},{1... | collective-permute-start | bytes 442376 | tf_op jit(solution)/shard_map/ppermute | solution.py:207
  9.4 11.6 %collective-permute-start.8 = (bf16[144,512]{1,0:T(8,128)(2,1)S(1)}, bf16[144,512]{1,0:T(8,128)(2,1)S(1)}, u32[]{:S(2)}, u32[]{:S(2)}) collective-permute-start(bf16[144,512]{1,0:T(8,128)(2,1)S(1)} %pad.4.v0), channel_id=1, source_target_pairs={{0,2},{1,3},{2,4},{3,5},{4,6},{5,7},{6,8},{7,9},{8,10},{9,11},{10,... | collective-permute-start | bytes 442376 | tf_op jit(solution)/shard_map/ppermute | solution.py:207
  11.6 0.7 %copy-start.3 = (s32[128]{0:T(128)S(1)}, s32[128]{0:T(128)}, u32[]{:S(2)}) copy-start(s32[128]{0:T(128)} %param.10) | copy-start | bytes 1540
  12.3 1.5 %collective-permute-start.2 = (s32[8,128]{1,0:T(8,128)S(1)}, s32[8,128]{1,0:T(8,128)S(1)}, u32[]{:S(2)}, u32[]{:S(2)}) collective-permute-start(s32[8,128]{1,0:T(8,128)S(1)} %nodes.1.mine_ref), channel_id=1, source_target_pairs={{0,1},{1,0},{2,3},{3,2},{4,5},{5,4},{6,7},{7,6},{8,9},{9,8},{10,11... | collective-permute-start | bytes 12296 | tf_op jit(solution)/shard_map/ppermute | solution.py:212
  12.3 2.8 %collective-permute-start.4 = (bf16[128,512]{1,0:T(8,128)(2,1)S(1)}, bf16[128,512]{1,0:T(8,128)(2,1)S(1)}, u32[]{:S(2)}, u32[]{:S(2)}) collective-permute-start(bf16[128,512]{1,0:T(8,128)(2,1)S(1)} %collective-permute-done.3.k1), channel_id=1, source_target_pairs={{0,1},{1,0},{2,3},{3,2},{4,5},{5,4},{6,7},{7,6},{8,9},{9,8},{10,11... | collective-permute-start | bytes 393224 | tf_op jit(solution)/shard_map/ppermute | solution.py:212
  12.8 0.7 %copy-start.4 = (s32[84]{0:T(128)S(1)}, s32[84]{0:T(128)}, u32[]{:S(2)}) copy-start(s32[84]{0:T(128)} %param.11) | copy-start | bytes 1012
  13.4 0.9 %copy-start.2 = (bf16[128,512]{1,0:T(8,128)(2,1)S(1)}, bf16[128,512]{1,0:T(8,128)(2,1)}, u32[]{:S(2)}) copy-start(bf16[128,512]{1,0:T(8,128)(2,1)} %k0.1) | copy-start | bytes 393220
  13.8 2.6 %copy-start = (bf16[128,4096]{1,0:T(8,128)(2,1)S(1)}, bf16[128,4096]{1,0:T(8,128)(2,1)}, u32[]{:S(2)}) copy-start(bf16[128,4096]{1,0:T(8,128)(2,1)} %q_ref.7) | copy-start | bytes 3145732
  13.8 2.6 %copy-start.1 = (bf16[128,4096]{1,0:T(8,128)(2,1)S(1)}, bf16[128,4096]{1,0:T(8,128)(2,1)}, u32[]{:S(2)}) copy-start(bf16[128,4096]{1,0:T(8,128)(2,1)} %do_ref.3) | copy-start | bytes 3145732
  14.3 1.3 %collective-permute-start.6 = (bf16[128,512]{1,0:T(8,128)(2,1)S(1)}, bf16[128,512]{1,0:T(8,128)(2,1)S(1)}, u32[]{:S(2)}, u32[]{:S(2)}) collective-permute-start(bf16[128,512]{1,0:T(8,128)(2,1)S(1)} %copy-done.2), channel_id=1, source_target_pairs={{0,1},{1,0},{2,3},{3,2},{4,5},{5,4},{6,7},{7,6},{8,9},{9,8},{10,11... | collective-permute-start | bytes 393224 | tf_op jit(solution)/shard_map/ppermute | solution.py:212
  15.0 1.3 %collective-permute-start.7 = (bf16[128,512]{1,0:T(8,128)(2,1)S(1)}, bf16[128,512]{1,0:T(8,128)(2,1)S(1)}, u32[]{:S(2)}, u32[]{:S(2)}) collective-permute-start(bf16[128,512]{1,0:T(8,128)(2,1)S(1)} %collective-permute-done.5.k3), channel_id=1, source_target_pairs={{0,1},{1,0},{2,3},{3,2},{4,5},{5,4},{6,7},{7,6},{8,9},{9,8},{10,11... | collective-permute-start | bytes 393224 | tf_op jit(solution)/shard_map/ppermute | solution.py:212
  15.1 9.8 %collective-permute-start.11 = (bf16[144,512]{1,0:T(8,128)(2,1)S(1)}, bf16[144,512]{1,0:T(8,128)(2,1)S(1)}, u32[]{:S(2)}, u32[]{:S(2)}) collective-permute-start(bf16[144,512]{1,0:T(8,128)(2,1)S(1)} %pad.4.v0), channel_id=1, source_target_pairs={{0,1},{1,0},{2,3},{3,2},{4,5},{5,4},{6,7},{7,6},{8,9},{9,8},{10,11... | collective-permute-start | bytes 442376 | tf_op jit(solution)/shard_map/ppermute | solution.py:212
  21.0 3.9 %collective-permute-start.10 = (bf16[144,512]{1,0:T(8,128)(2,1)S(1)}, bf16[144,512]{1,0:T(8,128)(2,1)S(1)}, u32[]{:S(2)}, u32[]{:S(2)}) collective-permute-start(bf16[144,512]{1,0:T(8,128)(2,1)S(1)} %collective-permute-done.8.v1), channel_id=1, source_target_pairs={{0,1},{1,0},{2,3},{3,2},{4,5},{5,4},{6,7},{7,6},{8,9},{9,8},{10,11... | collective-permute-start | bytes 442376 | tf_op jit(solution)/shard_map/ppermute | solution.py:212
  21.0 3.9 %collective-permute-start.12 = (bf16[144,512]{1,0:T(8,128)(2,1)S(1)}, bf16[144,512]{1,0:T(8,128)(2,1)S(1)}, u32[]{:S(2)}, u32[]{:S(2)}) collective-permute-start(bf16[144,512]{1,0:T(8,128)(2,1)S(1)} %collective-permute-done.9.v3), channel_id=1, source_target_pairs={{0,1},{1,0},{2,3},{3,2},{4,5},{5,4},{6,7},{7,6},{8,9},{9,8},{10,11... | collective-permute-start | bytes 442376 | tf_op jit(solution)/shard_map/ppermute | solution.py:212
  24.3 2.9 %collective-permute-start.13 = (bf16[128,512]{1,0:T(8,128)(2,1)S(1)}, bf16[128,512]{1,0:T(8,128)(2,1)S(1)}, u32[]{:S(2)}, u32[]{:S(2)}) collective-permute-start(bf16[128,512]{1,0:T(8,128)(2,1)S(1)} %get-tuple-element.94), channel_id=1, source_target_pairs={{0,1},{1,0},{2,3},{3,2},{4,5},{5,4},{6,7},{7,6},{8,9},{9,8},{10,11... | collective-permute-start | bytes 393224 | tf_op jit(solution)/shard_map/ppermute | solution.py:212
  24.4 2.8 %collective-permute-start.14 = (bf16[128,512]{1,0:T(8,128)(2,1)S(1)}, bf16[128,512]{1,0:T(8,128)(2,1)S(1)}, u32[]{:S(2)}, u32[]{:S(2)}) collective-permute-start(bf16[128,512]{1,0:T(8,128)(2,1)S(1)} %get-tuple-element.95), channel_id=1, source_target_pairs={{0,1},{1,0},{2,3},{3,2},{4,5},{5,4},{6,7},{7,6},{8,9},{9,8},{10,11... | collective-permute-start | bytes 393224 | tf_op jit(solution)/shard_map/ppermute | solution.py:212
  27.3 7.7 %collective-permute-start.17 = (bf16[144,512]{1,0:T(8,128)(2,1)S(1)}, bf16[144,512]{1,0:T(8,128)(2,1)S(1)}, u32[]{:S(2)}, u32[]{:S(2)}) collective-permute-start(bf16[144,512]{1,0:T(8,128)(2,1)S(1)} %get-tuple-element.118), channel_id=1, source_target_pairs={{0,12},{1,13},{2,14},{3,15},{4,0},{5,1},{6,2},{7,3},{8,4},{9,5},{1... | collective-permute-start | bytes 442376 | tf_op jit(solution)/shard_map/ppermute | solution.py:207
  28.1 7.1 %collective-permute-start.18 = (bf16[144,512]{1,0:T(8,128)(2,1)S(1)}, bf16[144,512]{1,0:T(8,128)(2,1)S(1)}, u32[]{:S(2)}, u32[]{:S(2)}) collective-permute-start(bf16[144,512]{1,0:T(8,128)(2,1)S(1)} %get-tuple-element.119), channel_id=1, source_target_pairs={{0,14},{1,15},{2,0},{3,1},{4,2},{5,3},{6,4},{7,5},{8,6},{9,7},{10,... | collective-permute-start | bytes 442376 | tf_op jit(solution)/shard_map/ppermute | solution.py:207
  31.8 1.4 %collective-permute-start.15 = (bf16[128,512]{1,0:T(8,128)(2,1)S(1)}, bf16[128,512]{1,0:T(8,128)(2,1)S(1)}, u32[]{:S(2)}, u32[]{:S(2)}) collective-permute-start(bf16[128,512]{1,0:T(8,128)(2,1)S(1)} %get-tuple-element.112), channel_id=1, source_target_pairs={{0,1},{1,0},{2,3},{3,2},{4,5},{5,4},{6,7},{7,6},{8,9},{9,8},{10,11... | collective-permute-start | bytes 393224 | tf_op jit(solution)/shard_map/ppermute | solution.py:212
  31.9 1.5 %collective-permute-start.16 = (bf16[128,512]{1,0:T(8,128)(2,1)S(1)}, bf16[128,512]{1,0:T(8,128)(2,1)S(1)}, u32[]{:S(2)}, u32[]{:S(2)}) collective-permute-start(bf16[128,512]{1,0:T(8,128)(2,1)S(1)} %get-tuple-element.113), channel_id=1, source_target_pairs={{0,1},{1,0},{2,3},{3,2},{4,5},{5,4},{6,7},{7,6},{8,9},{9,8},{10,11... | collective-permute-start | bytes 393224 | tf_op jit(solution)/shard_map/ppermute | solution.py:212
  33.5 6.4 %collective-permute-start.19 = (bf16[128,512]{1,0:T(8,128)(2,1)S(1)}, bf16[128,512]{1,0:T(8,128)(2,1)S(1)}, u32[]{:S(2)}, u32[]{:S(2)}) collective-permute-start(bf16[128,512]{1,0:T(8,128)(2,1)S(1)} %get-tuple-element.125), channel_id=1, source_target_pairs={{0,12},{1,13},{2,14},{3,15},{4,0},{5,1},{6,2},{7,3},{8,4},{9,5},{1... | collective-permute-start | bytes 393224 | tf_op jit(solution)/shard_map/ppermute | solution.py:207
  34.0 6.5 %collective-permute-start.20 = (bf16[128,512]{1,0:T(8,128)(2,1)S(1)}, bf16[128,512]{1,0:T(8,128)(2,1)S(1)}, u32[]{:S(2)}, u32[]{:S(2)}) collective-permute-start(bf16[128,512]{1,0:T(8,128)(2,1)S(1)} %get-tuple-element.126), channel_id=1, source_target_pairs={{0,14},{1,15},{2,0},{3,1},{4,2},{5,3},{6,4},{7,5},{8,6},{9,7},{10,... | collective-permute-start | bytes 393224 | tf_op jit(solution)/shard_map/ppermute | solution.py:207
